TPU v7x, 32 devices: a whole 2x2x4 slice. The times are simulated.
32 devices in a mesh: dp: 16 (over z, x, core), ctx: 2 (over y).
Axes of the slice: x: 2, y: 2, z: 4, core: 2. Of those that a mesh axis runs over, the one named last changes fastest.
Arguments:
- query_vecs: bfloat16 [16, 256, 1024], P('dp', 'ctx'), may hold values from -12 to 12, as said below
- key_vecs: bfloat16 [16, 256, 1024], P('dp', 'ctx'), may hold values from -12 to 12
- value_vecs: bfloat16 [16, 256, 1024], P('dp', 'ctx'), may hold values from -6 to 6
- residual: bfloat16 [16, 256, 2048], P('dp', 'ctx'), may hold values from -45 to 45
- w_out: bfloat16 [1024, 2048], P('dp'), may hold values from -0.75 to 0.75
- norm_gain: float32 [2048], replicated, may hold values from 0.25 to 1.75
- w_gate_up: bfloat16 [16, 2, 2048, 1408], P('dp', None, None, 'ctx'), may hold values from -0.125 to 0.125
- w_down: bfloat16 [16, 1408, 2048], P('dp', 'ctx'), may hold values from -0.15625 to 0.15625
- expert_ids: int32 [16, 256, 6], P('dp', 'ctx'), may hold values from 0 to 15, as said below
- route_gates: float32 [16, 256, 6], P('dp', 'ctx'), may hold values from 0.1 to 0.9
- capacity: int32 [16, 2, 2], P('dp', 'ctx'), may hold values from 12 to 24, as said below
- expert_owner: int32 [16], replicated, may hold values from 0 to 15, each once
Outputs:
- attn_proj: bfloat16 [16, 256, 2048], P('dp', 'ctx')
- expert_sum: bfloat16 [16, 256, 2048], P('dp', 'ctx')
Inputs may be any that keep to these rules, and one draw needn't show every extreme that they name: `query_vecs`: q and k are drawn together. `expert_ids`: each position names 6 different experts; in each aligned block of 128 positions, experts 0 to 1 are each named by at least 24 positions. In each block some expert has capacity 24. `expert_owner`: each index of dp holds one expert.
All inputs are finite; a program needn't handle non-finite values.
Results may differ from a plain program's by a relative error of at most 0.019.
Values may be sent and summed in bfloat16 or wider, within the bound.
No kernel may reach another device: no remote copies, remote signals or barrier semaphores. Data moves between devices by JAX's collectives and lax.ppermute only.
A program may use at most 128 MiB of HBM per device.

v0:
```python
import jax
import jax.numpy as jnp
from jax import lax
from jax.experimental import pallas as pl
from jax.experimental.pallas import tpu as pltpu
from jax.sharding import PartitionSpec as P

HEADS = 8
HD = 128
PASS_SPECIALISTS = 2
CAP = 24


EPSILON = 1e-06
LOWEST = -1e30


def broadcast(array, axis, root):
    mine = lax.axis_index(axis) == root
    return lax.psum(jnp.where(mine, array, jnp.zeros_like(array)), axis)


def hop(array, axis, size, bit):
    return lax.ppermute(array, axis, [(i, i ^ bit) for i in range(size)])


def route_slots(expert_ids, route_gates, capacity, expert):
    matches = expert_ids == expert
    routed = jnp.any(matches, axis=1)
    gate_value = jnp.sum(jnp.where(matches, route_gates, 0.0), axis=1)
    slot_rank = jnp.cumsum(routed.astype(jnp.int32)) - 1
    kept_mask = routed & (slot_rank < capacity[expert])
    return (slot_rank, kept_mask, gate_value)


def attend(queries, key_block, value_block, visible):
    width = key_block.shape[0]
    token_count = queries.shape[0]
    query_heads = queries.reshape(token_count, HEADS, HD)
    key_heads = key_block.reshape(width, HEADS, HD)
    value_heads = value_block.reshape(width, HEADS, HD)
    gating_logits = jnp.einsum(
        "qhd,khd->qhk", query_heads, key_heads, preferred_element_type=jnp.float32
    ) * HD ** (-0.5)
    gating_logits = jnp.where(visible[:, None, :], gating_logits, -jnp.inf)
    row_top = jnp.max(gating_logits, axis=-1)
    weights = jnp.exp(gating_logits - row_top[:, :, None])
    denominator = jnp.sum(weights, axis=-1)
    weighted = jnp.einsum(
        "qhk,khd->qhd",
        weights.astype(jnp.bfloat16),
        value_heads,
        preferred_element_type=jnp.float32,
    )
    attended = (weighted / denominator[:, :, None]).astype(jnp.bfloat16)
    return attended.reshape(token_count, HEADS * HD)


def feed_forward(rows, gate_up, down_part):
    gate_proj = jnp.dot(rows, gate_up[0], preferred_element_type=jnp.float32)
    up_proj = jnp.dot(rows, gate_up[1], preferred_element_type=jnp.float32)
    hidden = (jax.nn.silu(gate_proj) * up_proj).astype(jnp.bfloat16)
    return jnp.dot(hidden, down_part, preferred_element_type=jnp.float32).astype(jnp.bfloat16)


def normalise(attn_proj, residual, norm_gain):
    combined = residual.astype(jnp.float32) + attn_proj.astype(jnp.float32)
    return (
        combined
        * lax.rsqrt(jnp.mean(combined * combined, axis=-1, keepdims=True) + EPSILON)
        * norm_gain
    ).astype(jnp.bfloat16)


def pick_rows(routing, normed):
    slot_ids = jnp.arange(CAP)
    select = [
        (slot_rank[None, :] == slot_ids[:, None]) & kept_mask[None, :]
        for slot_rank, kept_mask, _ in routing
    ]
    select = jnp.concatenate(select, axis=0).astype(jnp.bfloat16)
    chosen = jnp.dot(select, normed, preferred_element_type=jnp.float32).astype(jnp.bfloat16)
    return chosen.reshape(PASS_SPECIALISTS, CAP, normed.shape[1])


def combine_rows(routing, produced):
    slot_ids = jnp.arange(CAP)
    summed = 0.0
    for expert in range(PASS_SPECIALISTS):
        slot_rank, kept_mask, gate_value = routing[expert]
        place = ((slot_rank[:, None] == slot_ids[None, :]) & kept_mask[:, None]).astype(
            jnp.bfloat16
        )
        picked = jnp.dot(place, produced[expert], preferred_element_type=jnp.float32)
        summed = summed + gate_value[:, None] * picked
    return summed.astype(jnp.bfloat16)


def body_move_weights(
    query_vecs,
    key_vecs,
    value_vecs,
    residual,
    w_out,
    norm_gain,
    w_gate_up,
    w_down,
    expert_ids,
    route_gates,
    capacity,
    expert_owner,
):
    token_count = query_vecs.shape[1]
    weights_in = []
    for expert in range(PASS_SPECIALISTS):
        weights_in.append(
            (
                broadcast(w_gate_up[0], "dp", expert_owner[expert]),
                broadcast(w_down[0], "dp", expert_owner[expert]),
            )
        )
    keys = lax.all_gather(key_vecs[0], "ctx", axis=0, tiled=True)
    values = lax.all_gather(value_vecs[0], "ctx", axis=0, tiled=True)
    first_row = lax.axis_index("ctx") * token_count
    query_pos = first_row + jnp.arange(token_count)
    visible = jnp.arange(keys.shape[0])[None, :] <= query_pos[:, None]
    attended = attend(query_vecs[0], keys, values, visible)
    projected = jnp.dot(
        attended,
        lax.all_gather(w_out, "dp", axis=0, tiled=True),
        preferred_element_type=jnp.float32,
    )
    attn_proj = projected.astype(jnp.bfloat16)
    normed = normalise(attn_proj, residual[0], norm_gain)
    routing = [
        route_slots(expert_ids[0], route_gates[0], capacity[0, 0], expert)
        for expert in range(PASS_SPECIALISTS)
    ]
    chosen = pick_rows(routing, normed)
    routed_rows = lax.all_gather(jnp.swapaxes(chosen, 0, 1), "ctx", axis=0, tiled=True)
    outputs = [
        feed_forward(routed_rows[:, expert], *weights_in[expert])
        for expert in range(PASS_SPECIALISTS)
    ]
    expert_out = lax.psum_scatter(
        jnp.stack(outputs, axis=1), "ctx", scatter_dimension=0, tiled=True
    )
    expert_sum = combine_rows(routing, [expert_out[:, e] for e in range(PASS_SPECIALISTS)])
    return (attn_proj[None], expert_sum[None])


def attend_kernel(info, query, key, value, key_before, value_before, ids, gates, attended, place, gate_values):
    token_count = query.shape[0]
    row = lax.broadcasted_iota(jnp.int32, (token_count, token_count), 0)
    col = lax.broadcasted_iota(jnp.int32, (token_count, token_count), 1)
    own_visible = col <= row
    before_visible = jnp.broadcast_to(info[0], (token_count, token_count)) == 1
    contract_last = (((1,), (1,)), ((), ()))
    for head in range(HEADS):
        span = slice(head * HD, (head + 1) * HD)
        heads = query[:, span]
        own = lax.dot_general(
            heads, key[:, span], contract_last, preferred_element_type=jnp.float32
        )
        before = lax.dot_general(
            heads, key_before[:, span], contract_last, preferred_element_type=jnp.float32
        )
        own = jnp.where(own_visible, own * HD ** (-0.5), -jnp.inf)
        before = jnp.where(before_visible, before * HD ** (-0.5), -jnp.inf)
        top = jnp.maximum(
            jnp.max(own, axis=1, keepdims=True), jnp.max(before, axis=1, keepdims=True)
        )
        own = jnp.exp(own - top)
        before = jnp.exp(before - top)
        total = jnp.sum(own, axis=1, keepdims=True) + jnp.sum(before, axis=1, keepdims=True)
        mixed = jnp.dot(
            own.astype(jnp.bfloat16), value[:, span], preferred_element_type=jnp.float32
        ) + jnp.dot(
            before.astype(jnp.bfloat16), value_before[:, span], preferred_element_type=jnp.float32
        )
        mixed = mixed / total
        swapped = pltpu.roll(mixed, HD // 2, 1)
        mixed = jnp.where(jnp.broadcast_to(info[2], mixed.shape) == 0, mixed, swapped)
        attended[head ^ info[1]] = mixed.astype(jnp.bfloat16)

    slots = PASS_SPECIALISTS * CAP
    lane = lax.broadcasted_iota(jnp.int32, (token_count, slots), 1)
    routed = jnp.zeros((token_count, slots), jnp.float32)
    limit = jnp.zeros((token_count, slots), jnp.int32)
    for expert in range(PASS_SPECIALISTS):
        matches = ids[...] == expert
        named = jnp.max(matches.astype(jnp.float32), axis=1, keepdims=True)
        gate_values[:, expert : expert + 1] = jnp.sum(
            jnp.where(matches, gates[...], 0.0), axis=1, keepdims=True
        )
        mine = (lane >= expert * CAP) & (lane < (expert + 1) * CAP)
        routed = jnp.where(mine, named, routed)
        limit = jnp.where(mine, info[3 + expert], limit)
    earlier = (col < row).astype(jnp.bfloat16)
    rank = jnp.dot(
        earlier, routed.astype(jnp.bfloat16), preferred_element_type=jnp.float32
    ).astype(jnp.int32)
    slot = jnp.where(lane >= CAP, lane - CAP, lane)
    place[...] = ((routed > 0.0) & (rank == slot) & (rank < limit)).astype(jnp.bfloat16)


def project_kernel(*refs):
    attended, residual, gain, place = refs[:4]
    near = refs[4 : 4 + HEADS]
    far = refs[4 + HEADS : 4 + 2 * HEADS]
    attn_proj, chosen, combined = refs[4 + 2 * HEADS :]
    token_count, width = residual.shape
    tile = 512
    squares = jnp.zeros((token_count, 1), jnp.float32)
    for start in range(0, width, tile):
        span = slice(start, start + tile)
        total = jnp.zeros((token_count, tile), jnp.float32)
        for pair in range(0, HEADS, 2):
            left = jnp.concatenate([attended[pair], attended[pair + 1]], axis=1)
            right = jnp.concatenate(
                [near[pair][:, span], far[pair][:, span]]
                + [near[pair + 1][:, span], far[pair + 1][:, span]],
                axis=0,
            )
            total = total + jnp.dot(left, right, preferred_element_type=jnp.float32)
        rounded = total.astype(jnp.bfloat16)
        attn_proj[:, span] = rounded
        added = residual[:, span].astype(jnp.float32) + rounded.astype(jnp.float32)
        combined[:, span] = added
        squares = squares + jnp.sum(added * added, axis=1, keepdims=True)
    scale = lax.rsqrt(squares / width + EPSILON)
    for start in range(0, width, tile):
        span = slice(start, start + tile)
        normed = (combined[:, span] * scale * gain[:, span]).astype(jnp.bfloat16)
        chosen[:, span] = lax.dot_general(
            place[...], normed, (((0,), (0,)), ((), ())), preferred_element_type=jnp.float32
        ).astype(jnp.bfloat16)


def expert_kernel(other, rows, gate_up_near, gate_up_far, down_near, down_far, made, gate_up, down, hidden, sems):
    units = down.shape[0]
    starts = list(range(0, units, 256))

    def copies(gate_up_from, down_from):
        out = []
        for k, start in enumerate(starts):
            size = min(256, units - start)
            span = pl.ds(start, size)
            for part in range(2):
                out.append(
                    pltpu.make_async_copy(
                        gate_up_from.at[part, span], gate_up.at[part, span], sems.at[2 * k + part]
                    )
                )
        out.append(pltpu.make_async_copy(down_from, down, sems.at[2 * len(starts)]))
        return out

    @pl.when(other[0] == 0)
    def _():
        for copy in copies(gate_up_near, down_near):
            copy.start()

    @pl.when(other[0] != 0)
    def _():
        for copy in copies(gate_up_far, down_far):
            copy.start()

    arrived = copies(gate_up_near, down_near)
    contract_last = (((1,), (1,)), ((), ()))
    for k, start in enumerate(starts):
        size = min(256, units - start)
        span = slice(start, start + size)
        arrived[2 * k].wait()
        gate_proj = lax.dot_general(
            rows[...], gate_up[0, span], contract_last, preferred_element_type=jnp.float32
        )
        arrived[2 * k + 1].wait()
        up_proj = lax.dot_general(
            rows[...], gate_up[1, span], contract_last, preferred_element_type=jnp.float32
        )
        hidden[:, span] = (gate_proj / (1.0 + jnp.exp(-gate_proj)) * up_proj).astype(jnp.bfloat16)
    arrived[-1].wait()
    width = made.shape[1]
    for start in range(0, width, 512):
        span = slice(start, start + 512)
        made[:, span] = jnp.dot(
            hidden[...], down[:, span], preferred_element_type=jnp.float32
        ).astype(jnp.bfloat16)


def gather_rows(unit, bits, dp_size):
    for bit in bits[:-1]:
        unit = jnp.concatenate([unit, hop(unit, "dp", dp_size, bit)], axis=0)
    half = unit.shape[1] // 2
    left, right = unit[:, :half], unit[:, half:]
    left = jnp.stack([left, hop(left, "dp", dp_size, bits[-1])])
    right = jnp.stack([right, hop(right, "ctx", 2, 1)])
    left = jnp.stack([left, hop(left, "ctx", 2, 1)])
    right = jnp.stack([right, hop(right, "dp", dp_size, bits[-1])], axis=1)
    rows = jnp.concatenate([left, right], axis=-1)
    return rows.reshape(-1, rows.shape[-1])


def scatter_rows(rows, bits, dp_size, offset):
    half = rows.shape[1] // 2
    rows = rows.reshape(2, 2, -1, rows.shape[1])
    left, right = rows[..., :half], rows[..., half:]

    def add(kept, came):
        return (kept.astype(jnp.float32) + came.astype(jnp.float32)).astype(jnp.bfloat16)

    near = (offset & bits[-1]) == 0
    left = add(left[0], hop(left[1], "ctx", 2, 1))
    right = jnp.where(near, right[:, 0], hop(right[:, 1], "dp", dp_size, bits[-1]))
    left = jnp.where(near, left[0], hop(left[1], "dp", dp_size, bits[-1]))
    right = add(right[0], hop(right[1], "ctx", 2, 1))
    unit = jnp.concatenate([left, right], axis=-1)
    for bit in reversed(bits[:-1]):
        kept, sent = jnp.split(unit, 2, axis=0)
        unit = jnp.where((offset & bit) == 0, kept, hop(sent, "dp", dp_size, bit))
    return unit


def vmem(count):
    return [pl.BlockSpec(memory_space=pltpu.VMEM)] * count


def body_move_rows(
    query_vecs,
    key_vecs,
    value_vecs,
    residual,
    w_out,
    norm_gain,
    w_gate_up,
    w_down,
    expert_ids,
    route_gates,
    capacity,
    expert_owner,
):
    token_count = query_vecs.shape[1]
    width = residual.shape[2]
    dp_size = lax.axis_size("dp")
    me = lax.axis_index("dp")
    core = me & 1
    ctx = lax.axis_index("ctx")
    bits = [1 << k for k in reversed(range(1, dp_size.bit_length() - 1))]

    key_before = lax.ppermute(key_vecs[0], "ctx", [(0, 1)])
    value_before = lax.ppermute(value_vecs[0], "ctx", [(0, 1)])
    z_far, z_near, x_bit = bits
    half = width // 2
    near = [None] * HEADS
    near[0] = w_out
    near[z_near >> 1] = hop(w_out, "dp", dp_size, z_near)
    near[z_far >> 1] = hop(w_out, "dp", dp_size, z_far)
    near[x_bit >> 1] = hop(w_out, "dp", dp_size, x_bit)
    near[(z_near | x_bit) >> 1] = hop(near[z_near >> 1], "dp", dp_size, x_bit)
    near[(z_far | x_bit) >> 1] = hop(near[z_far >> 1], "dp", dp_size, x_bit)
    z_both = jnp.concatenate(
        [
            hop(near[z_far >> 1][:, :half], "dp", dp_size, z_near),
            hop(near[z_near >> 1][:, half:], "dp", dp_size, z_far),
        ],
        axis=1,
    )
    near[(z_far | z_near) >> 1] = z_both
    near[(z_far | z_near | x_bit) >> 1] = hop(z_both, "dp", dp_size, x_bit)
    far = [None] * HEADS
    for group in ([0, z_near >> 1, z_far >> 1, x_bit >> 1], [(z_near | x_bit) >> 1, (z_far | x_bit) >> 1], [(z_far | z_near) >> 1, (z_far | z_near | x_bit) >> 1]):
        came = hop(jnp.stack([near[j] for j in group]), "dp", dp_size, 1)
        for k, j in enumerate(group):
            far[j] = came[k]
    gate_up_near = jnp.swapaxes(w_gate_up[0], 1, 2)
    gate_up_far = hop(gate_up_near, "dp", dp_size, 1)
    down_far = hop(w_down[0], "dp", dp_size, 1)

    info = jnp.stack([ctx, me >> 1, core, capacity[0, 0, 0], capacity[0, 0, 1]]).astype(jnp.int32)
    slots = PASS_SPECIALISTS * CAP
    attended, place, gate_values = pl.pallas_call(
        attend_kernel,
        out_shape=(
            jax.ShapeDtypeStruct((HEADS, token_count, HD), jnp.bfloat16),
            jax.ShapeDtypeStruct((token_count, slots), jnp.bfloat16),
            jax.ShapeDtypeStruct((token_count, PASS_SPECIALISTS), jnp.float32),
        ),
        in_specs=[pl.BlockSpec(memory_space=pltpu.SMEM)] + vmem(7),
        out_specs=tuple(vmem(3)),
        cost_estimate=pl.CostEstimate(
            flops=4 * HEADS * HD * 2 * token_count * token_count,
            bytes_accessed=6 * 2 * token_count * HEADS * HD,
            transcendentals=2 * HEADS * token_count * token_count,
        ),
        compiler_params=pltpu.CompilerParams(vmem_limit_bytes=16 * 2**20),
    )(
        info,
        query_vecs[0],
        key_vecs[0],
        value_vecs[0],
        key_before,
        value_before,
        expert_ids[0],
        route_gates[0],
    )
    attn_proj, chosen = pl.pallas_call(
        project_kernel,
        out_shape=(
            jax.ShapeDtypeStruct((token_count, width), jnp.bfloat16),
            jax.ShapeDtypeStruct((slots, width), jnp.bfloat16),
        ),
        in_specs=vmem(4 + 2 * HEADS),
        out_specs=tuple(vmem(2)),
        scratch_shapes=[pltpu.VMEM((token_count, width), jnp.float32)],
        cost_estimate=pl.CostEstimate(
            flops=2 * token_count * HEADS * HD * width,
            bytes_accessed=2 * HEADS * HD * width,
            transcendentals=0,
        ),
        compiler_params=pltpu.CompilerParams(vmem_limit_bytes=24 * 2**20),
    )(attended, residual[0], norm_gain[None], place, *near, *far)

    owners = expert_owner[:PASS_SPECIALISTS]
    differ = owners[0] ^ owners[1]
    branch = 0
    split_bit = 0
    for k in reversed(range(len(bits))):
        parted = (differ & bits[k]) != 0
        branch = jnp.where(parted, k, branch)
        split_bit = jnp.where(parted, bits[k], split_bit)
    same = split_bit == 0
    side = jnp.where(((me ^ owners[0]) & split_bit) == 0, 0, 1)
    units = w_down.shape[1]
    row_count = dp_size * CAP

    def dispatch(bit):
        rest = [b for b in bits if b != bit]

        def run(kept, sent):
            unit = jnp.concatenate([kept, hop(sent, "dp", dp_size, bit)], axis=0)
            return gather_rows(unit, rest, dp_size)

        return run

    def give_back(bit):
        rest = [b for b in bits if b != bit]

        def run(made, offset):
            unit = scatter_rows(made, rest, dp_size, offset)
            return unit[:CAP], hop(unit[CAP:], "dp", dp_size, bit)

        return run

    def one_pass(step, produced):
        local = jnp.where(same, step, side)
        sent_expert = jnp.where(same, step, 1 - side)
        owner = jnp.where(local == 0, owners[0], owners[1])
        offset = me ^ owner
        kept = jnp.where(local == 0, chosen[:CAP], chosen[CAP:])
        sent = jnp.where(sent_expert == 0, chosen[:CAP], chosen[CAP:])
        rows = lax.switch(branch, [dispatch(bit) for bit in bits], kept, sent)
        made = pl.pallas_call(
            expert_kernel,
            out_shape=jax.ShapeDtypeStruct((row_count, width), jnp.bfloat16),
            in_specs=[pl.BlockSpec(memory_space=pltpu.SMEM)]
            + vmem(1)
            + [pl.BlockSpec(memory_space=pl.ANY)] * 4,
            out_specs=vmem(1)[0],
            scratch_shapes=[
                pltpu.VMEM((2, units, width), jnp.bfloat16),
                pltpu.VMEM((units, width), jnp.bfloat16),
                pltpu.VMEM((row_count, units), jnp.bfloat16),
                pltpu.SemaphoreType.DMA((2 * -(-units // 256) + 1,)),
            ],
            cost_estimate=pl.CostEstimate(
                flops=6 * row_count * units * width,
                bytes_accessed=6 * units * width,
                transcendentals=row_count * units,
            ),
            compiler_params=pltpu.CompilerParams(vmem_limit_bytes=40 * 2**20),
        )((offset & 1)[None], rows, gate_up_near, gate_up_far, w_down[0], down_far)
        own, other = lax.switch(branch, [give_back(bit) for bit in bits], made, offset)
        served = jnp.where((offset & bits[0]) == 0, own, other)
        first = jnp.where(same, served, jnp.where(local == 0, own, other))
        second = jnp.where(same, served, jnp.where(local == 0, other, own))
        return (
            jnp.where(same & (step != 0), produced[0], first),
            jnp.where(same & (step != 1), produced[1], second),
        )

    nothing = jnp.zeros((CAP, width), jnp.bfloat16)
    produced = lax.fori_loop(0, jnp.where(same, 2, 1), one_pass, (nothing, nothing))
    summed = 0.0
    for expert in range(PASS_SPECIALISTS):
        picked = jnp.dot(
            place[:, expert * CAP : (expert + 1) * CAP],
            produced[expert],
            preferred_element_type=jnp.float32,
        )
        summed = summed + gate_values[:, expert : expert + 1] * picked
    expert_sum = summed.astype(jnp.bfloat16)
    return (attn_proj[None], expert_sum[None])


def solution(mesh):
    placed = (
        P("dp", "ctx", None),
        P("dp", "ctx", None),
        P("dp", "ctx", None),
        P("dp", "ctx", None),
        P("dp", None),
        P(),
        P("dp", None, None, "ctx"),
        P("dp", "ctx", None),
        P("dp", "ctx", None),
        P("dp", "ctx", None),
        P("dp", "ctx", None),
        P(),
    )
    dp_size, ctx_size = mesh.shape["dp"], mesh.shape["ctx"]
    small = ctx_size == 2 and dp_size == 2 * HEADS
    return jax.shard_map(
        body_move_rows if small else body_move_weights,
        mesh=mesh,
        in_specs=placed,
        out_specs=(P("dp", "ctx", None), P("dp", "ctx", None)),
        check_vma=False,
    )
```

profile of v0, /device:TPU:0, one launch (start us, length us, event | category | flops | bytes accessed | tf_op | source)
XLA Modules:
  0.0 136.9 jit_solution(8030015547370966507)
XLA Ops:
  0.6 0.5 collective-permute-start.49
  1.2 3.7 %collective-permute-start.41 = (bf16[64,2048]{1,0:T(8,128)(2,1)}, bf16[64,2048]{1,0:T(8,128)(2,1)S(1)}, u32[]{:S(2)}, u32[]{:S(2)}) collective-permute-start(bf16[64,2048]{1,0:T(8,128)(2,1)} %refs_4_.1), channel_id=1, source_target_pairs={{0,16},{2,18},{4,20},{6,22},{8,24},{10,26},{12,28},{14,30},{16,0},... | collective-permute-start | bytes 786440 | tf_op jit(solution)/shard_map/ppermute | solution.py:24
  4.8 1.6 %collective-permute-start.39 = (bf16[64,2048]{1,0:T(8,128)(2,1)}, bf16[64,2048]{1,0:T(8,128)(2,1)S(1)}, u32[]{:S(2)}, u32[]{:S(2)}) collective-permute-start(bf16[64,2048]{1,0:T(8,128)(2,1)} %refs_4_.1), channel_id=1, source_target_pairs={{0,8},{2,10},{4,12},{6,14},{8,0},{10,2},{12,4},{14,6},{16,24},{18,... | collective-permute-start | bytes 786440 | tf_op jit(solution)/shard_map/ppermute | solution.py:24
  6.4 11.3 %collective-permute-done.41.refs_8_ = bf16[64,2048]{1,0:T(8,128)(2,1)S(1)} collective-permute-done((bf16[64,2048]{1,0:T(8,128)(2,1)}, bf16[64,2048]{1,0:T(8,128)(2,1)S(1)}, u32[]{:S(2)}, u32[]{:S(2)}) %collective-permute-start.41) | collective-permute-done | bytes 262176 | tf_op jit(solution)/shard_map/ppermute | solution.py:24
  17.7 0.8 collective-permute-start.43
  18.5 1.5 %collective-permute-start.42 = (bf16[64,2048]{1,0:T(8,128)(2,1)S(1)}, bf16[64,2048]{1,0:T(8,128)(2,1)S(1)}, u32[]{:S(2)}, u32[]{:S(2)}) collective-permute-start(bf16[64,2048]{1,0:T(8,128)(2,1)S(1)} %collective-permute-done.41.refs_8_), channel_id=1, source_target_pairs={{0,4},{2,6},{4,0},{6,2},{8,12},{10,14},{12,8},{14,10},{16,20},{18,... | collective-permute-start | bytes 786440 | tf_op jit(solution)/shard_map/ppermute | solution.py:24
  20.0 1.4 %fusion.36 = (s32[1,1,1]{2,1,0:T(1,128)}, s32[1,1,1]{2,1,0:T(1,128)}) fusion(s32[1,1,2]{2,1,0:T(1,128)} %param.30), kind=kLoop, calls=%fused_computation.121 | loop fusion | bytes 16 | tf_op jit(solution)/shard_map/slice | solution.py:379
  21.4 3.3 %collective-permute-start.44 = (bf16[64,1024]{1,0:T(8,128)(2,1)S(1)}, bf16[64,1024]{1,0:T(8,128)(2,1)S(1)}, u32[]{:S(2)}, u32[]{:S(2)}) collective-permute-start(bf16[64,1024]{1,0:T(8,128)(2,1)S(1)} %slice.264), channel_id=1, source_target_pairs={{0,16},{2,18},{4,20},{6,22},{8,24},{10,26},{12,28},{14,30},{16,0},... | collective-permute-start | bytes 393224 | tf_op jit(solution)/shard_map/ppermute | solution.py:24
  24.7 0.5 collective-permute-start.40
  25.3 1.3 fusion.35
  28.5 0.8 copy.34
  29.3 0.8 copy.35
  30.1 1.3 stack.156.info
  31.5 1.6 %collective-permute-start.38 = (bf16[64,2048]{1,0:T(8,128)(2,1)}, bf16[64,2048]{1,0:T(8,128)(2,1)S(1)}, u32[]{:S(2)}, u32[]{:S(2)}) collective-permute-start(bf16[64,2048]{1,0:T(8,128)(2,1)} %refs_4_.1), channel_id=1, source_target_pairs={{0,4},{2,6},{4,0},{6,2},{8,12},{10,14},{12,8},{14,10},{16,20},{18,... | collective-permute-start | bytes 786440 | tf_op jit(solution)/shard_map/ppermute | solution.py:24
  33.0 3.4 %collective-permute-start.36 = (bf16[128,1024]{1,0:T(8,128)(2,1)}, bf16[128,1024]{1,0:T(8,128)(2,1)S(1)}, u32[]{:S(2)}, u32[]{:S(2)}) collective-permute-start(bf16[128,1024]{1,0:T(8,128)(2,1)} %bitcast.202), channel_id=1, source_target_pairs={{0,1},{2,3},{4,5},{6,7},{8,9},{10,11},{12,13},{14,15},{16,17},{18,... | collective-permute-start | bytes 786440 | tf_op jit(solution)/shard_map/ppermute | solution.py:350
  36.5 1.3 collective-permute-start.37
  37.9 5.6 %collective-permute-done.36.key_before = bf16[128,1024]{1,0:T(8,128)(2,1)S(1)} collective-permute-done((bf16[128,1024]{1,0:T(8,128)(2,1)}, bf16[128,1024]{1,0:T(8,128)(2,1)S(1)}, u32[]{:S(2)}, u32[]{:S(2)}) %collective-permute-start.36) | collective-permute-done | bytes 262176 | tf_op jit(solution)/shard_map/ppermute | solution.py:350
  43.5 0.5 collective-permute-start.45
  44.0 0.1 pad_maximum_fusion.12
  44.2 2.6 %collective-permute-done.37.value_before = bf16[128,1024]{1,0:T(8,128)(2,1)S(1)} collective-permute-done((bf16[128,1024]{1,0:T(8,128)(2,1)}, bf16[128,1024]{1,0:T(8,128)(2,1)S(1)}, u32[]{:S(2)}, u32[]{:S(2)}) %collective-permute-start.37) | collective-permute-done | bytes 262176 | tf_op jit(solution)/shard_map/ppermute | solution.py:351
  46.8 3.2 %shard_map.131 = (bf16[8,128,128]{2,1,0:T(8,128)(2,1)S(1)}, bf16[128,48]{1,0:T(8,128)(2,1)S(1)}, f32[128,2]{1,0:T(8,128)S(1)}) custom-call(s32[5]{0:T(128)S(1)} %stack.156.info, bf16[128,1024]{1,0:T(8,128)(2,1)S(1)} %bitcast.201, bf16[128,1024]{1,0:T(8,128)(2,1)S(1)} %bitcast.203, bf16[128,1024]{1,0:T(8,128)(2,1)S(1)} %bitcast.205, ...), custom_call_target="tpu_custom_call" | custom-call | flops 134217728 | bytes 1572864 | tf_op jit(solution)/shard_map/pallas_call | solution.py:381
  50.0 0.1 pad_maximum_fusion.14
  50.0 0.6 collective-permute-start.48
  50.6 0.2 slice_reduce_fusion.1
  50.9 1.3 collective-permute-done.48
  52.2 0.1 slice_bitcast_fusion.33
  52.4 1.7 %shard_map.132 = (bf16[128,2048]{1,0:T(8,128)(2,1)}, bf16[48,2048]{1,0:T(8,128)(2,1)S(1)}) custom-call(bf16[8,128,128]{2,1,0:T(8,128)(2,1)S(1)} %get-tuple-element.216.refs_0_, bf16[128,2048]{1,0:T(8,128)(2,1)S(1)} %bitcast.200, f32[1,2048]{1,0:T(1,128)S(1)} %bitcast.208, bf16[128,48]{1,0:T(8,128)(2,1)S(1)} %get-tuple-element.217.refs_3_, ...), custom_call_target="tpu_custom_call" | custom-call | flops 536870912 | bytes 4194304 | tf_op jit(solution)/shard_map/pallas_call | solution.py:406
  54.1 81.4 %while.14 = (s32[]{:T(128)}, bf16[24,2048]{1,0:T(8,128)(2,1)S(1)}, bf16[24,2048]{1,0:T(8,128)(2,1)S(1)}, s32[]{:T(128)}, pred[]{:T(512)}, /*index=5*/s32[]{:T(12...) while((s32[]{:T(128)}, bf16[24,2048]{1,0:T(8,128)(2,1)S(1)}, ...), condition=%wide.region_7.8_spmd, body=%wide.region_0.7_spmd.sunk | while | flops 3331768320 | bytes 46400416 | solution.py:492
  54.3 0.6 fusion.40
  56.2 35.8 %conditional.4 = (bf16[384,2048]{1,0:T(8,128)(2,1)S(1)}) conditional(s32[]{:T(128)} %get-tuple-element.463, (bf16[24,2048]{1,0:T(8,128)(2,1)S(1)}, bf16[24,2048]{1,0:T(8,128)(2,1)S(1)}) %tuple.87, (bf16[24,2048]{1,0:T(8,128)(2,1)S(1)}, bf16[24,2048]{1,0:T(8,128)(2,1)S(1)}) %tuple.87, (bf16[24,2048]{1,0:T(8,128)(2,1)S(1)}, ...), branch_computations={%region_1.1_spmd, %region_2.2_spmd, %region_3.3_spmd} | conditional | flops 7077888 | bytes 16908536 | solution.py:461
  56.3 0.7 collective-permute-start.12
  57.0 4.4 %collective-permute-done.12 = bf16[24,2048]{1,0:T(8,128)(2,1)S(1)} collective-permute-done((bf16[24,2048]{1,0:T(8,128)(2,1)S(1)}, bf16[24,2048]{1,0:T(8,128)(2,1)S(1)}, u32[]{:S(2)}, u32[]{:S(2)}) %collective-permute-start.12) | collective-permute-done | bytes 98336 | tf_op jit(solution)/shard_map/while/body/cond/branch_2_fun/ppermute | solution.py:24
  61.4 1.2 collective-permute-start.13
  62.6 10.2 %collective-permute-done.13 = bf16[48,2048]{1,0:T(8,128)(2,1)S(1)} collective-permute-done((bf16[48,2048]{1,0:T(8,128)(2,1)S(1)}, bf16[48,2048]{1,0:T(8,128)(2,1)S(1)}, u32[]{:S(2)}, u32[]{:S(2)}) %collective-permute-start.13) | collective-permute-done | bytes 196640 | tf_op jit(solution)/shard_map/while/body/cond/branch_2_fun/ppermute | solution.py:24
  72.8 0.1 slice_bitcast_fusion.5
  72.9 2.4 %collective-permute-start.16 = (bf16[96,1024]{1,0:T(8,128)(2,1)S(1)}, bf16[96,1024]{1,0:T(8,128)(2,1)S(1)}, u32[]{:S(2)}, u32[]{:S(2)}) collective-permute-start(bf16[96,1024]{1,0:T(8,128)(2,1)S(1)} %get-tuple-element.275), channel_id=1, source_target_pairs={{0,1},{1,0},{2,3},{3,2},{4,5},{5,4},{6,7},{7,6},{8,9},{9,8},{10,11... | collective-permute-start | bytes 589832 | tf_op jit(solution)/shard_map/while/body/cond/branch_2_fun/ppermute | solution.py:24
  75.3 5.1 %collective-permute-done.16 = bf16[96,1024]{1,0:T(8,128)(2,1)S(1)} collective-permute-done((bf16[96,1024]{1,0:T(8,128)(2,1)S(1)}, bf16[96,1024]{1,0:T(8,128)(2,1)S(1)}, u32[]{:S(2)}, u32[]{:S(2)}) %collective-permute-start.16) | collective-permute-done | bytes 196640 | tf_op jit(solution)/shard_map/while/body/cond/branch_2_fun/ppermute | solution.py:24
  80.4 0.1 fusion.4
  80.4 0.1 collective-permute-start.17
  80.5 1.3 collective-permute-done.14
  81.9 0.1 fusion.5
  81.9 0.5 collective-permute-start.15
  82.4 8.6 %collective-permute-done.17 = bf16[2,96,1024]{2,1,0:T(8,128)(2,1)S(1)} collective-permute-done((bf16[2,96,1024]{2,1,0:T(8,128)(2,1)S(1)}, bf16[2,96,1024]{2,1,0:T(8,128)(2,1)S(1)}, u32[]{:S(2)}, u32[]{:S(2)}) %collective-permute-start.17) | collective-permute-done | bytes 393248 | tf_op jit(solution)/shard_map/while/body/cond/branch_2_fun/ppermute | solution.py:24
  91.0 0.8 collective-permute-done.15
  91.8 0.1 maximum_maximum_fusion.2
  92.0 0.1 copy.30
  92.1 1.1 copy-done.6
  93.2 10.0 %body.3 = bf16[384,2048]{1,0:T(8,128)(2,1)S(1)} custom-call(s32[1]{0:T(128)} %bitcast.190.other, bf16[384,2048]{1,0:T(8,128)(2,1)} %copy-done.6, bf16[2,704,2048]{2,1,0:T(8,128)(2,1)} %get-tuple-element.465.gate_up_near, bf16[2,704,2048]{2,1,0:T(8,128)(2,1)} %get-tuple-element.466.gate_up_far, bf16[704,2048]{1,0:T(8,128)(2,1)} %bitcast.227, ...), custom_call_target="tpu_custom_call" | custom-call | flops 3321888768 | bytes 8650752 | tf_op jit(solution)/shard_map/while/body/pallas_call | solution.py:462
  103.2 31.3 %conditional.5 = (bf16[24,2048]{1,0:T(8,128)(2,1)S(1)}, bf16[24,2048]{1,0:T(8,128)(2,1)}) conditional(s32[]{:T(128)} %get-tuple-element.463, (s32[]{:T(128)}, bf16[384,2048]{1,0:T(8,128)(2,1)S(1)}) %tuple.88, (s32[]{:T(128)}, bf16[384,2048]{1,0:T(8,128)(2,1)S(1)}) %tuple.88, (s32[]{:T(128)}, bf16[384,2048]{1,0:T(8,128)(2,1)S(1)}) %tuple.88), branch_computations={%region_4.4_spmd, %region_5.5_spmd, %region_6.6_spmd} | conditional | flops 2359300 | bytes 13566253 | solution.py:482
  103.3 0.8 collective-permute-start.30
  104.2 1.8 %collective-permute-start.32 = (bf16[2,96,1024]{2,1,0:T(8,128)(2,1)S(1)}, bf16[2,96,1024]{2,1,0:T(8,128)(2,1)S(1)}, u32[]{:S(2)}, u32[]{:S(2)}) collective-permute-start(bf16[2,96,1024]{2,1,0:T(8,128)(2,1)S(1)} %slice_bitcast_fusion.22), channel_id=1, source_target_pairs={{0,8},{2,10},{4,12},{6,14},{8,0},{10,2},{12,4},{14,6},{16,24},{18,... | collective-permute-start | bytes 1179656 | tf_op jit(solution)/shard_map/while/body/cond/branch_2_fun/ppermute | solution.py:24
  105.9 6.5 %collective-permute-done.30 = bf16[2,96,1024]{2,1,0:T(8,128)(2,1)} collective-permute-done((bf16[2,96,1024]{2,1,0:T(8,128)(2,1)S(1)}, bf16[2,96,1024]{2,1,0:T(8,128)(2,1)}, u32[]{:S(2)}, u32[]{:S(2)}) %collective-permute-start.30) | collective-permute-done | bytes 393248 | tf_op jit(solution)/shard_map/while/body/cond/branch_2_fun/ppermute | solution.py:24
  112.4 1.1 fusion.18
  113.6 1.5 %collective-permute-start.31 = (bf16[96,1024]{1,0:T(8,128)(2,1)S(1)}, bf16[96,1024]{1,0:T(8,128)(2,1)S(1)}, u32[]{:S(2)}, u32[]{:S(2)}) collective-permute-start(bf16[96,1024]{1,0:T(8,128)(2,1)S(1)} %slice_bitcast_fusion.28), channel_id=1, source_target_pairs={{0,8},{2,10},{4,12},{6,14},{8,0},{10,2},{12,4},{14,6},{16,24},{18,... | collective-permute-start | bytes 589832 | tf_op jit(solution)/shard_map/while/body/cond/branch_2_fun/ppermute | solution.py:24
  115.1 1.2 collective-permute-start.33
  116.3 3.0 %collective-permute-done.31 = bf16[96,1024]{1,0:T(8,128)(2,1)S(1)} collective-permute-done((bf16[96,1024]{1,0:T(8,128)(2,1)S(1)}, bf16[96,1024]{1,0:T(8,128)(2,1)S(1)}, u32[]{:S(2)}, u32[]{:S(2)}) %collective-permute-start.31) | collective-permute-done | bytes 196640 | tf_op jit(solution)/shard_map/while/body/cond/branch_2_fun/ppermute | solution.py:24
  119.3 1.5 %collective-permute-done.33 = bf16[96,1024]{1,0:T(8,128)(2,1)S(1)} collective-permute-done((bf16[96,1024]{1,0:T(8,128)(2,1)S(1)}, bf16[96,1024]{1,0:T(8,128)(2,1)S(1)}, u32[]{:S(2)}, u32[]{:S(2)}) %collective-permute-start.33) | collective-permute-done | bytes 196640 | tf_op jit(solution)/shard_map/while/body/cond/branch_2_fun/ppermute | solution.py:24
  121.0 1.3 collective-permute-start.34
  122.2 7.5 %collective-permute-done.34 = bf16[48,2048]{1,0:T(8,128)(2,1)S(1)} collective-permute-done((bf16[48,2048]{1,0:T(8,128)(2,1)S(1)}, bf16[48,2048]{1,0:T(8,128)(2,1)S(1)}, u32[]{:S(2)}, u32[]{:S(2)}) %collective-permute-start.34) | collective-permute-done | bytes 196640 | tf_op jit(solution)/shard_map/while/body/cond/branch_2_fun/ppermute | solution.py:24
  129.8 0.3 collective-permute-start.35
  130.1 4.5 %collective-permute-done.35 = bf16[24,2048]{1,0:T(8,128)(2,1)} collective-permute-done((bf16[24,2048]{1,0:T(8,128)(2,1)S(1)}, bf16[24,2048]{1,0:T(8,128)(2,1)}, u32[]{:S(2)}, u32[]{:S(2)}) %collective-permute-start.35) | collective-permute-done | bytes 98336 | tf_op jit(solution)/shard_map/while/body/cond/branch_2_fun/ppermute | solution.py:24
  134.6 0.9 select_select_fusion.3
  135.5 0.3 fusion.29
  135.8 1.1 fusion.24
  (55 shorter events, 0.6 us)
Async XLA Ops:
  0.6 43.4 %copy-start = (bf16[64,2048]{1,0:T(8,128)(2,1)S(1)}, bf16[64,2048]{1,0:T(8,128)(2,1)}, u32[]{:S(2)}) copy-start(bf16[64,2048]{1,0:T(8,128)(2,1)} %refs_4_.1) | copy-start | bytes 786436
  0.6 53.4 %collective-permute-start.49 = (bf16[2,704,2048]{2,1,0:T(8,128)(2,1)}, bf16[2,704,2048]{2,1,0:T(8,128)(2,1)}, u32[]{:S(2)}, u32[]{:S(2)}) collective-permute-start(bf16[2,704,2048]{2,1,0:T(8,128)(2,1)} %bitcast.224), channel_id=1, source_target_pairs={{0,2},{2,0},{4,6},{6,4},{8,10},{10,8},{12,14},{14,12},{16,18},{18,... | collective-permute-start | bytes 17301512 | tf_op jit(solution)/shard_map/ppermute | solution.py:24
  1.2 16.5 %collective-permute-start.41 = (bf16[64,2048]{1,0:T(8,128)(2,1)}, bf16[64,2048]{1,0:T(8,128)(2,1)S(1)}, u32[]{:S(2)}, u32[]{:S(2)}) collective-permute-start(bf16[64,2048]{1,0:T(8,128)(2,1)} %refs_4_.1), channel_id=1, source_target_pairs={{0,16},{2,18},{4,20},{6,22},{8,24},{10,26},{12,28},{14,30},{16,0},... | collective-permute-start | bytes 786440 | tf_op jit(solution)/shard_map/ppermute | solution.py:24
  4.8 16.5 %collective-permute-start.39 = (bf16[64,2048]{1,0:T(8,128)(2,1)}, bf16[64,2048]{1,0:T(8,128)(2,1)S(1)}, u32[]{:S(2)}, u32[]{:S(2)}) collective-permute-start(bf16[64,2048]{1,0:T(8,128)(2,1)} %refs_4_.1), channel_id=1, source_target_pairs={{0,8},{2,10},{4,12},{6,14},{8,0},{10,2},{12,4},{14,6},{16,24},{18,... | collective-permute-start | bytes 786440 | tf_op jit(solution)/shard_map/ppermute | solution.py:24
  6.4 47.6 %collective-permute-start.50 = (bf16[704,2048]{1,0:T(8,128)(2,1)}, bf16[704,2048]{1,0:T(8,128)(2,1)}, u32[]{:S(2)}, u32[]{:S(2)}) collective-permute-start(bf16[704,2048]{1,0:T(8,128)(2,1)} %bitcast.226), channel_id=1, source_target_pairs={{0,2},{2,0},{4,6},{6,4},{8,10},{10,8},{12,14},{14,12},{16,18},{18,... | collective-permute-start | bytes 8650760 | tf_op jit(solution)/shard_map/ppermute | solution.py:24
  17.7 7.0 %collective-permute-start.43 = (bf16[64,1024]{1,0:T(8,128)(2,1)S(1)}, bf16[64,1024]{1,0:T(8,128)(2,1)S(1)}, u32[]{:S(2)}, u32[]{:S(2)}) collective-permute-start(bf16[64,1024]{1,0:T(8,128)(2,1)S(1)} %slice.263), channel_id=1, source_target_pairs={{0,8},{2,10},{4,12},{6,14},{8,0},{10,2},{12,4},{14,6},{16,24},{18,... | collective-permute-start | bytes 393224 | tf_op jit(solution)/shard_map/ppermute | solution.py:24
  18.5 14.5 %collective-permute-start.42 = (bf16[64,2048]{1,0:T(8,128)(2,1)S(1)}, bf16[64,2048]{1,0:T(8,128)(2,1)S(1)}, u32[]{:S(2)}, u32[]{:S(2)}) collective-permute-start(bf16[64,2048]{1,0:T(8,128)(2,1)S(1)} %collective-permute-done.41.refs_8_), channel_id=1, source_target_pairs={{0,4},{2,6},{4,0},{6,2},{8,12},{10,14},{12,8},{14,10},{16,20},{18,... | collective-permute-start | bytes 786440 | tf_op jit(solution)/shard_map/ppermute | solution.py:24
  21.4 10.1 %collective-permute-start.44 = (bf16[64,1024]{1,0:T(8,128)(2,1)S(1)}, bf16[64,1024]{1,0:T(8,128)(2,1)S(1)}, u32[]{:S(2)}, u32[]{:S(2)}) collective-permute-start(bf16[64,1024]{1,0:T(8,128)(2,1)S(1)} %slice.264), channel_id=1, source_target_pairs={{0,16},{2,18},{4,20},{6,22},{8,24},{10,26},{12,28},{14,30},{16,0},... | collective-permute-start | bytes 393224 | tf_op jit(solution)/shard_map/ppermute | solution.py:24
  24.7 11.8 %collective-permute-start.40 = (bf16[64,2048]{1,0:T(8,128)(2,1)S(1)}, bf16[64,2048]{1,0:T(8,128)(2,1)S(1)}, u32[]{:S(2)}, u32[]{:S(2)}) collective-permute-start(bf16[64,2048]{1,0:T(8,128)(2,1)S(1)} %collective-permute-done.39.refs_6_), channel_id=1, source_target_pairs={{0,4},{2,6},{4,0},{6,2},{8,12},{10,14},{12,8},{14,10},{16,20},{18,... | collective-permute-start | bytes 786440 | tf_op jit(solution)/shard_map/ppermute | solution.py:24
  31.5 12.6 %collective-permute-start.38 = (bf16[64,2048]{1,0:T(8,128)(2,1)}, bf16[64,2048]{1,0:T(8,128)(2,1)S(1)}, u32[]{:S(2)}, u32[]{:S(2)}) collective-permute-start(bf16[64,2048]{1,0:T(8,128)(2,1)} %refs_4_.1), channel_id=1, source_target_pairs={{0,4},{2,6},{4,0},{6,2},{8,12},{10,14},{12,8},{14,10},{16,20},{18,... | collective-permute-start | bytes 786440 | tf_op jit(solution)/shard_map/ppermute | solution.py:24
  33.0 10.5 %collective-permute-start.36 = (bf16[128,1024]{1,0:T(8,128)(2,1)}, bf16[128,1024]{1,0:T(8,128)(2,1)S(1)}, u32[]{:S(2)}, u32[]{:S(2)}) collective-permute-start(bf16[128,1024]{1,0:T(8,128)(2,1)} %bitcast.202), channel_id=1, source_target_pairs={{0,1},{2,3},{4,5},{6,7},{8,9},{10,11},{12,13},{14,15},{16,17},{18,... | collective-permute-start | bytes 786440 | tf_op jit(solution)/shard_map/ppermute | solution.py:350
  36.5 10.3 %collective-permute-start.37 = (bf16[128,1024]{1,0:T(8,128)(2,1)}, bf16[128,1024]{1,0:T(8,128)(2,1)S(1)}, u32[]{:S(2)}, u32[]{:S(2)}) collective-permute-start(bf16[128,1024]{1,0:T(8,128)(2,1)} %bitcast.204), channel_id=1, source_target_pairs={{0,1},{2,3},{4,5},{6,7},{8,9},{10,11},{12,13},{14,15},{16,17},{18,... | collective-permute-start | bytes 786440 | tf_op jit(solution)/shard_map/ppermute | solution.py:351
  37.8 9.0 %copy-start.2 = (bf16[1,128,1024]{2,1,0:T(8,128)(2,1)S(1)}, bf16[1,128,1024]{2,1,0:T(8,128)(2,1)}, u32[]{:S(2)}) copy-start(bf16[1,128,1024]{2,1,0:T(8,128)(2,1)} %param.20) | copy-start | bytes 786436
  37.8 8.9 %copy-start.3 = (bf16[1,128,1024]{2,1,0:T(8,128)(2,1)S(1)}, bf16[1,128,1024]{2,1,0:T(8,128)(2,1)}, u32[]{:S(2)}) copy-start(bf16[1,128,1024]{2,1,0:T(8,128)(2,1)} %param.21) | copy-start | bytes 786436
  37.8 8.9 %copy-start.4 = (bf16[1,128,1024]{2,1,0:T(8,128)(2,1)S(1)}, bf16[1,128,1024]{2,1,0:T(8,128)(2,1)}, u32[]{:S(2)}) copy-start(bf16[1,128,1024]{2,1,0:T(8,128)(2,1)} %param.22) | copy-start | bytes 786436
  43.5 6.5 %collective-permute-start.45 = (bf16[64,2048]{1,0:T(8,128)(2,1)S(1)}, bf16[64,2048]{1,0:T(8,128)(2,1)S(1)}, u32[]{:S(2)}, u32[]{:S(2)}) collective-permute-start(bf16[64,2048]{1,0:T(8,128)(2,1)S(1)} %constant_dynamic-update-slice_fusion.9.refs_10_), channel_id=1, source_target_pairs={{0,4},{2,6},{4,0},{6,2},{8,12},{10,14},{12,8},{14,10},{16,20},{18,... | collective-permute-start | bytes 786440 | tf_op jit(solution)/shard_map/ppermute | solution.py:24
  44.0 6.8 %collective-permute-start.47 = (bf16[2,64,2048]{2,1,0:T(8,128)(2,1)S(1)}, bf16[2,64,2048]{2,1,0:T(8,128)(2,1)S(1)}, u32[]{:S(2)}, u32[]{:S(2)}) collective-permute-start(bf16[2,64,2048]{2,1,0:T(8,128)(2,1)S(1)} %pad_maximum_fusion.13), channel_id=1, source_target_pairs={{0,2},{2,0},{4,6},{6,4},{8,10},{10,8},{12,14},{14,12},{16,18},{18,... | collective-permute-start | bytes 1572872 | tf_op jit(solution)/shard_map/ppermute | solution.py:24
  46.7 5.5 %collective-permute-start.46 = (bf16[4,64,2048]{2,1,0:T(8,128)(2,1)S(1)}, bf16[4,64,2048]{2,1,0:T(8,128)(2,1)S(1)}, u32[]{:S(2)}, u32[]{:S(2)}) collective-permute-start(bf16[4,64,2048]{2,1,0:T(8,128)(2,1)S(1)} %pad_maximum_fusion.12), channel_id=1, source_target_pairs={{0,2},{2,0},{4,6},{6,4},{8,10},{10,8},{12,14},{14,12},{16,18},{18,... | collective-permute-start | bytes 3145736 | tf_op jit(solution)/shard_map/ppermute | solution.py:24
  50.0 2.1 %collective-permute-start.48 = (bf16[2,64,2048]{2,1,0:T(8,128)(2,1)S(1)}, bf16[2,64,2048]{2,1,0:T(8,128)(2,1)S(1)}, u32[]{:S(2)}, u32[]{:S(2)}) collective-permute-start(bf16[2,64,2048]{2,1,0:T(8,128)(2,1)S(1)} %pad_maximum_fusion.14), channel_id=1, source_target_pairs={{0,2},{2,0},{4,6},{6,4},{8,10},{10,8},{12,14},{14,12},{16,18},{18,... | collective-permute-start | bytes 1572872 | tf_op jit(solution)/shard_map/ppermute | solution.py:24
  50.9 1.5 %copy-start.1 = (bf16[1,128,2048]{2,1,0:T(8,128)(2,1)S(1)}, bf16[1,128,2048]{2,1,0:T(8,128)(2,1)}, u32[]{:S(2)}) copy-start(bf16[1,128,2048]{2,1,0:T(8,128)(2,1)} %param.23) | copy-start | bytes 1572868
  50.9 1.5 %copy-start.5 = (f32[2048]{0:T(1024)S(1)}, f32[2048]{0:T(1024)}, u32[]{:S(2)}) copy-start(f32[2048]{0:T(1024)} %param.25) | copy-start | bytes 24580
  52.3 1.7 %copy-start.7 = (s32[16]{0:T(128)S(1)}, s32[16]{0:T(128)}, u32[]{:S(2)}) copy-start(s32[16]{0:T(128)} %param.31) | copy-start | bytes 196
  56.3 5.1 %collective-permute-start.12 = (bf16[24,2048]{1,0:T(8,128)(2,1)S(1)}, bf16[24,2048]{1,0:T(8,128)(2,1)S(1)}, u32[]{:S(2)}, u32[]{:S(2)}) collective-permute-start(bf16[24,2048]{1,0:T(8,128)(2,1)S(1)} %get-tuple-element.181), channel_id=1, source_target_pairs={{0,4},{2,6},{4,0},{6,2},{8,12},{10,14},{12,8},{14,10},{16,20},{18,... | collective-permute-start | bytes 294920 | tf_op jit(solution)/shard_map/while/body/cond/branch_2_fun/ppermute | solution.py:24
  61.4 11.3 %collective-permute-start.13 = (bf16[48,2048]{1,0:T(8,128)(2,1)S(1)}, bf16[48,2048]{1,0:T(8,128)(2,1)S(1)}, u32[]{:S(2)}, u32[]{:S(2)}) collective-permute-start(bf16[48,2048]{1,0:T(8,128)(2,1)S(1)} %pad_maximum_fusion.8), channel_id=1, source_target_pairs={{0,16},{2,18},{4,20},{6,22},{8,24},{10,26},{12,28},{14,30},{16,0},... | collective-permute-start | bytes 589832 | tf_op jit(solution)/shard_map/while/body/cond/branch_2_fun/ppermute | solution.py:24
  72.9 7.5 %collective-permute-start.16 = (bf16[96,1024]{1,0:T(8,128)(2,1)S(1)}, bf16[96,1024]{1,0:T(8,128)(2,1)S(1)}, u32[]{:S(2)}, u32[]{:S(2)}) collective-permute-start(bf16[96,1024]{1,0:T(8,128)(2,1)S(1)} %get-tuple-element.275), channel_id=1, source_target_pairs={{0,1},{1,0},{2,3},{3,2},{4,5},{5,4},{6,7},{7,6},{8,9},{9,8},{10,11... | collective-permute-start | bytes 589832 | tf_op jit(solution)/shard_map/while/body/cond/branch_2_fun/ppermute | solution.py:24
  75.3 6.5 %collective-permute-start.14 = (bf16[96,1024]{1,0:T(8,128)(2,1)S(1)}, bf16[96,1024]{1,0:T(8,128)(2,1)S(1)}, u32[]{:S(2)}, u32[]{:S(2)}) collective-permute-start(bf16[96,1024]{1,0:T(8,128)(2,1)S(1)} %get-tuple-element.276), channel_id=1, source_target_pairs={{0,8},{2,10},{4,12},{6,14},{8,0},{10,2},{12,4},{14,6},{16,24},{18,... | collective-permute-start | bytes 589832 | tf_op jit(solution)/shard_map/while/body/cond/branch_2_fun/ppermute | solution.py:24
  80.4 10.6 %collective-permute-start.17 = (bf16[2,96,1024]{2,1,0:T(8,128)(2,1)S(1)}, bf16[2,96,1024]{2,1,0:T(8,128)(2,1)S(1)}, u32[]{:S(2)}, u32[]{:S(2)}) collective-permute-start(bf16[2,96,1024]{2,1,0:T(8,128)(2,1)S(1)} %get-tuple-element.278), channel_id=1, source_target_pairs={{0,8},{2,10},{4,12},{6,14},{8,0},{10,2},{12,4},{14,6},{16,24},{18,... | collective-permute-start | bytes 1179656 | tf_op jit(solution)/shard_map/while/body/cond/branch_2_fun/ppermute | solution.py:24
  81.9 9.9 %collective-permute-start.15 = (bf16[2,96,1024]{2,1,0:T(8,128)(2,1)S(1)}, bf16[2,96,1024]{2,1,0:T(8,128)(2,1)S(1)}, u32[]{:S(2)}, u32[]{:S(2)}) collective-permute-start(bf16[2,96,1024]{2,1,0:T(8,128)(2,1)S(1)} %get-tuple-element.272), channel_id=1, source_target_pairs={{0,1},{1,0},{2,3},{3,2},{4,5},{5,4},{6,7},{7,6},{8,9},{9,8},{10,11... | collective-permute-start | bytes 1179656 | tf_op jit(solution)/shard_map/while/body/cond/branch_2_fun/ppermute | solution.py:24
  92.1 1.2 copy-start.6
  103.3 9.1 %collective-permute-start.30 = (bf16[2,96,1024]{2,1,0:T(8,128)(2,1)S(1)}, bf16[2,96,1024]{2,1,0:T(8,128)(2,1)}, u32[]{:S(2)}, u32[]{:S(2)}) collective-permute-start(bf16[2,96,1024]{2,1,0:T(8,128)(2,1)S(1)} %slice_bitcast_fusion.24), channel_id=1, source_target_pairs={{0,1},{1,0},{2,3},{3,2},{4,5},{5,4},{6,7},{7,6},{8,9},{9,8},{10,11... | collective-permute-start | bytes 1179656 | tf_op jit(solution)/shard_map/while/body/cond/branch_2_fun/ppermute | solution.py:24
  104.2 10.9 %collective-permute-start.32 = (bf16[2,96,1024]{2,1,0:T(8,128)(2,1)S(1)}, bf16[2,96,1024]{2,1,0:T(8,128)(2,1)S(1)}, u32[]{:S(2)}, u32[]{:S(2)}) collective-permute-start(bf16[2,96,1024]{2,1,0:T(8,128)(2,1)S(1)} %slice_bitcast_fusion.22), channel_id=1, source_target_pairs={{0,8},{2,10},{4,12},{6,14},{8,0},{10,2},{12,4},{14,6},{16,24},{18,... | collective-permute-start | bytes 1179656 | tf_op jit(solution)/shard_map/while/body/cond/branch_2_fun/ppermute | solution.py:24
  113.6 5.7 %collective-permute-start.31 = (bf16[96,1024]{1,0:T(8,128)(2,1)S(1)}, bf16[96,1024]{1,0:T(8,128)(2,1)S(1)}, u32[]{:S(2)}, u32[]{:S(2)}) collective-permute-start(bf16[96,1024]{1,0:T(8,128)(2,1)S(1)} %slice_bitcast_fusion.28), channel_id=1, source_target_pairs={{0,8},{2,10},{4,12},{6,14},{8,0},{10,2},{12,4},{14,6},{16,24},{18,... | collective-permute-start | bytes 589832 | tf_op jit(solution)/shard_map/while/body/cond/branch_2_fun/ppermute | solution.py:24
  115.1 5.7 %collective-permute-start.33 = (bf16[96,1024]{1,0:T(8,128)(2,1)S(1)}, bf16[96,1024]{1,0:T(8,128)(2,1)S(1)}, u32[]{:S(2)}, u32[]{:S(2)}) collective-permute-start(bf16[96,1024]{1,0:T(8,128)(2,1)S(1)} %slice_bitcast_fusion.26), channel_id=1, source_target_pairs={{0,1},{1,0},{2,3},{3,2},{4,5},{5,4},{6,7},{7,6},{8,9},{9,8},{10,11... | collective-permute-start | bytes 589832 | tf_op jit(solution)/shard_map/while/body/cond/branch_2_fun/ppermute | solution.py:24
  121.0 8.7 %collective-permute-start.34 = (bf16[48,2048]{1,0:T(8,128)(2,1)S(1)}, bf16[48,2048]{1,0:T(8,128)(2,1)S(1)}, u32[]{:S(2)}, u32[]{:S(2)}) collective-permute-start(bf16[48,2048]{1,0:T(8,128)(2,1)S(1)} %pad_maximum_fusion.11), channel_id=1, source_target_pairs={{0,16},{2,18},{4,20},{6,22},{8,24},{10,26},{12,28},{14,30},{16,0},... | collective-permute-start | bytes 589832 | tf_op jit(solution)/shard_map/while/body/cond/branch_2_fun/ppermute | solution.py:24
  129.8 4.8 %collective-permute-start.35 = (bf16[24,2048]{1,0:T(8,128)(2,1)S(1)}, bf16[24,2048]{1,0:T(8,128)(2,1)}, u32[]{:S(2)}, u32[]{:S(2)}) collective-permute-start(bf16[24,2048]{1,0:T(8,128)(2,1)S(1)} %get-tuple-element.283), channel_id=1, source_target_pairs={{0,4},{2,6},{4,0},{6,2},{8,12},{10,14},{12,8},{14,10},{16,20},{18,... | collective-permute-start | bytes 294920 | tf_op jit(solution)/shard_map/while/body/cond/branch_2_fun/ppermute | solution.py:24
where the time goes:
time: 135 us; the launch traced here: 137 us
  waiting for transfers between devices  74.1 us (55%)
  starting transfers between devices  31 us (23%)
  Pallas kernels  14.9 us (11%)
  local copies, waits for them, and re-layouts  8.1 us (6%)
  between operations  2.82 us (2%)
  other arithmetic  2.74 us (2%)
  loops' own time  1.79 us (1%)
  matrix products  1.41 us (1%)
    ppermute x25, waiting for transfers between devices, hop(): return lax.ppermute(array, axis, [(i, i ^ bit) for i in range(size)])  66 us
    ppermute x25, starting transfers between devices, hop(): return lax.ppermute(array, axis, [(i, i ^ bit) for i in range(size)])  26.3 us
    pallas_call x1, Pallas kernels, one_pass(): pl.pallas_call(expert_kernel, out_shape=jax.ShapeDtypeStruct((row_count,...  10 us
    ppermute x1, waiting for transfers between devices, body_move_rows(): key_before = lax.ppermute(key_vecs[0], 'ctx', [(0, 1)])  5.61 us
    ppermute x1, starting transfers between devices, body_move_rows(): key_before = lax.ppermute(key_vecs[0], 'ctx', [(0, 1)])  3.43 us
    pallas_call x1, Pallas kernels, body_move_rows(): pl.pallas_call(attend_kernel, out_shape=(jax.ShapeDtypeStruct((HEADS, tok...  3.22 us
  transfers between devices with their start and end apart: 27, of which 15 were waited for; matrix products, arithmetic and copies ran while one was open for 6% of the time, Pallas kernels for 4%

commit v1 on v0

--- a/solution.py
+++ b/solution.py
@@ -149,7 +149,7 @@
     return (attn_proj[None], expert_sum[None])
 
 
-def attend_kernel(info, query, key, value, key_before, value_before, ids, gates, attended, place, gate_values):
+def attend_kernel(info, query, key, value, before_both, ids, gates, attended, place, gate_values):
     token_count = query.shape[0]
     row = lax.broadcasted_iota(jnp.int32, (token_count, token_count), 0)
     col = lax.broadcasted_iota(jnp.int32, (token_count, token_count), 1)
@@ -163,7 +163,7 @@
             heads, key[:, span], contract_last, preferred_element_type=jnp.float32
         )
         before = lax.dot_general(
-            heads, key_before[:, span], contract_last, preferred_element_type=jnp.float32
+            heads, before_both[0, :, span], contract_last, preferred_element_type=jnp.float32
         )
         own = jnp.where(own_visible, own * HD ** (-0.5), -jnp.inf)
         before = jnp.where(before_visible, before * HD ** (-0.5), -jnp.inf)
@@ -176,7 +176,7 @@
         mixed = jnp.dot(
             own.astype(jnp.bfloat16), value[:, span], preferred_element_type=jnp.float32
         ) + jnp.dot(
-            before.astype(jnp.bfloat16), value_before[:, span], preferred_element_type=jnp.float32
+            before.astype(jnp.bfloat16), before_both[1, :, span], preferred_element_type=jnp.float32
         )
         mixed = mixed / total
         swapped = pltpu.roll(mixed, HD // 2, 1)
@@ -272,19 +272,20 @@
         span = slice(start, start + size)
         arrived[2 * k].wait()
         gate_proj = lax.dot_general(
-            rows[...], gate_up[0, span], contract_last, preferred_element_type=jnp.float32
+            gate_up[0, span], rows[...], contract_last, preferred_element_type=jnp.float32
         )
         arrived[2 * k + 1].wait()
         up_proj = lax.dot_general(
-            rows[...], gate_up[1, span], contract_last, preferred_element_type=jnp.float32
-        )
-        hidden[:, span] = (gate_proj / (1.0 + jnp.exp(-gate_proj)) * up_proj).astype(jnp.bfloat16)
+            gate_up[1, span], rows[...], contract_last, preferred_element_type=jnp.float32
+        )
+        hidden[span] = (gate_proj / (1.0 + jnp.exp(-gate_proj)) * up_proj).astype(jnp.bfloat16)
     arrived[-1].wait()
     width = made.shape[1]
+    contract_first = (((0,), (0,)), ((), ()))
     for start in range(0, width, 512):
         span = slice(start, start + 512)
-        made[:, span] = jnp.dot(
-            hidden[...], down[:, span], preferred_element_type=jnp.float32
+        made[:, span] = lax.dot_general(
+            hidden[...], down[:, span], contract_first, preferred_element_type=jnp.float32
         ).astype(jnp.bfloat16)
 
 
@@ -347,34 +348,32 @@
     ctx = lax.axis_index("ctx")
     bits = [1 << k for k in reversed(range(1, dp_size.bit_length() - 1))]
 
-    key_before = lax.ppermute(key_vecs[0], "ctx", [(0, 1)])
-    value_before = lax.ppermute(value_vecs[0], "ctx", [(0, 1)])
+    before = lax.ppermute(jnp.stack([key_vecs[0], value_vecs[0]]), "ctx", [(0, 1)])
     z_far, z_near, x_bit = bits
-    half = width // 2
-    near = [None] * HEADS
-    near[0] = w_out
-    near[z_near >> 1] = hop(w_out, "dp", dp_size, z_near)
-    near[z_far >> 1] = hop(w_out, "dp", dp_size, z_far)
-    near[x_bit >> 1] = hop(w_out, "dp", dp_size, x_bit)
-    near[(z_near | x_bit) >> 1] = hop(near[z_near >> 1], "dp", dp_size, x_bit)
-    near[(z_far | x_bit) >> 1] = hop(near[z_far >> 1], "dp", dp_size, x_bit)
-    z_both = jnp.concatenate(
-        [
-            hop(near[z_far >> 1][:, :half], "dp", dp_size, z_near),
-            hop(near[z_near >> 1][:, half:], "dp", dp_size, z_far),
-        ],
-        axis=1,
-    )
-    near[(z_far | z_near) >> 1] = z_both
-    near[(z_far | z_near | x_bit) >> 1] = hop(z_both, "dp", dp_size, x_bit)
-    far = [None] * HEADS
-    for group in ([0, z_near >> 1, z_far >> 1, x_bit >> 1], [(z_near | x_bit) >> 1, (z_far | x_bit) >> 1], [(z_far | z_near) >> 1, (z_far | z_near | x_bit) >> 1]):
+    z_both = z_far | z_near
+    near = {0: w_out}
+    for bit in (z_near, x_bit, z_far):
+        near[bit] = hop(w_out, "dp", dp_size, bit)
+    near[z_near], near[x_bit] = lax.optimization_barrier((near[z_near], near[x_bit]))
+    near[z_near | x_bit] = hop(near[z_near], "dp", dp_size, x_bit)
+    near[z_far], before = lax.optimization_barrier((near[z_far], before))
+    near[z_both] = hop(near[z_far], "dp", dp_size, z_near)
+    next_sent, near[z_near | x_bit] = lax.optimization_barrier(
+        (near[z_far], near[z_near | x_bit])
+    )
+    near[z_far | x_bit] = hop(next_sent, "dp", dp_size, x_bit)
+    near[z_both | x_bit] = hop(near[z_both], "dp", dp_size, x_bit)
+    far = {}
+    for group in (
+        (0, z_near, x_bit, z_far),
+        (z_near | x_bit, z_far | x_bit, z_both),
+        (z_both | x_bit,),
+    ):
         came = hop(jnp.stack([near[j] for j in group]), "dp", dp_size, 1)
         for k, j in enumerate(group):
             far[j] = came[k]
+    shares = [near[2 * j] for j in range(HEADS)] + [far[2 * j] for j in range(HEADS)]
     gate_up_near = jnp.swapaxes(w_gate_up[0], 1, 2)
-    gate_up_far = hop(gate_up_near, "dp", dp_size, 1)
-    down_far = hop(w_down[0], "dp", dp_size, 1)
 
     info = jnp.stack([ctx, me >> 1, core, capacity[0, 0, 0], capacity[0, 0, 1]]).astype(jnp.int32)
     slots = PASS_SPECIALISTS * CAP
@@ -385,7 +384,7 @@
             jax.ShapeDtypeStruct((token_count, slots), jnp.bfloat16),
             jax.ShapeDtypeStruct((token_count, PASS_SPECIALISTS), jnp.float32),
         ),
-        in_specs=[pl.BlockSpec(memory_space=pltpu.SMEM)] + vmem(7),
+        in_specs=[pl.BlockSpec(memory_space=pltpu.SMEM)] + vmem(6),
         out_specs=tuple(vmem(3)),
         cost_estimate=pl.CostEstimate(
             flops=4 * HEADS * HD * 2 * token_count * token_count,
@@ -398,8 +397,7 @@
         query_vecs[0],
         key_vecs[0],
         value_vecs[0],
-        key_before,
-        value_before,
+        before,
         expert_ids[0],
         route_gates[0],
     )
@@ -418,7 +416,7 @@
             transcendentals=0,
         ),
         compiler_params=pltpu.CompilerParams(vmem_limit_bytes=24 * 2**20),
-    )(attended, residual[0], norm_gain[None], place, *near, *far)
+    )(attended, residual[0], norm_gain[None], place, *shares)
 
     owners = expert_owner[:PASS_SPECIALISTS]
     differ = owners[0] ^ owners[1]
@@ -437,8 +435,10 @@
         rest = [b for b in bits if b != bit]
 
         def run(kept, sent):
+            gate_up_far = hop(gate_up_near, "dp", dp_size, 1)
+            down_far = hop(w_down[0], "dp", dp_size, 1)
             unit = jnp.concatenate([kept, hop(sent, "dp", dp_size, bit)], axis=0)
-            return gather_rows(unit, rest, dp_size)
+            return gather_rows(unit, rest, dp_size), gate_up_far, down_far
 
         return run
 
@@ -458,7 +458,9 @@
         offset = me ^ owner
         kept = jnp.where(local == 0, chosen[:CAP], chosen[CAP:])
         sent = jnp.where(sent_expert == 0, chosen[:CAP], chosen[CAP:])
-        rows = lax.switch(branch, [dispatch(bit) for bit in bits], kept, sent)
+        rows, gate_up_far, down_far = lax.switch(
+            branch, [dispatch(bit) for bit in bits], kept, sent
+        )
         made = pl.pallas_call(
             expert_kernel,
             out_shape=jax.ShapeDtypeStruct((row_count, width), jnp.bfloat16),
@@ -469,7 +471,7 @@
             scratch_shapes=[
                 pltpu.VMEM((2, units, width), jnp.bfloat16),
                 pltpu.VMEM((units, width), jnp.bfloat16),
-                pltpu.VMEM((row_count, units), jnp.bfloat16),
+                pltpu.VMEM((units, row_count), jnp.bfloat16),
                 pltpu.SemaphoreType.DMA((2 * -(-units // 256) + 1,)),
             ],
             cost_estimate=pl.CostEstimate(
@@ -477,7 +479,7 @@
                 bytes_accessed=6 * units * width,
                 transcendentals=row_count * units,
             ),
-            compiler_params=pltpu.CompilerParams(vmem_limit_bytes=40 * 2**20),
+            compiler_params=pltpu.CompilerParams(vmem_limit_bytes=52 * 2**20),
         )((offset & 1)[None], rows, gate_up_near, gate_up_far, w_down[0], down_far)
         own, other = lax.switch(branch, [give_back(bit) for bit in bits], made, offset)
         served = jnp.where((offset & bits[0]) == 0, own, other)

time: 135 us -> 127 us (0.941); the launches traced: 137 us -> 125 us
  waiting for transfers between devices: 74.1 us -> 65.6 us
  other arithmetic: 2.74 us -> 7.36 us
  starting transfers between devices: 31 us -> 26.5 us
  Pallas kernels: 14.9 us -> 12 us
    ppermute x2 -> x1, waiting for transfers between devices: 8.17 us -> 0.01 us  [body_move_rows(): lax.ppermute(jnp.stack([key_vecs[0], value_vecs[0]]), 'ctx', [(0, 1)])]
    ppermute x25 -> x24, starting transfers between devices: 26.3 us -> 21.6 us  [hop(): return lax.ppermute(array, axis, [(i, i ^ bit) for i in range(size)])]
    another operation x3 -> x2, other arithmetic: 0.24 us -> 3.13 us  [body_move_rows(): came = hop(jnp.stack([near[j] for j in group]), 'dp', dp_size, 1)]
    pallas_call x1, Pallas kernels: 10 us -> 7.13 us  [one_pass(): pl.pallas_call(expert_kernel, out_shape=jax.ShapeDtypeStruct((row_count,...]
    squeeze x3 -> x2, local copies, waits for them, and re-layouts: 0.18 us -> 2.46 us  [body_move_rows(): far[j] = came[k]]
    unnamed x17 -> x22, local copies, waits for them, and re-layouts: 1.64 us -> 0.28 us
    ppermute x25 -> x24, waiting for transfers between devices: 66 us -> 65.6 us  [hop(): return lax.ppermute(array, axis, [(i, i ^ bit) for i in range(size)])]
    ppermute x2 -> x1, starting transfers between devices: 4.74 us -> 4.9 us  [body_move_rows(): lax.ppermute(jnp.stack([key_vecs[0], value_vecs[0]]), 'ctx', [(0, 1)])]
  transfers between devices with their start and end apart: 27 -> 25, of which waited for: 15 -> 17; matrix products, arithmetic and copies ran while one was open for 6% -> 8% of each run, Pallas kernels for 4% -> 3%
where the time goes in v1:
time: 127 us; the launch traced here: 125 us
  waiting for transfers between devices  65.6 us (52%)
  starting transfers between devices  26.5 us (21%)
  Pallas kernels  12 us (9%)
  other arithmetic  7.36 us (6%)
  local copies, waits for them, and re-layouts  7.04 us (6%)
  between operations  2.7 us (2%)
  matrix products  2.31 us (2%)
  loops' own time  1.51 us (1%)
    ppermute x24, waiting for transfers between devices, hop(): return lax.ppermute(array, axis, [(i, i ^ bit) for i in range(size)])  65.6 us
    ppermute x24, starting transfers between devices, hop(): return lax.ppermute(array, axis, [(i, i ^ bit) for i in range(size)])  21.6 us
    pallas_call x1, Pallas kernels, one_pass(): pl.pallas_call(expert_kernel, out_shape=jax.ShapeDtypeStruct((row_count,...  7.13 us
    ppermute x1, starting transfers between devices, body_move_rows(): lax.ppermute(jnp.stack([key_vecs[0], value_vecs[0]]), 'ctx', [(0, 1)])  4.9 us
    pallas_call x1, Pallas kernels, body_move_rows(): pl.pallas_call(attend_kernel, out_shape=(jax.ShapeDtypeStruct((HEADS, tok...  3.22 us
    another operation x2, other arithmetic, body_move_rows(): came = hop(jnp.stack([near[j] for j in group]), 'dp', dp_size, 1)  3.13 us
  transfers between devices with their start and end apart: 25, of which 17 were waited for; matrix products, arithmetic and copies ran while one was open for 8% of the time, Pallas kernels for 3%

profile of v1, /device:TPU:0, one launch (start us, length us, event | category | flops | bytes accessed | tf_op | source)
XLA Modules:
  0.0 125.0 jit_solution(12801091833798734564)
XLA Ops:
  0.6 1.1 pad_maximum_fusion.14
  1.7 4.9 %collective-permute-start.43 = (bf16[2,128,1024]{2,1,0:T(8,128)(2,1)S(1)}, bf16[2,128,1024]{2,1,0:T(8,128)(2,1)S(1)}, u32[]{:S(2)}, u32[]{:S(2)}) collective-permute-start(bf16[2,128,1024]{2,1,0:T(8,128)(2,1)S(1)} %pad_maximum_fusion.14), channel_id=1, source_target_pairs={{0,1},{2,3},{4,5},{6,7},{8,9},{10,11},{12,13},{14,15},{16,17},{18,... | collective-permute-start | bytes 1572872 | tf_op jit(solution)/shard_map/ppermute | solution.py:351
  6.6 1.6 %collective-permute-start.45 = (bf16[64,2048]{1,0:T(8,128)(2,1)}, bf16[64,2048]{1,0:T(8,128)(2,1)S(1)}, u32[]{:S(2)}, u32[]{:S(2)}) collective-permute-start(bf16[64,2048]{1,0:T(8,128)(2,1)} %refs_4_.1), channel_id=1, source_target_pairs={{0,4},{2,6},{4,0},{6,2},{8,12},{10,14},{12,8},{14,10},{16,20},{18,... | collective-permute-start | bytes 786440 | tf_op jit(solution)/shard_map/ppermute | solution.py:24
  8.2 1.6 %collective-permute-start.44 = (bf16[64,2048]{1,0:T(8,128)(2,1)}, bf16[64,2048]{1,0:T(8,128)(2,1)S(1)}, u32[]{:S(2)}, u32[]{:S(2)}) collective-permute-start(bf16[64,2048]{1,0:T(8,128)(2,1)} %refs_4_.1), channel_id=1, source_target_pairs={{0,8},{2,10},{4,12},{6,14},{8,0},{10,2},{12,4},{14,6},{16,24},{18,... | collective-permute-start | bytes 786440 | tf_op jit(solution)/shard_map/ppermute | solution.py:24
  9.8 2.6 %collective-permute-start.42 = (bf16[64,2048]{1,0:T(8,128)(2,1)}, bf16[64,2048]{1,0:T(8,128)(2,1)S(1)}, u32[]{:S(2)}, u32[]{:S(2)}) collective-permute-start(bf16[64,2048]{1,0:T(8,128)(2,1)} %refs_4_.1), channel_id=1, source_target_pairs={{0,16},{2,18},{4,20},{6,22},{8,24},{10,26},{12,28},{14,30},{16,0},... | collective-permute-start | bytes 786440 | tf_op jit(solution)/shard_map/ppermute | solution.py:24
  12.3 2.3 %collective-permute-done.45.refs_5_ = bf16[64,2048]{1,0:T(8,128)(2,1)S(1)} collective-permute-done((bf16[64,2048]{1,0:T(8,128)(2,1)}, bf16[64,2048]{1,0:T(8,128)(2,1)S(1)}, u32[]{:S(2)}, u32[]{:S(2)}) %collective-permute-start.45) | collective-permute-done | bytes 262176 | tf_op jit(solution)/shard_map/ppermute | solution.py:24
  14.7 6.7 %collective-permute-done.44.refs_6_ = bf16[64,2048]{1,0:T(8,128)(2,1)S(1)} collective-permute-done((bf16[64,2048]{1,0:T(8,128)(2,1)}, bf16[64,2048]{1,0:T(8,128)(2,1)S(1)}, u32[]{:S(2)}, u32[]{:S(2)}) %collective-permute-start.44) | collective-permute-done | bytes 262176 | tf_op jit(solution)/shard_map/ppermute | solution.py:24
  21.4 0.5 collective-permute-start.46
  21.9 1.9 %collective-permute-done.42.refs_8_ = bf16[64,2048]{1,0:T(8,128)(2,1)S(1)} collective-permute-done((bf16[64,2048]{1,0:T(8,128)(2,1)}, bf16[64,2048]{1,0:T(8,128)(2,1)S(1)}, u32[]{:S(2)}, u32[]{:S(2)}) %collective-permute-start.42) | collective-permute-done | bytes 262176 | tf_op jit(solution)/shard_map/ppermute | solution.py:24
  23.8 2.1 %pad_maximum_fusion.12 = bf16[4,64,2048]{2,1,0:T(8,128)(2,1)} fusion(bf16[1,64,2048]{2,1,0:T(8,128)(2,1)S(1)} %bitcast.201, bf16[1,64,2048]{2,1,0:T(8,128)(2,1)S(1)} %bitcast.199, bf16[1,64,2048]{2,1,0:T(8,128)(2,1)S(1)} %bitcast.200, bf16[1,64,2048]{2,1,0:T(8,128)(2,1)} %bitcast.198), kind=kLoop, calls=%fused_computation.100 | loop fusion | flops 1572864 | bytes 2097152 | tf_op jit(solution)/shard_map/stack | solution.py:372
  26.0 1.8 %collective-permute-done.46.refs_7_ = bf16[64,2048]{1,0:T(8,128)(2,1)S(1)} collective-permute-done((bf16[64,2048]{1,0:T(8,128)(2,1)S(1)}, bf16[64,2048]{1,0:T(8,128)(2,1)S(1)}, u32[]{:S(2)}, u32[]{:S(2)}) %collective-permute-start.46) | collective-permute-done | bytes 262176 | tf_op jit(solution)/shard_map/ppermute | solution.py:24
  27.7 0.5 collective-permute-start.47
  28.3 6.4 %collective-permute-done.47.refs_9_ = bf16[64,2048]{1,0:T(8,128)(2,1)S(1)} collective-permute-done((bf16[64,2048]{1,0:T(8,128)(2,1)S(1)}, bf16[64,2048]{1,0:T(8,128)(2,1)S(1)}, u32[]{:S(2)}, u32[]{:S(2)}) %collective-permute-start.47) | collective-permute-done | bytes 262176 | tf_op jit(solution)/shard_map/ppermute | solution.py:24
  34.7 0.3 collective-permute-done.48.refs_10_
  34.9 1.0 pad_maximum_fusion.13
  35.9 1.5 %collective-permute-start.49 = (bf16[64,2048]{1,0:T(8,128)(2,1)S(1)}, bf16[64,2048]{1,0:T(8,128)(2,1)S(1)}, u32[]{:S(2)}, u32[]{:S(2)}) collective-permute-start(bf16[64,2048]{1,0:T(8,128)(2,1)S(1)} %collective-permute-done.48.refs_10_), channel_id=1, source_target_pairs={{0,4},{2,6},{4,0},{6,2},{8,12},{10,14},{12,8},{14,10},{16,20},{18,... | collective-permute-start | bytes 786440 | tf_op jit(solution)/shard_map/ppermute | solution.py:24
  37.4 0.6 fusion.33
  39.9 0.1 copy.34
  40.0 0.1 copy.35
  40.1 0.6 fusion.34
  40.8 1.3 %stack.156.info = s32[5]{0:T(128)S(1)} concatenate(s32[1]{0:T(128)} %bitcast.64, s32[1]{0:T(128)} %bitcast.65, s32[1]{0:T(128)} %bitcast.66, s32[1]{0:T(128)} %bitcast.67, s32[1]{0:T(128)} %bitcast.68), dimensions={0} | concatenate | bytes 40 | tf_op jit(solution)/shard_map/stack | solution.py:378
  42.1 3.2 %shard_map.131 = (bf16[8,128,128]{2,1,0:T(8,128)(2,1)S(1)}, bf16[128,48]{1,0:T(8,128)(2,1)S(1)}, f32[128,2]{1,0:T(8,128)S(1)}) custom-call(s32[5]{0:T(128)S(1)} %stack.156.info, bf16[128,1024]{1,0:T(8,128)(2,1)S(1)} %bitcast.205, bf16[128,1024]{1,0:T(8,128)(2,1)S(1)} %bitcast.196, bf16[128,1024]{1,0:T(8,128)(2,1)S(1)} %bitcast.197, ...), custom_call_target="tpu_custom_call" | custom-call | flops 134217728 | bytes 1572864 | tf_op jit(solution)/shard_map/pallas_call | solution.py:380
  45.4 0.2 slice_reduce_fusion.1
  45.6 0.3 collective-permute-start.52
  45.9 1.3 %slice_bitcast_fusion.32 = (bf16[64,2048]{1,0:T(8,128)(2,1)S(1)}, bf16[64,2048]{1,0:T(8,128)(2,1)S(1)}, bf16[64,2048]{1,0:T(8,128)(2,1)S(1)}, bf16[64,2048]{1,0:T(8,128)(2,1)S(1)}) fusion(bf16[4,64,2048]{2,1,0:T(8,128)(2,1)} %collective-permute-done.50), kind=kLoop, calls=%fused_computation.105 | loop fusion | bytes 2097152 | tf_op jit(solution)/shard_map/squeeze | solution.py:374
  47.2 1.2 slice_bitcast_fusion.30
  48.4 1.7 %shard_map.132 = (bf16[128,2048]{1,0:T(8,128)(2,1)}, bf16[48,2048]{1,0:T(8,128)(2,1)S(1)}) custom-call(bf16[8,128,128]{2,1,0:T(8,128)(2,1)S(1)} %get-tuple-element.220.refs_0_, bf16[128,2048]{1,0:T(8,128)(2,1)S(1)} %bitcast.202, f32[1,2048]{1,0:T(1,128)S(1)} %bitcast.208, bf16[128,48]{1,0:T(8,128)(2,1)S(1)} %get-tuple-element.221.refs_3_, ...), custom_call_target="tpu_custom_call" | custom-call | flops 536870912 | bytes 4194304 | tf_op jit(solution)/shard_map/pallas_call | solution.py:404
  50.1 0.6 broadcast_in_dim.17
  50.7 72.0 %while.14 = (s32[]{:T(128)}, bf16[24,2048]{1,0:T(8,128)(2,1)}, bf16[24,2048]{1,0:T(8,128)(2,1)S(1)}, s32[]{:T(128)}, pred[]{:T(512)}, /*index=5*/s32[]{:T(128)},...) while((s32[]{:T(128)}, bf16[24,2048]{1,0:T(8,128)(2,1)}, ...), condition=%wide.region_7.8_spmd, body=%wide.region_0.7_spmd.sunk | while | flops 3331768320 | bytes 74712032 | solution.py:494
  50.7 0.6 fusion.38
  52.6 30.7 %conditional.4 = (bf16[384,2048]{1,0:T(8,128)(2,1)S(1)}, bf16[2,704,2048]{2,1,0:T(8,128)(2,1)}, bf16[704,2048]{1,0:T(8,128)(2,1)}) conditional(s32[]{:T(128)} %get-tuple-element.468, (bf16[24,2048]{1,0:T(8,128)(2,1)S(1)}, bf16[24,2048]{1,0:T(8,128)(2,1)S(1)}, bf16[2,704,2048]{2,1,0:T(8,128)(2,1)}, ...), branch_computations={%region_1.1_spmd, %region_2.2_spmd, %region_3.3_spmd} | conditional | flops 7077888 | bytes 51511640 | solution.py:461
  52.7 0.3 collective-permute-start.6
  53.0 0.2 collective-permute-start.7
  53.2 1.5 %collective-permute-start = (bf16[24,2048]{1,0:T(8,128)(2,1)S(1)}, bf16[24,2048]{1,0:T(8,128)(2,1)S(1)}, u32[]{:S(2)}, u32[]{:S(2)}) collective-permute-start(bf16[24,2048]{1,0:T(8,128)(2,1)S(1)} %get-tuple-element.167), channel_id=1, source_target_pairs={{0,16},{2,18},{4,20},{6,22},{8,24},{10,26},{12,28},{14,30},{16,0},... | collective-permute-start | bytes 294920 | tf_op jit(solution)/shard_map/while/body/cond/branch_0_fun/ppermute | solution.py:24
  54.7 6.5 %collective-permute-done = bf16[24,2048]{1,0:T(8,128)(2,1)S(1)} collective-permute-done((bf16[24,2048]{1,0:T(8,128)(2,1)S(1)}, bf16[24,2048]{1,0:T(8,128)(2,1)S(1)}, u32[]{:S(2)}, u32[]{:S(2)}) %collective-permute-start) | collective-permute-done | bytes 98336 | tf_op jit(solution)/shard_map/while/body/cond/branch_0_fun/ppermute | solution.py:24
  61.2 0.1 collective-permute-start.1
  61.3 6.6 %collective-permute-done.1 = bf16[48,2048]{1,0:T(8,128)(2,1)S(1)} collective-permute-done((bf16[48,2048]{1,0:T(8,128)(2,1)S(1)}, bf16[48,2048]{1,0:T(8,128)(2,1)S(1)}, u32[]{:S(2)}, u32[]{:S(2)}) %collective-permute-start.1) | collective-permute-done | bytes 196640 | tf_op jit(solution)/shard_map/while/body/cond/branch_0_fun/ppermute | solution.py:24
  67.9 0.1 slice_bitcast_fusion.1
  68.1 0.6 collective-permute-start.2
  68.7 5.1 %collective-permute-done.4 = bf16[96,1024]{1,0:T(8,128)(2,1)S(1)} collective-permute-done((bf16[96,1024]{1,0:T(8,128)(2,1)S(1)}, bf16[96,1024]{1,0:T(8,128)(2,1)S(1)}, u32[]{:S(2)}, u32[]{:S(2)}) %collective-permute-start.4) | collective-permute-done | bytes 196640 | tf_op jit(solution)/shard_map/while/body/cond/branch_0_fun/ppermute | solution.py:24
  73.8 0.6 collective-permute-start.5
  74.5 2.0 %collective-permute-start.3 = (bf16[2,96,1024]{2,1,0:T(8,128)(2,1)S(1)}, bf16[2,96,1024]{2,1,0:T(8,128)(2,1)S(1)}, u32[]{:S(2)}, u32[]{:S(2)}) collective-permute-start(bf16[2,96,1024]{2,1,0:T(8,128)(2,1)S(1)} %get-tuple-element.261), channel_id=1, source_target_pairs={{0,1},{1,0},{2,3},{3,2},{4,5},{5,4},{6,7},{7,6},{8,9},{9,8},{10,11... | collective-permute-start | bytes 1179656 | tf_op jit(solution)/shard_map/while/body/cond/branch_0_fun/ppermute | solution.py:24
  76.5 6.1 %collective-permute-done.5 = bf16[2,96,1024]{2,1,0:T(8,128)(2,1)S(1)} collective-permute-done((bf16[2,96,1024]{2,1,0:T(8,128)(2,1)S(1)}, bf16[2,96,1024]{2,1,0:T(8,128)(2,1)S(1)}, u32[]{:S(2)}, u32[]{:S(2)}) %collective-permute-start.5) | collective-permute-done | bytes 393248 | tf_op jit(solution)/shard_map/while/body/cond/branch_0_fun/ppermute | solution.py:24
  82.6 0.4 collective-permute-done.3
  83.1 0.1 maximum_maximum_fusion
  83.2 0.1 copy.26
  83.3 7.1 %body.3 = bf16[384,2048]{1,0:T(8,128)(2,1)S(1)} custom-call(s32[1]{0:T(128)} %bitcast.191.other, bf16[384,2048]{1,0:T(8,128)(2,1)S(1)} %get-tuple-element.402.rows, bf16[2,704,2048]{2,1,0:T(8,128)(2,1)} %get-tuple-element.466.gate_up_near, bf16[2,704,2048]{2,1,0:T(8,128)(2,1)} %get-tuple-element.403.gate_up_far, bf16[704,2048]{1,0:T(8,128)(2,1)} %bitcast.225, ...), custom_call_target="tpu_custom_call" | custom-call | flops 3321888768 | bytes 8650752 | tf_op jit(solution)/shard_map/while/body/pallas_call | solution.py:464
  90.5 30.7 %conditional.5 = (bf16[24,2048]{1,0:T(8,128)(2,1)S(1)}, bf16[24,2048]{1,0:T(8,128)(2,1)}) conditional(s32[]{:T(128)} %get-tuple-element.468, (s32[]{:T(128)}, bf16[384,2048]{1,0:T(8,128)(2,1)S(1)}) %tuple.97, (s32[]{:T(128)}, bf16[384,2048]{1,0:T(8,128)(2,1)S(1)}) %tuple.97, (s32[]{:T(128)}, bf16[384,2048]{1,0:T(8,128)(2,1)S(1)}) %tuple.97), branch_computations={%region_4.4_spmd, %region_5.5_spmd, %region_6.6_spmd} | conditional | flops 2359300 | bytes 13566253 | solution.py:484
  90.5 1.7 %collective-permute-start.24 = (bf16[2,96,1024]{2,1,0:T(8,128)(2,1)S(1)}, bf16[2,96,1024]{2,1,0:T(8,128)(2,1)}, u32[]{:S(2)}, u32[]{:S(2)}) collective-permute-start(bf16[2,96,1024]{2,1,0:T(8,128)(2,1)S(1)} %slice_bitcast_fusion.8), channel_id=1, source_target_pairs={{0,1},{1,0},{2,3},{3,2},{4,5},{5,4},{6,7},{7,6},{8,9},{9,8},{10,11... | collective-permute-start | bytes 1179656 | tf_op jit(solution)/shard_map/while/body/cond/branch_0_fun/ppermute | solution.py:24
  92.3 0.7 collective-permute-start.26
  93.0 6.2 %collective-permute-done.24 = bf16[2,96,1024]{2,1,0:T(8,128)(2,1)} collective-permute-done((bf16[2,96,1024]{2,1,0:T(8,128)(2,1)S(1)}, bf16[2,96,1024]{2,1,0:T(8,128)(2,1)}, u32[]{:S(2)}, u32[]{:S(2)}) %collective-permute-start.24) | collective-permute-done | bytes 393248 | tf_op jit(solution)/shard_map/while/body/cond/branch_0_fun/ppermute | solution.py:24
  99.2 1.1 fusion.6
  100.3 0.8 collective-permute-start.25
  101.2 0.5 collective-permute-done.26
  101.7 1.1 collective-permute-start.27
  102.8 3.2 %collective-permute-done.25 = bf16[96,1024]{1,0:T(8,128)(2,1)S(1)} collective-permute-done((bf16[96,1024]{1,0:T(8,128)(2,1)S(1)}, bf16[96,1024]{1,0:T(8,128)(2,1)S(1)}, u32[]{:S(2)}, u32[]{:S(2)}) %collective-permute-start.25) | collective-permute-done | bytes 196640 | tf_op jit(solution)/shard_map/while/body/cond/branch_0_fun/ppermute | solution.py:24
  106.1 1.4 %collective-permute-done.27 = bf16[96,1024]{1,0:T(8,128)(2,1)S(1)} collective-permute-done((bf16[96,1024]{1,0:T(8,128)(2,1)S(1)}, bf16[96,1024]{1,0:T(8,128)(2,1)S(1)}, u32[]{:S(2)}, u32[]{:S(2)}) %collective-permute-start.27) | collective-permute-done | bytes 196640 | tf_op jit(solution)/shard_map/while/body/cond/branch_0_fun/ppermute | solution.py:24
  107.5 1.1 collective-permute-start.28
  108.6 5.7 %collective-permute-done.28 = bf16[48,2048]{1,0:T(8,128)(2,1)S(1)} collective-permute-done((bf16[48,2048]{1,0:T(8,128)(2,1)S(1)}, bf16[48,2048]{1,0:T(8,128)(2,1)S(1)}, u32[]{:S(2)}, u32[]{:S(2)}) %collective-permute-start.28) | collective-permute-done | bytes 196640 | tf_op jit(solution)/shard_map/while/body/cond/branch_0_fun/ppermute | solution.py:24
  114.4 2.1 %collective-permute-start.29 = (bf16[24,2048]{1,0:T(8,128)(2,1)S(1)}, bf16[24,2048]{1,0:T(8,128)(2,1)}, u32[]{:S(2)}, u32[]{:S(2)}) collective-permute-start(bf16[24,2048]{1,0:T(8,128)(2,1)S(1)} %get-tuple-element.284), channel_id=1, source_target_pairs={{0,16},{2,18},{4,20},{6,22},{8,24},{10,26},{12,28},{14,30},{16,0},... | collective-permute-start | bytes 294920 | tf_op jit(solution)/shard_map/while/body/cond/branch_0_fun/ppermute | solution.py:24
  116.5 4.6 %collective-permute-done.29 = bf16[24,2048]{1,0:T(8,128)(2,1)} collective-permute-done((bf16[24,2048]{1,0:T(8,128)(2,1)S(1)}, bf16[24,2048]{1,0:T(8,128)(2,1)}, u32[]{:S(2)}, u32[]{:S(2)}) %collective-permute-start.29) | collective-permute-done | bytes 98336 | tf_op jit(solution)/shard_map/while/body/cond/branch_0_fun/ppermute | solution.py:24
  121.1 1.6 %select_select_fusion.3 = (bf16[24,2048]{1,0:T(8,128)(2,1)S(1)}, bf16[24,2048]{1,0:T(8,128)(2,1)}) fusion(bf16[24,2048]{1,0:T(8,128)(2,1)S(1)} %get-tuple-element.442, bf16[24,2048]{1,0:T(8,128)(2,1)} %get-tuple-element.405, bf16[24,2048]{1,0:T(8,128)(2,1)S(1)} %get-tuple-element.406, pred[]{:T(512)S(6)} %and.65, pred[]{:T(512)S(6)} %eq.47, ...), kind=kLoop, calls=%fused_computation.90.clone.1 | loop fusion | flops 344064 | bytes 589829 | tf_op jit(solution)/shard_map/while/body/jit(_where)/select_n | solution.py:490
  122.7 0.3 convolution_multiply_fusion
  123.1 2.0 %fusion.26 = bf16[1,128,2048]{2,1,0:T(8,128)(2,1)} fusion(f32[128,2048]{1,0:T(8,128)S(1)} %convolution_multiply_fusion, bf16[24,2048]{1,0:T(8,128)(2,1)} %get-tuple-element.230, f32[128]{0:T(128)S(1)} %get-tuple-element.232, bf16[128,48]{1,0:T(8,128)(2,1)S(1)} %get-tuple-element.221.refs_3_), kind=kOutput, calls=%fused_computation.99 | convolution fusion | flops 13369344 | bytes 1683968 | tf_op jit(solution)/shard_map/dot_general | solution.py:497
  (50 shorter events, 0.6 us)
Async XLA Ops:
  1.7 22.0 %collective-permute-start.43 = (bf16[2,128,1024]{2,1,0:T(8,128)(2,1)S(1)}, bf16[2,128,1024]{2,1,0:T(8,128)(2,1)S(1)}, u32[]{:S(2)}, u32[]{:S(2)}) collective-permute-start(bf16[2,128,1024]{2,1,0:T(8,128)(2,1)S(1)} %pad_maximum_fusion.14), channel_id=1, source_target_pairs={{0,1},{2,3},{4,5},{6,7},{8,9},{10,11},{12,13},{14,15},{16,17},{18,... | collective-permute-start | bytes 1572872 | tf_op jit(solution)/shard_map/ppermute | solution.py:351
  6.6 8.0 %collective-permute-start.45 = (bf16[64,2048]{1,0:T(8,128)(2,1)}, bf16[64,2048]{1,0:T(8,128)(2,1)S(1)}, u32[]{:S(2)}, u32[]{:S(2)}) collective-permute-start(bf16[64,2048]{1,0:T(8,128)(2,1)} %refs_4_.1), channel_id=1, source_target_pairs={{0,4},{2,6},{4,0},{6,2},{8,12},{10,14},{12,8},{14,10},{16,20},{18,... | collective-permute-start | bytes 786440 | tf_op jit(solution)/shard_map/ppermute | solution.py:24
  8.2 13.2 %collective-permute-start.44 = (bf16[64,2048]{1,0:T(8,128)(2,1)}, bf16[64,2048]{1,0:T(8,128)(2,1)S(1)}, u32[]{:S(2)}, u32[]{:S(2)}) collective-permute-start(bf16[64,2048]{1,0:T(8,128)(2,1)} %refs_4_.1), channel_id=1, source_target_pairs={{0,8},{2,10},{4,12},{6,14},{8,0},{10,2},{12,4},{14,6},{16,24},{18,... | collective-permute-start | bytes 786440 | tf_op jit(solution)/shard_map/ppermute | solution.py:24
  9.8 14.0 %collective-permute-start.42 = (bf16[64,2048]{1,0:T(8,128)(2,1)}, bf16[64,2048]{1,0:T(8,128)(2,1)S(1)}, u32[]{:S(2)}, u32[]{:S(2)}) collective-permute-start(bf16[64,2048]{1,0:T(8,128)(2,1)} %refs_4_.1), channel_id=1, source_target_pairs={{0,16},{2,18},{4,20},{6,22},{8,24},{10,26},{12,28},{14,30},{16,0},... | collective-permute-start | bytes 786440 | tf_op jit(solution)/shard_map/ppermute | solution.py:24
  21.4 6.4 %collective-permute-start.46 = (bf16[64,2048]{1,0:T(8,128)(2,1)S(1)}, bf16[64,2048]{1,0:T(8,128)(2,1)S(1)}, u32[]{:S(2)}, u32[]{:S(2)}) collective-permute-start(bf16[64,2048]{1,0:T(8,128)(2,1)S(1)} %collective-permute-done.44.refs_6_), channel_id=1, source_target_pairs={{0,4},{2,6},{4,0},{6,2},{8,12},{10,14},{12,8},{14,10},{16,20},{18,... | collective-permute-start | bytes 786440 | tf_op jit(solution)/shard_map/ppermute | solution.py:24
  23.8 13.7 %copy-start.6 = (s32[16]{0:T(128)S(1)}, s32[16]{0:T(128)}, u32[]{:S(2)}) copy-start(s32[16]{0:T(128)} %param.31) | copy-start | bytes 196
  23.8 16.1 %copy-start.7 = (s32[1,128,6]{1,0,2:T(1,128)S(1)}, s32[1,128,6]{1,0,2:T(1,128)}, u32[]{:S(2)}) copy-start(s32[1,128,6]{1,0,2:T(1,128)} %param.28) | copy-start | bytes 9220
  23.8 16.3 %copy-start.8 = (f32[1,128,6]{1,0,2:T(1,128)S(1)}, f32[1,128,6]{1,0,2:T(1,128)}, u32[]{:S(2)}) copy-start(f32[1,128,6]{1,0,2:T(1,128)} %param.29) | copy-start | bytes 9220
  23.8 16.4 %copy-start.9 = (s32[1,1,2]{2,1,0:T(1,128)S(1)}, s32[1,1,2]{2,1,0:T(1,128)}, u32[]{:S(2)}) copy-start(s32[1,1,2]{2,1,0:T(1,128)} %param.30) | copy-start | bytes 28
  23.8 18.3 %copy-start = (bf16[1,128,1024]{2,1,0:T(8,128)(2,1)S(1)}, bf16[1,128,1024]{2,1,0:T(8,128)(2,1)}, u32[]{:S(2)}) copy-start(bf16[1,128,1024]{2,1,0:T(8,128)(2,1)} %param.21) | copy-start | bytes 786436
  23.8 18.3 %copy-start.1 = (bf16[1,128,1024]{2,1,0:T(8,128)(2,1)S(1)}, bf16[1,128,1024]{2,1,0:T(8,128)(2,1)}, u32[]{:S(2)}) copy-start(bf16[1,128,1024]{2,1,0:T(8,128)(2,1)} %param.22) | copy-start | bytes 786436
  23.8 18.3 %copy-start.4 = (bf16[1,128,1024]{2,1,0:T(8,128)(2,1)S(1)}, bf16[1,128,1024]{2,1,0:T(8,128)(2,1)}, u32[]{:S(2)}) copy-start(bf16[1,128,1024]{2,1,0:T(8,128)(2,1)} %param.20) | copy-start | bytes 786436
  26.0 19.9 %collective-permute-start.50 = (bf16[4,64,2048]{2,1,0:T(8,128)(2,1)}, bf16[4,64,2048]{2,1,0:T(8,128)(2,1)}, u32[]{:S(2)}, u32[]{:S(2)}) collective-permute-start(bf16[4,64,2048]{2,1,0:T(8,128)(2,1)} %pad_maximum_fusion.12), channel_id=1, source_target_pairs={{0,2},{2,0},{4,6},{6,4},{8,10},{10,8},{12,14},{14,12},{16,18},{18,... | collective-permute-start | bytes 3145736 | tf_op jit(solution)/shard_map/ppermute | solution.py:24
  27.7 6.9 %collective-permute-start.47 = (bf16[64,2048]{1,0:T(8,128)(2,1)S(1)}, bf16[64,2048]{1,0:T(8,128)(2,1)S(1)}, u32[]{:S(2)}, u32[]{:S(2)}) collective-permute-start(bf16[64,2048]{1,0:T(8,128)(2,1)S(1)} %collective-permute-done.42.refs_8_), channel_id=1, source_target_pairs={{0,4},{2,6},{4,0},{6,2},{8,12},{10,14},{12,8},{14,10},{16,20},{18,... | collective-permute-start | bytes 786440 | tf_op jit(solution)/shard_map/ppermute | solution.py:24
  28.3 6.7 %collective-permute-start.48 = (bf16[64,2048]{1,0:T(8,128)(2,1)S(1)}, bf16[64,2048]{1,0:T(8,128)(2,1)S(1)}, u32[]{:S(2)}, u32[]{:S(2)}) collective-permute-start(bf16[64,2048]{1,0:T(8,128)(2,1)S(1)} %collective-permute-done.42.refs_8_), channel_id=1, source_target_pairs={{0,8},{2,10},{4,12},{6,14},{8,0},{10,2},{12,4},{14,6},{16,24},{18,... | collective-permute-start | bytes 786440 | tf_op jit(solution)/shard_map/ppermute | solution.py:24
  35.9 11.3 %collective-permute-start.51 = (bf16[3,64,2048]{2,1,0:T(8,128)(2,1)}, bf16[3,64,2048]{2,1,0:T(8,128)(2,1)}, u32[]{:S(2)}, u32[]{:S(2)}) collective-permute-start(bf16[3,64,2048]{2,1,0:T(8,128)(2,1)} %pad_maximum_fusion.13), channel_id=1, source_target_pairs={{0,2},{2,0},{4,6},{6,4},{8,10},{10,8},{12,14},{14,12},{16,18},{18,... | collective-permute-start | bytes 2359304 | tf_op jit(solution)/shard_map/ppermute | solution.py:24
  35.9 9.6 %collective-permute-start.49 = (bf16[64,2048]{1,0:T(8,128)(2,1)S(1)}, bf16[64,2048]{1,0:T(8,128)(2,1)S(1)}, u32[]{:S(2)}, u32[]{:S(2)}) collective-permute-start(bf16[64,2048]{1,0:T(8,128)(2,1)S(1)} %collective-permute-done.48.refs_10_), channel_id=1, source_target_pairs={{0,4},{2,6},{4,0},{6,2},{8,12},{10,14},{12,8},{14,10},{16,20},{18,... | collective-permute-start | bytes 786440 | tf_op jit(solution)/shard_map/ppermute | solution.py:24
  45.5 2.8 %copy-start.2 = (bf16[64,2048]{1,0:T(8,128)(2,1)S(1)}, bf16[64,2048]{1,0:T(8,128)(2,1)}, u32[]{:S(2)}) copy-start(bf16[64,2048]{1,0:T(8,128)(2,1)} %refs_4_.1) | copy-start | bytes 786436
  45.6 2.8 %copy-start.3 = (bf16[1,128,2048]{2,1,0:T(8,128)(2,1)S(1)}, bf16[1,128,2048]{2,1,0:T(8,128)(2,1)}, u32[]{:S(2)}) copy-start(bf16[1,128,2048]{2,1,0:T(8,128)(2,1)} %param.23) | copy-start | bytes 1572868
  45.6 2.8 %copy-start.5 = (f32[2048]{0:T(1024)S(1)}, f32[2048]{0:T(1024)}, u32[]{:S(2)}) copy-start(f32[2048]{0:T(1024)} %param.25) | copy-start | bytes 24580
  45.6 2.8 %collective-permute-start.52 = (bf16[1,64,2048]{2,1,0:T(8,128)(2,1)S(1)}, bf16[1,64,2048]{2,1,0:T(8,128)(2,1)S(1)}, u32[]{:S(2)}, u32[]{:S(2)}) collective-permute-start(bf16[1,64,2048]{2,1,0:T(8,128)(2,1)S(1)} %bitcast.203), channel_id=1, source_target_pairs={{0,2},{2,0},{4,6},{6,4},{8,10},{10,8},{12,14},{14,12},{16,18},{18,... | collective-permute-start | bytes 786440 | tf_op jit(solution)/shard_map/ppermute | solution.py:24
  52.7 30.7 %collective-permute-start.6 = (bf16[2,704,2048]{2,1,0:T(8,128)(2,1)}, bf16[2,704,2048]{2,1,0:T(8,128)(2,1)}, u32[]{:S(2)}, u32[]{:S(2)}) collective-permute-start(bf16[2,704,2048]{2,1,0:T(8,128)(2,1)} %get-tuple-element.168), channel_id=1, source_target_pairs={{0,2},{2,0},{4,6},{6,4},{8,10},{10,8},{12,14},{14,12},{16,18},{18,... | collective-permute-start | bytes 17301512 | tf_op jit(solution)/shard_map/while/body/cond/branch_0_fun/ppermute | solution.py:24
  53.0 30.3 %collective-permute-start.7 = (bf16[704,2048]{1,0:T(8,128)(2,1)}, bf16[704,2048]{1,0:T(8,128)(2,1)}, u32[]{:S(2)}, u32[]{:S(2)}) collective-permute-start(bf16[704,2048]{1,0:T(8,128)(2,1)} %bitcast.226), channel_id=1, source_target_pairs={{0,2},{2,0},{4,6},{6,4},{8,10},{10,8},{12,14},{14,12},{16,18},{18,... | collective-permute-start | bytes 8650760 | tf_op jit(solution)/shard_map/while/body/cond/branch_0_fun/ppermute | solution.py:24
  53.2 8.0 %collective-permute-start = (bf16[24,2048]{1,0:T(8,128)(2,1)S(1)}, bf16[24,2048]{1,0:T(8,128)(2,1)S(1)}, u32[]{:S(2)}, u32[]{:S(2)}) collective-permute-start(bf16[24,2048]{1,0:T(8,128)(2,1)S(1)} %get-tuple-element.167), channel_id=1, source_target_pairs={{0,16},{2,18},{4,20},{6,22},{8,24},{10,26},{12,28},{14,30},{16,0},... | collective-permute-start | bytes 294920 | tf_op jit(solution)/shard_map/while/body/cond/branch_0_fun/ppermute | solution.py:24
  61.2 6.7 %collective-permute-start.1 = (bf16[48,2048]{1,0:T(8,128)(2,1)S(1)}, bf16[48,2048]{1,0:T(8,128)(2,1)S(1)}, u32[]{:S(2)}, u32[]{:S(2)}) collective-permute-start(bf16[48,2048]{1,0:T(8,128)(2,1)S(1)} %pad_maximum_fusion.2), channel_id=1, source_target_pairs={{0,8},{2,10},{4,12},{6,14},{8,0},{10,2},{12,4},{14,6},{16,24},{18,... | collective-permute-start | bytes 589832 | tf_op jit(solution)/shard_map/while/body/cond/branch_0_fun/ppermute | solution.py:24
  68.0 5.8 %collective-permute-start.4 = (bf16[96,1024]{1,0:T(8,128)(2,1)S(1)}, bf16[96,1024]{1,0:T(8,128)(2,1)S(1)}, u32[]{:S(2)}, u32[]{:S(2)}) collective-permute-start(bf16[96,1024]{1,0:T(8,128)(2,1)S(1)} %get-tuple-element.264), channel_id=1, source_target_pairs={{0,1},{1,0},{2,3},{3,2},{4,5},{5,4},{6,7},{7,6},{8,9},{9,8},{10,11... | collective-permute-start | bytes 589832 | tf_op jit(solution)/shard_map/while/body/cond/branch_0_fun/ppermute | solution.py:24
  68.1 6.4 %collective-permute-start.2 = (bf16[96,1024]{1,0:T(8,128)(2,1)S(1)}, bf16[96,1024]{1,0:T(8,128)(2,1)S(1)}, u32[]{:S(2)}, u32[]{:S(2)}) collective-permute-start(bf16[96,1024]{1,0:T(8,128)(2,1)S(1)} %get-tuple-element.265), channel_id=1, source_target_pairs={{0,4},{2,6},{4,0},{6,2},{8,12},{10,14},{12,8},{14,10},{16,20},{18,... | collective-permute-start | bytes 589832 | tf_op jit(solution)/shard_map/while/body/cond/branch_0_fun/ppermute | solution.py:24
  73.8 8.8 %collective-permute-start.5 = (bf16[2,96,1024]{2,1,0:T(8,128)(2,1)S(1)}, bf16[2,96,1024]{2,1,0:T(8,128)(2,1)S(1)}, u32[]{:S(2)}, u32[]{:S(2)}) collective-permute-start(bf16[2,96,1024]{2,1,0:T(8,128)(2,1)S(1)} %get-tuple-element.267), channel_id=1, source_target_pairs={{0,4},{2,6},{4,0},{6,2},{8,12},{10,14},{12,8},{14,10},{16,20},{18,... | collective-permute-start | bytes 1179656 | tf_op jit(solution)/shard_map/while/body/cond/branch_0_fun/ppermute | solution.py:24
  74.5 8.5 %collective-permute-start.3 = (bf16[2,96,1024]{2,1,0:T(8,128)(2,1)S(1)}, bf16[2,96,1024]{2,1,0:T(8,128)(2,1)S(1)}, u32[]{:S(2)}, u32[]{:S(2)}) collective-permute-start(bf16[2,96,1024]{2,1,0:T(8,128)(2,1)S(1)} %get-tuple-element.261), channel_id=1, source_target_pairs={{0,1},{1,0},{2,3},{3,2},{4,5},{5,4},{6,7},{7,6},{8,9},{9,8},{10,11... | collective-permute-start | bytes 1179656 | tf_op jit(solution)/shard_map/while/body/cond/branch_0_fun/ppermute | solution.py:24
  90.5 8.6 %collective-permute-start.24 = (bf16[2,96,1024]{2,1,0:T(8,128)(2,1)S(1)}, bf16[2,96,1024]{2,1,0:T(8,128)(2,1)}, u32[]{:S(2)}, u32[]{:S(2)}) collective-permute-start(bf16[2,96,1024]{2,1,0:T(8,128)(2,1)S(1)} %slice_bitcast_fusion.8), channel_id=1, source_target_pairs={{0,1},{1,0},{2,3},{3,2},{4,5},{5,4},{6,7},{7,6},{8,9},{9,8},{10,11... | collective-permute-start | bytes 1179656 | tf_op jit(solution)/shard_map/while/body/cond/branch_0_fun/ppermute | solution.py:24
  92.3 9.4 %collective-permute-start.26 = (bf16[2,96,1024]{2,1,0:T(8,128)(2,1)S(1)}, bf16[2,96,1024]{2,1,0:T(8,128)(2,1)S(1)}, u32[]{:S(2)}, u32[]{:S(2)}) collective-permute-start(bf16[2,96,1024]{2,1,0:T(8,128)(2,1)S(1)} %slice_bitcast_fusion.6), channel_id=1, source_target_pairs={{0,4},{2,6},{4,0},{6,2},{8,12},{10,14},{12,8},{14,10},{16,20},{18,... | collective-permute-start | bytes 1179656 | tf_op jit(solution)/shard_map/while/body/cond/branch_0_fun/ppermute | solution.py:24
  100.3 5.7 %collective-permute-start.25 = (bf16[96,1024]{1,0:T(8,128)(2,1)S(1)}, bf16[96,1024]{1,0:T(8,128)(2,1)S(1)}, u32[]{:S(2)}, u32[]{:S(2)}) collective-permute-start(bf16[96,1024]{1,0:T(8,128)(2,1)S(1)} %slice_bitcast_fusion.12), channel_id=1, source_target_pairs={{0,4},{2,6},{4,0},{6,2},{8,12},{10,14},{12,8},{14,10},{16,20},{18,... | collective-permute-start | bytes 589832 | tf_op jit(solution)/shard_map/while/body/cond/branch_0_fun/ppermute | solution.py:24
  101.7 5.7 %collective-permute-start.27 = (bf16[96,1024]{1,0:T(8,128)(2,1)S(1)}, bf16[96,1024]{1,0:T(8,128)(2,1)S(1)}, u32[]{:S(2)}, u32[]{:S(2)}) collective-permute-start(bf16[96,1024]{1,0:T(8,128)(2,1)S(1)} %slice_bitcast_fusion.10), channel_id=1, source_target_pairs={{0,1},{1,0},{2,3},{3,2},{4,5},{5,4},{6,7},{7,6},{8,9},{9,8},{10,11... | collective-permute-start | bytes 589832 | tf_op jit(solution)/shard_map/while/body/cond/branch_0_fun/ppermute | solution.py:24
  107.5 6.8 %collective-permute-start.28 = (bf16[48,2048]{1,0:T(8,128)(2,1)S(1)}, bf16[48,2048]{1,0:T(8,128)(2,1)S(1)}, u32[]{:S(2)}, u32[]{:S(2)}) collective-permute-start(bf16[48,2048]{1,0:T(8,128)(2,1)S(1)} %pad_maximum_fusion.9), channel_id=1, source_target_pairs={{0,8},{2,10},{4,12},{6,14},{8,0},{10,2},{12,4},{14,6},{16,24},{18,... | collective-permute-start | bytes 589832 | tf_op jit(solution)/shard_map/while/body/cond/branch_0_fun/ppermute | solution.py:24
  114.4 6.7 %collective-permute-start.29 = (bf16[24,2048]{1,0:T(8,128)(2,1)S(1)}, bf16[24,2048]{1,0:T(8,128)(2,1)}, u32[]{:S(2)}, u32[]{:S(2)}) collective-permute-start(bf16[24,2048]{1,0:T(8,128)(2,1)S(1)} %get-tuple-element.284), channel_id=1, source_target_pairs={{0,16},{2,18},{4,20},{6,22},{8,24},{10,26},{12,28},{14,30},{16,0},... | collective-permute-start | bytes 294920 | tf_op jit(solution)/shard_map/while/body/cond/branch_0_fun/ppermute | solution.py:24

commit v2 on v1

--- a/solution.py
+++ b/solution.py
@@ -1,3 +1,5 @@
+import functools
+
 import jax
 import jax.numpy as jnp
 from jax import lax
@@ -204,11 +206,12 @@
     place[...] = ((routed > 0.0) & (rank == slot) & (rank < limit)).astype(jnp.bfloat16)
 
 
-def project_kernel(*refs):
+def project_kernel(far_place, *refs):
     attended, residual, gain, place = refs[:4]
     near = refs[4 : 4 + HEADS]
-    far = refs[4 + HEADS : 4 + 2 * HEADS]
-    attn_proj, chosen, combined = refs[4 + 2 * HEADS :]
+    groups = refs[4 + HEADS : -3]
+    far = [groups[group].at[k] for group, k in far_place]
+    attn_proj, chosen, combined = refs[-3:]
     token_count, width = residual.shape
     tile = 512
     squares = jnp.zeros((token_count, 1), jnp.float32)
@@ -289,20 +292,29 @@
         ).astype(jnp.bfloat16)
 
 
-def gather_rows(unit, bits, dp_size):
-    for bit in bits[:-1]:
-        unit = jnp.concatenate([unit, hop(unit, "dp", dp_size, bit)], axis=0)
+def gather_rows(kept, sent, first, bits, dp_size):
+    second, last = bits
+    unit = jnp.concatenate(
+        [
+            kept,
+            hop(sent, "dp", dp_size, first),
+            hop(kept, "dp", dp_size, second),
+            hop(sent, "dp", dp_size, first | second),
+        ],
+        axis=0,
+    )
     half = unit.shape[1] // 2
     left, right = unit[:, :half], unit[:, half:]
-    left = jnp.stack([left, hop(left, "dp", dp_size, bits[-1])])
+    left = jnp.stack([left, hop(left, "dp", dp_size, last)])
     right = jnp.stack([right, hop(right, "ctx", 2, 1)])
     left = jnp.stack([left, hop(left, "ctx", 2, 1)])
-    right = jnp.stack([right, hop(right, "dp", dp_size, bits[-1])], axis=1)
+    right = jnp.stack([right, hop(right, "dp", dp_size, last)], axis=1)
     rows = jnp.concatenate([left, right], axis=-1)
     return rows.reshape(-1, rows.shape[-1])
 
 
-def scatter_rows(rows, bits, dp_size, offset):
+def scatter_rows(rows, first, bits, dp_size, offset, other_offset):
+    second, last = bits
     half = rows.shape[1] // 2
     rows = rows.reshape(2, 2, -1, rows.shape[1])
     left, right = rows[..., :half], rows[..., half:]
@@ -310,16 +322,20 @@
     def add(kept, came):
         return (kept.astype(jnp.float32) + came.astype(jnp.float32)).astype(jnp.bfloat16)
 
-    near = (offset & bits[-1]) == 0
+    near = (offset & last) == 0
     left = add(left[0], hop(left[1], "ctx", 2, 1))
-    right = jnp.where(near, right[:, 0], hop(right[:, 1], "dp", dp_size, bits[-1]))
-    left = jnp.where(near, left[0], hop(left[1], "dp", dp_size, bits[-1]))
+    right = jnp.where(near, right[:, 0], hop(right[:, 1], "dp", dp_size, last))
+    left = jnp.where(near, left[0], hop(left[1], "dp", dp_size, last))
     right = add(right[0], hop(right[1], "ctx", 2, 1))
     unit = jnp.concatenate([left, right], axis=-1)
-    for bit in reversed(bits[:-1]):
-        kept, sent = jnp.split(unit, 2, axis=0)
-        unit = jnp.where((offset & bit) == 0, kept, hop(sent, "dp", dp_size, bit))
-    return unit
+    here, across, beside, beyond = jnp.split(unit, 4, axis=0)
+    across = hop(across, "dp", dp_size, first)
+    beside = hop(beside, "dp", dp_size, second)
+    beyond = hop(beyond, "dp", dp_size, first | second)
+    return (
+        jnp.where((offset & second) == 0, here, beside),
+        jnp.where((other_offset & second) == 0, across, beyond),
+    )
 
 
 def vmem(count):
@@ -348,34 +364,22 @@
     ctx = lax.axis_index("ctx")
     bits = [1 << k for k in reversed(range(1, dp_size.bit_length() - 1))]
 
+    info = jnp.stack([ctx, me >> 1, core, capacity[0, 0, 0], capacity[0, 0, 1]]).astype(jnp.int32)
     before = lax.ppermute(jnp.stack([key_vecs[0], value_vecs[0]]), "ctx", [(0, 1)])
     z_far, z_near, x_bit = bits
     z_both = z_far | z_near
     near = {0: w_out}
     for bit in (z_near, x_bit, z_far):
         near[bit] = hop(w_out, "dp", dp_size, bit)
-    near[z_near], near[x_bit] = lax.optimization_barrier((near[z_near], near[x_bit]))
+    near[z_near], near[x_bit], info, ids, gates = lax.optimization_barrier(
+        (near[z_near], near[x_bit], info, expert_ids[0], route_gates[0])
+    )
     near[z_near | x_bit] = hop(near[z_near], "dp", dp_size, x_bit)
-    near[z_far], before = lax.optimization_barrier((near[z_far], before))
     near[z_both] = hop(near[z_far], "dp", dp_size, z_near)
-    next_sent, near[z_near | x_bit] = lax.optimization_barrier(
-        (near[z_far], near[z_near | x_bit])
+    next_sent, near[z_near | x_bit], before = lax.optimization_barrier(
+        (near[z_far], near[z_near | x_bit], before)
     )
     near[z_far | x_bit] = hop(next_sent, "dp", dp_size, x_bit)
-    near[z_both | x_bit] = hop(near[z_both], "dp", dp_size, x_bit)
-    far = {}
-    for group in (
-        (0, z_near, x_bit, z_far),
-        (z_near | x_bit, z_far | x_bit, z_both),
-        (z_both | x_bit,),
-    ):
-        came = hop(jnp.stack([near[j] for j in group]), "dp", dp_size, 1)
-        for k, j in enumerate(group):
-            far[j] = came[k]
-    shares = [near[2 * j] for j in range(HEADS)] + [far[2 * j] for j in range(HEADS)]
-    gate_up_near = jnp.swapaxes(w_gate_up[0], 1, 2)
-
-    info = jnp.stack([ctx, me >> 1, core, capacity[0, 0, 0], capacity[0, 0, 1]]).astype(jnp.int32)
     slots = PASS_SPECIALISTS * CAP
     attended, place, gate_values = pl.pallas_call(
         attend_kernel,
@@ -387,7 +391,7 @@
         in_specs=[pl.BlockSpec(memory_space=pltpu.SMEM)] + vmem(6),
         out_specs=tuple(vmem(3)),
         cost_estimate=pl.CostEstimate(
-            flops=4 * HEADS * HD * 2 * token_count * token_count,
+            flops=64 * HEADS * HD * 2 * token_count * token_count,
             bytes_accessed=6 * 2 * token_count * HEADS * HD,
             transcendentals=2 * HEADS * token_count * token_count,
         ),
@@ -398,16 +402,42 @@
         key_vecs[0],
         value_vecs[0],
         before,
-        expert_ids[0],
-        route_gates[0],
-    )
+        ids,
+        gates,
+    )
+    near[z_both], near[z_far | x_bit], attended = lax.optimization_barrier(
+        (near[z_both], near[z_far | x_bit], attended)
+    )
+    near[z_both | x_bit] = hop(near[z_both], "dp", dp_size, x_bit)
+    far = [
+        hop(jnp.stack([near[j] for j in group]), "dp", dp_size, 1)
+        for group in (
+            (0, z_near, x_bit, z_far),
+            (z_near | x_bit, z_far | x_bit, z_both),
+            (z_both | x_bit,),
+        )
+    ]
+    far_place = {
+        0: (0, 0),
+        z_near: (0, 1),
+        x_bit: (0, 2),
+        z_far: (0, 3),
+        z_near | x_bit: (1, 0),
+        z_far | x_bit: (1, 1),
+        z_both: (1, 2),
+        z_both | x_bit: (2, 0),
+    }
+    far_place = [far_place[2 * j] for j in range(HEADS)]
+    shares = [near[2 * j] for j in range(HEADS)] + far
+    gate_up_near = jnp.swapaxes(w_gate_up[0], 1, 2)
+
     attn_proj, chosen = pl.pallas_call(
-        project_kernel,
+        functools.partial(project_kernel, far_place),
         out_shape=(
             jax.ShapeDtypeStruct((token_count, width), jnp.bfloat16),
             jax.ShapeDtypeStruct((slots, width), jnp.bfloat16),
         ),
-        in_specs=vmem(4 + 2 * HEADS),
+        in_specs=vmem(4 + len(shares)),
         out_specs=tuple(vmem(2)),
         scratch_shapes=[pltpu.VMEM((token_count, width), jnp.float32)],
         cost_estimate=pl.CostEstimate(
@@ -437,17 +467,16 @@
         def run(kept, sent):
             gate_up_far = hop(gate_up_near, "dp", dp_size, 1)
             down_far = hop(w_down[0], "dp", dp_size, 1)
-            unit = jnp.concatenate([kept, hop(sent, "dp", dp_size, bit)], axis=0)
-            return gather_rows(unit, rest, dp_size), gate_up_far, down_far
+            rows = gather_rows(kept, sent, bit, rest, dp_size)
+            return rows, gate_up_far, down_far
 
         return run
 
     def give_back(bit):
         rest = [b for b in bits if b != bit]
 
-        def run(made, offset):
-            unit = scatter_rows(made, rest, dp_size, offset)
-            return unit[:CAP], hop(unit[CAP:], "dp", dp_size, bit)
+        def run(made, offset, other_offset):
+            return scatter_rows(made, bit, rest, dp_size, offset, other_offset)
 
         return run
 
@@ -456,6 +485,7 @@
         sent_expert = jnp.where(same, step, 1 - side)
         owner = jnp.where(local == 0, owners[0], owners[1])
         offset = me ^ owner
+        other_offset = me ^ jnp.where(sent_expert == 0, owners[0], owners[1])
         kept = jnp.where(local == 0, chosen[:CAP], chosen[CAP:])
         sent = jnp.where(sent_expert == 0, chosen[:CAP], chosen[CAP:])
         rows, gate_up_far, down_far = lax.switch(
@@ -479,9 +509,9 @@
                 bytes_accessed=6 * units * width,
                 transcendentals=row_count * units,
             ),
-            compiler_params=pltpu.CompilerParams(vmem_limit_bytes=52 * 2**20),
+            compiler_params=pltpu.CompilerParams(vmem_limit_bytes=30 * 2**20),
         )((offset & 1)[None], rows, gate_up_near, gate_up_far, w_down[0], down_far)
-        own, other = lax.switch(branch, [give_back(bit) for bit in bits], made, offset)
+        own, other = lax.switch(branch, [give_back(bit) for bit in bits], made, offset, other_offset)
         served = jnp.where((offset & bits[0]) == 0, own, other)
         first = jnp.where(same, served, jnp.where(local == 0, own, other))
         second = jnp.where(same, served, jnp.where(local == 0, other, own))

time: 127 us -> 124 us (0.976)
  waiting for transfers between devices: 65.6 us -> 57.5 us
  starting transfers between devices: 26.5 us -> 29.8 us
  local copies, waits for them, and re-layouts: 7.04 us -> 9.57 us
  other arithmetic: 7.36 us -> 5.69 us
  loops' own time: 1.51 us -> 2.96 us
  Pallas kernels: 12 us -> 13.4 us
    ppermute x24 -> x26, waiting for transfers between devices: 65.6 us -> 57.5 us  [hop(): return lax.ppermute(array, axis, [(i, i ^ bit) for i in range(size)])]
    unnamed x22 -> x28, local copies, waits for them, and re-layouts: 0.28 us -> 5.31 us
    ppermute x24 -> x26, starting transfers between devices: 21.6 us -> 26.4 us  [hop(): return lax.ppermute(array, axis, [(i, i ^ bit) for i in range(size)])]
    squeeze x4 -> x2, local copies, waits for them, and re-layouts: 2.5 us -> 0.04 us  [the longest x1 0.03 us: scatter_rows(): right = jnp.where(near, right[:, 0], hop(right[:, 1], 'dp', dp_size, last))]
    select_n x1, other arithmetic: 1.58 us -> 0.06 us  [one_pass(): jnp.where(same & (step != 1), produced[1], second)]
    ppermute x1, starting transfers between devices: 4.9 us -> 3.46 us  [body_move_rows(): lax.ppermute(jnp.stack([key_vecs[0], value_vecs[0]]), 'ctx', [(0, 1)])]
    another operation x1, loops' own time: 1.32 us -> 2.76 us  [body_move_rows(): lax.fori_loop(0, jnp.where(same, 2, 1), one_pass, (nothing, nothing))]
    pallas_call x1, Pallas kernels: 1.66 us -> 3.07 us  [body_move_rows(): pl.pallas_call(functools.partial(project_kernel, far_place), out_shape=(j...]
  transfers between devices with their start and end apart: 25 -> 27, of which waited for: 17 -> 14; matrix products, arithmetic and copies ran while one was open for 8% -> 9% of each run, Pallas kernels for 3% -> 3%
where the time goes in v2:
time: 124 us; the launch traced here: 123 us
  waiting for transfers between devices  57.5 us (46%)
  starting transfers between devices  29.8 us (24%)
  Pallas kernels  13.4 us (11%)
  local copies, waits for them, and re-layouts  9.57 us (8%)
  other arithmetic  5.69 us (5%)
  loops' own time  2.96 us (2%)
  between operations  2.85 us (2%)
  matrix products  1.42 us (1%)
    ppermute x26, waiting for transfers between devices, hop(): return lax.ppermute(array, axis, [(i, i ^ bit) for i in range(size)])  57.5 us
    ppermute x26, starting transfers between devices, hop(): return lax.ppermute(array, axis, [(i, i ^ bit) for i in range(size)])  26.4 us
    pallas_call x1, Pallas kernels, one_pass(): pl.pallas_call(expert_kernel, out_shape=jax.ShapeDtypeStruct((row_count,...  7.12 us
    unnamed x28, local copies, waits for them, and re-layouts  5.31 us
    ppermute x1, starting transfers between devices, body_move_rows(): lax.ppermute(jnp.stack([key_vecs[0], value_vecs[0]]), 'ctx', [(0, 1)])  3.46 us
    pallas_call x1, Pallas kernels, body_move_rows(): pl.pallas_call(attend_kernel, out_shape=(jax.ShapeDtypeStruct((HEADS, tok...  3.22 us
    pallas_call x1, Pallas kernels, body_move_rows(): pl.pallas_call(functools.partial(project_kernel, far_place), out_shape=(j...  3.07 us
    another operation x2, other arithmetic, body_move_rows(): jnp.stack([near[j] for j in group])  3.06 us
  transfers between devices with their start and end apart: 27, of which 14 were waited for; matrix products, arithmetic and copies ran while one was open for 9% of the time, Pallas kernels for 3%

profile of v2, /device:TPU:0, one launch (start us, length us, event | category | flops | bytes accessed | tf_op | source)
XLA Modules:
  0.0 123.3 jit_solution(3229233557045503142)
XLA Ops:
  0.6 3.0 %collective-permute-start.51 = (bf16[64,2048]{1,0:T(8,128)(2,1)}, bf16[64,2048]{1,0:T(8,128)(2,1)S(1)}, u32[]{:S(2)}, u32[]{:S(2)}) collective-permute-start(bf16[64,2048]{1,0:T(8,128)(2,1)} %refs_4_.1), channel_id=1, source_target_pairs={{0,4},{2,6},{4,0},{6,2},{8,12},{10,14},{12,8},{14,10},{16,20},{18,... | collective-permute-start | bytes 786440 | tf_op jit(solution)/shard_map/ppermute | solution.py:26
  3.7 1.6 %collective-permute-start.50 = (bf16[64,2048]{1,0:T(8,128)(2,1)}, bf16[64,2048]{1,0:T(8,128)(2,1)S(1)}, u32[]{:S(2)}, u32[]{:S(2)}) collective-permute-start(bf16[64,2048]{1,0:T(8,128)(2,1)} %refs_4_.1), channel_id=1, source_target_pairs={{0,8},{2,10},{4,12},{6,14},{8,0},{10,2},{12,4},{14,6},{16,24},{18,... | collective-permute-start | bytes 786440 | tf_op jit(solution)/shard_map/ppermute | solution.py:26
  5.2 1.1 pad_maximum_fusion.11
  6.3 3.5 %collective-permute-start.53 = (bf16[2,128,1024]{2,1,0:T(8,128)(2,1)S(1)}, bf16[2,128,1024]{2,1,0:T(8,128)(2,1)S(1)}, u32[]{:S(2)}, u32[]{:S(2)}) collective-permute-start(bf16[2,128,1024]{2,1,0:T(8,128)(2,1)S(1)} %pad_maximum_fusion.11), channel_id=1, source_target_pairs={{0,1},{2,3},{4,5},{6,7},{8,9},{10,11},{12,13},{14,15},{16,17},{18,... | collective-permute-start | bytes 1572872 | tf_op jit(solution)/shard_map/ppermute | solution.py:368
  9.8 2.7 %collective-permute-start.48 = (bf16[64,2048]{1,0:T(8,128)(2,1)}, bf16[64,2048]{1,0:T(8,128)(2,1)S(1)}, u32[]{:S(2)}, u32[]{:S(2)}) collective-permute-start(bf16[64,2048]{1,0:T(8,128)(2,1)} %refs_4_.1), channel_id=1, source_target_pairs={{0,16},{2,18},{4,20},{6,22},{8,24},{10,26},{12,28},{14,30},{16,0},... | collective-permute-start | bytes 786440 | tf_op jit(solution)/shard_map/ppermute | solution.py:26
  12.4 1.4 %copy.34 = s32[1,128,6]{2,1,0:T(8,128)} copy(s32[1,128,6]{1,0,2:T(1,128)} %param.28) | data formatting | bytes 6144 | tf_op args[8]
  13.8 1.4 %copy.35 = f32[1,128,6]{2,1,0:T(8,128)} copy(f32[1,128,6]{1,0,2:T(1,128)} %param.29) | data formatting | bytes 6144 | tf_op args[9]
  15.3 1.3 %fusion.37 = (s32[1,1,1]{2,1,0:T(1,128)}, s32[1,1,1]{2,1,0:T(1,128)}) fusion(s32[1,1,2]{2,1,0:T(1,128)} %param.30), kind=kLoop, calls=%fused_computation.130 | loop fusion | bytes 16 | tf_op jit(solution)/shard_map/slice | solution.py:367
  16.6 1.2 stack.156.info
  17.8 0.6 collective-permute-start.52
  18.4 5.4 %collective-permute-done.48.refs_8_ = bf16[64,2048]{1,0:T(8,128)(2,1)S(1)} collective-permute-done((bf16[64,2048]{1,0:T(8,128)(2,1)}, bf16[64,2048]{1,0:T(8,128)(2,1)S(1)}, u32[]{:S(2)}, u32[]{:S(2)}) %collective-permute-start.48) | collective-permute-done | bytes 262176 | tf_op jit(solution)/shard_map/ppermute | solution.py:26
  23.8 1.0 collective-permute-done.52.refs_7_
  24.8 0.8 copy-done.9
  25.6 0.5 collective-permute-start.54
  26.1 2.1 %pad_maximum_fusion.9 = bf16[4,64,2048]{2,1,0:T(8,128)(2,1)} fusion(bf16[1,64,2048]{2,1,0:T(8,128)(2,1)S(1)} %bitcast.184, bf16[1,64,2048]{2,1,0:T(8,128)(2,1)S(1)} %bitcast.182, bf16[1,64,2048]{2,1,0:T(8,128)(2,1)S(1)} %bitcast.183, bf16[1,64,2048]{2,1,0:T(8,128)(2,1)} %bitcast.181), kind=kLoop, calls=%fused_computation.121 | loop fusion | flops 1572864 | bytes 2097152 | tf_op jit(solution)/shard_map/stack | solution.py:413
  28.3 3.2 %shard_map.131 = (bf16[8,128,128]{2,1,0:T(8,128)(2,1)S(1)}, bf16[128,48]{1,0:T(8,128)(2,1)S(1)}, f32[128,2]{1,0:T(8,128)S(1)}) custom-call(s32[5]{0:T(128)S(1)} %stack.156.info, bf16[128,1024]{1,0:T(8,128)(2,1)S(1)} %bitcast.191, bf16[128,1024]{1,0:T(8,128)(2,1)S(1)} %bitcast.186, bf16[128,1024]{1,0:T(8,128)(2,1)S(1)} %bitcast.187, ...), custom_call_target="tpu_custom_call" | custom-call | flops 2147483648 | bytes 1572864 | tf_op jit(solution)/shard_map/pallas_call | solution.py:384
  31.5 0.7 copy-done.2
  32.2 1.0 pad_maximum_fusion.10
  33.2 0.5 collective-permute-start.57
  33.7 1.5 %collective-permute-start.55 = (bf16[64,2048]{1,0:T(8,128)(2,1)S(1)}, bf16[64,2048]{1,0:T(8,128)(2,1)}, u32[]{:S(2)}, u32[]{:S(2)}) collective-permute-start(bf16[64,2048]{1,0:T(8,128)(2,1)S(1)} %collective-permute-done.49.refs_10_), channel_id=1, source_target_pairs={{0,4},{2,6},{4,0},{6,2},{8,12},{10,14},{12,8},{14,10},{16,20},{18,... | collective-permute-start | bytes 786440 | tf_op jit(solution)/shard_map/ppermute | solution.py:26
  35.2 6.8 %collective-permute-done.55.refs_11_ = bf16[64,2048]{1,0:T(8,128)(2,1)} collective-permute-done((bf16[64,2048]{1,0:T(8,128)(2,1)S(1)}, bf16[64,2048]{1,0:T(8,128)(2,1)}, u32[]{:S(2)}, u32[]{:S(2)}) %collective-permute-start.55) | collective-permute-done | bytes 262176 | tf_op jit(solution)/shard_map/ppermute | solution.py:26
  42.0 0.6 fusion.36
  44.6 0.2 slice_reduce_fusion.1
  44.9 0.9 copy-done.3
  45.8 3.1 %shard_map.132 = (bf16[128,2048]{1,0:T(8,128)(2,1)}, bf16[48,2048]{1,0:T(8,128)(2,1)}) custom-call(bf16[8,128,128]{2,1,0:T(8,128)(2,1)S(1)} %copy-done.3, bf16[128,2048]{1,0:T(8,128)(2,1)S(1)} %bitcast.185, f32[1,2048]{1,0:T(1,128)S(1)} %bitcast.190, bf16[128,48]{1,0:T(8,128)(2,1)S(1)} %get-tuple-element.241.refs_3_, bf16[64,2048]{1,0:T(8,128)(2,1)S(1)} %copy-done, ...), custom_call_target="tpu_custom_call" | custom-call | flops 536870912 | bytes 4194304 | tf_op jit(solution)/shard_map/pallas_call | solution.py:434
  48.9 72.9 %while.14 = (s32[]{:T(128)}, bf16[24,2048]{1,0:T(8,128)(2,1)S(1)}, bf16[24,2048]{1,0:T(8,128)(2,1)S(1)}, s32[]{:T(128)}, pred[]{:T(512)}, /*index=5*/s32[]{:T(12...) while((s32[]{:T(128)}, bf16[24,2048]{1,0:T(8,128)(2,1)S(1)}, ...), condition=%wide.region_7.8_spmd, body=%wide.region_0.7_spmd.sunk | while | flops 3331375104 | bytes 74122336 | solution.py:524
  49.1 0.7 fusion.41
  52.3 1.0 broadcast_select_fusion.7
  53.3 30.7 %conditional.4 = (bf16[384,2048]{1,0:T(8,128)(2,1)S(1)}, bf16[2,704,2048]{2,1,0:T(8,128)(2,1)}, bf16[704,2048]{1,0:T(8,128)(2,1)}) conditional(s32[]{:T(128)} %get-tuple-element.483, (bf16[24,2048]{1,0:T(8,128)(2,1)S(1)}, bf16[24,2048]{1,0:T(8,128)(2,1)S(1)}, bf16[2,704,2048]{2,1,0:T(8,128)(2,1)}, ...), branch_computations={%region_1.1_spmd, %region_2.2_spmd, %region_3.3_spmd} | conditional | flops 6684672 | bytes 51118464 | solution.py:491
  53.3 0.6 collective-permute-start.7
  53.9 0.1 collective-permute-start.8
  53.9 2.1 %collective-permute-start.2 = (bf16[24,2048]{1,0:T(8,128)(2,1)S(1)}, bf16[24,2048]{1,0:T(8,128)(2,1)S(1)}, u32[]{:S(2)}, u32[]{:S(2)}) collective-permute-start(bf16[24,2048]{1,0:T(8,128)(2,1)S(1)} %get-tuple-element.173), channel_id=1, source_target_pairs={{0,24},{2,26},{4,28},{6,30},{8,16},{10,18},{12,20},{14,22},{16,8},... | collective-permute-start | bytes 294920 | tf_op jit(solution)/shard_map/while/body/cond/branch_0_fun/ppermute | solution.py:26
  56.0 0.7 collective-permute-start
  56.8 1.6 %collective-permute-start.1 = (bf16[24,2048]{1,0:T(8,128)(2,1)S(1)}, bf16[24,2048]{1,0:T(8,128)(2,1)S(1)}, u32[]{:S(2)}, u32[]{:S(2)}) collective-permute-start(bf16[24,2048]{1,0:T(8,128)(2,1)S(1)} %get-tuple-element.172), channel_id=1, source_target_pairs={{0,8},{2,10},{4,12},{6,14},{8,0},{10,2},{12,4},{14,6},{16,24},{18,... | collective-permute-start | bytes 294920 | tf_op jit(solution)/shard_map/while/body/cond/branch_0_fun/ppermute | solution.py:26
  58.3 7.9 %collective-permute-done = bf16[24,2048]{1,0:T(8,128)(2,1)S(1)} collective-permute-done((bf16[24,2048]{1,0:T(8,128)(2,1)S(1)}, bf16[24,2048]{1,0:T(8,128)(2,1)S(1)}, u32[]{:S(2)}, u32[]{:S(2)}) %collective-permute-start) | collective-permute-done | bytes 98336 | tf_op jit(solution)/shard_map/while/body/cond/branch_0_fun/ppermute | solution.py:26
  66.3 0.1 slice_bitcast_fusion.1
  66.4 0.1 collective-permute-start.5
  66.4 1.2 collective-permute-start.3
  67.6 5.2 %collective-permute-done.5 = bf16[96,1024]{1,0:T(8,128)(2,1)S(1)} collective-permute-done((bf16[96,1024]{1,0:T(8,128)(2,1)S(1)}, bf16[96,1024]{1,0:T(8,128)(2,1)S(1)}, u32[]{:S(2)}, u32[]{:S(2)}) %collective-permute-start.5) | collective-permute-done | bytes 196640 | tf_op jit(solution)/shard_map/while/body/cond/branch_0_fun/ppermute | solution.py:26
  72.9 1.2 collective-permute-start.6
  74.2 0.5 collective-permute-start.4
  74.7 8.0 %collective-permute-done.6 = bf16[2,96,1024]{2,1,0:T(8,128)(2,1)S(1)} collective-permute-done((bf16[2,96,1024]{2,1,0:T(8,128)(2,1)S(1)}, bf16[2,96,1024]{2,1,0:T(8,128)(2,1)S(1)}, u32[]{:S(2)}, u32[]{:S(2)}) %collective-permute-start.6) | collective-permute-done | bytes 393248 | tf_op jit(solution)/shard_map/while/body/cond/branch_0_fun/ppermute | solution.py:26
  82.8 1.0 collective-permute-done.4
  83.7 0.1 maximum_maximum_fusion
  83.9 0.1 copy.26
  84.0 7.1 %body.3 = bf16[384,2048]{1,0:T(8,128)(2,1)S(1)} custom-call(s32[1]{0:T(128)} %bitcast.176.other, bf16[384,2048]{1,0:T(8,128)(2,1)S(1)} %get-tuple-element.417.rows, bf16[2,704,2048]{2,1,0:T(8,128)(2,1)} %get-tuple-element.481.gate_up_near, bf16[2,704,2048]{2,1,0:T(8,128)(2,1)} %get-tuple-element.418.gate_up_far, bf16[704,2048]{1,0:T(8,128)(2,1)} %bitcast.208, ...), custom_call_target="tpu_custom_call" | custom-call | flops 3321888768 | bytes 8650752 | tf_op jit(solution)/shard_map/while/body/pallas_call | solution.py:494
  91.2 30.6 %conditional.5 = (bf16[24,2048]{1,0:T(8,128)(2,1)S(1)}, bf16[24,2048]{1,0:T(8,128)(2,1)S(1)}) conditional(s32[]{:T(128)} %get-tuple-element.483, (s32[]{:T(128)}, bf16[384,2048]{1,0:T(8,128)(2,1)S(1)}, s32[]{:T(128)}) %tuple.95, (s32[]{:T(128)}, bf16[384,2048]{1,0:T(8,128)(2,1)S(1)}, s32[]{:T(128)}) %tuple.95, (s32[]{:T(128)}, ...), branch_computations={%region_4.4_spmd, %region_5.5_spmd, %region_6.6_spmd} | conditional | flops 2359302 | bytes 13369707 | solution.py:514
  91.2 0.7 collective-permute-start.27
  91.9 1.1 collective-permute-start.29
  93.0 6.9 %collective-permute-done.27 = bf16[2,96,1024]{2,1,0:T(8,128)(2,1)S(1)} collective-permute-done((bf16[2,96,1024]{2,1,0:T(8,128)(2,1)S(1)}, bf16[2,96,1024]{2,1,0:T(8,128)(2,1)S(1)}, u32[]{:S(2)}, u32[]{:S(2)}) %collective-permute-start.27) | collective-permute-done | bytes 393248 | tf_op jit(solution)/shard_map/while/body/cond/branch_0_fun/ppermute | solution.py:26
  99.8 0.1 fusion.6
  100.0 1.0 collective-permute-start.28
  101.0 0.4 collective-permute-done.29
  101.5 1.8 %collective-permute-start.30 = (bf16[96,1024]{1,0:T(8,128)(2,1)S(1)}, bf16[96,1024]{1,0:T(8,128)(2,1)S(1)}, u32[]{:S(2)}, u32[]{:S(2)}) collective-permute-start(bf16[96,1024]{1,0:T(8,128)(2,1)S(1)} %slice_bitcast_fusion.10), channel_id=1, source_target_pairs={{0,1},{1,0},{2,3},{3,2},{4,5},{5,4},{6,7},{7,6},{8,9},{9,8},{10,11... | collective-permute-start | bytes 589832 | tf_op jit(solution)/shard_map/while/body/cond/branch_0_fun/ppermute | solution.py:26
  103.3 2.4 %collective-permute-done.28 = bf16[96,1024]{1,0:T(8,128)(2,1)S(1)} collective-permute-done((bf16[96,1024]{1,0:T(8,128)(2,1)S(1)}, bf16[96,1024]{1,0:T(8,128)(2,1)S(1)}, u32[]{:S(2)}, u32[]{:S(2)}) %collective-permute-start.28) | collective-permute-done | bytes 196640 | tf_op jit(solution)/shard_map/while/body/cond/branch_0_fun/ppermute | solution.py:26
  105.8 1.4 %collective-permute-done.30 = bf16[96,1024]{1,0:T(8,128)(2,1)S(1)} collective-permute-done((bf16[96,1024]{1,0:T(8,128)(2,1)S(1)}, bf16[96,1024]{1,0:T(8,128)(2,1)S(1)}, u32[]{:S(2)}, u32[]{:S(2)}) %collective-permute-start.30) | collective-permute-done | bytes 196640 | tf_op jit(solution)/shard_map/while/body/cond/branch_0_fun/ppermute | solution.py:26
  107.3 0.3 collective-permute-start.31
  107.6 5.5 %collective-permute-done.31 = bf16[24,2048]{1,0:T(8,128)(2,1)S(1)} collective-permute-done((bf16[24,2048]{1,0:T(8,128)(2,1)S(1)}, bf16[24,2048]{1,0:T(8,128)(2,1)S(1)}, u32[]{:S(2)}, u32[]{:S(2)}) %collective-permute-start.31) | collective-permute-done | bytes 98336 | tf_op jit(solution)/shard_map/while/body/cond/branch_0_fun/ppermute | solution.py:26
  113.1 3.1 %collective-permute-start.33 = (bf16[24,2048]{1,0:T(8,128)(2,1)S(1)}, bf16[24,2048]{1,0:T(8,128)(2,1)S(1)}, u32[]{:S(2)}, u32[]{:S(2)}) collective-permute-start(bf16[24,2048]{1,0:T(8,128)(2,1)S(1)} %get-tuple-element.303), channel_id=1, source_target_pairs={{0,24},{2,26},{4,28},{6,30},{8,16},{10,18},{12,20},{14,22},{16,8},... | collective-permute-start | bytes 294920 | tf_op jit(solution)/shard_map/while/body/cond/branch_0_fun/ppermute | solution.py:26
  116.2 3.4 %collective-permute-done.33 = bf16[24,2048]{1,0:T(8,128)(2,1)S(1)} collective-permute-done((bf16[24,2048]{1,0:T(8,128)(2,1)S(1)}, bf16[24,2048]{1,0:T(8,128)(2,1)S(1)}, u32[]{:S(2)}, u32[]{:S(2)}) %collective-permute-start.33) | collective-permute-done | bytes 98336 | tf_op jit(solution)/shard_map/while/body/cond/branch_0_fun/ppermute | solution.py:26
  119.6 2.1 %collective-permute-done.32 = bf16[24,2048]{1,0:T(8,128)(2,1)S(1)} collective-permute-done((bf16[24,2048]{1,0:T(8,128)(2,1)S(1)}, bf16[24,2048]{1,0:T(8,128)(2,1)S(1)}, u32[]{:S(2)}, u32[]{:S(2)}) %collective-permute-start.32) | collective-permute-done | bytes 98336 | tf_op jit(solution)/shard_map/while/body/cond/branch_0_fun/ppermute | solution.py:26
  121.8 0.1 select_select_fusion.3
  121.8 0.3 convolution_multiply_fusion
  122.2 1.1 fusion.32
  (58 shorter events, 0.5 us)
Async XLA Ops:
  0.6 27.6 %copy-start.5 = (bf16[1,128,1024]{2,1,0:T(8,128)(2,1)S(1)}, bf16[1,128,1024]{2,1,0:T(8,128)(2,1)}, u32[]{:S(2)}) copy-start(bf16[1,128,1024]{2,1,0:T(8,128)(2,1)} %param.22) | copy-start | bytes 786436
  0.6 27.6 %copy-start.4 = (bf16[1,128,1024]{2,1,0:T(8,128)(2,1)S(1)}, bf16[1,128,1024]{2,1,0:T(8,128)(2,1)}, u32[]{:S(2)}) copy-start(bf16[1,128,1024]{2,1,0:T(8,128)(2,1)} %param.21) | copy-start | bytes 786436
  0.6 17.1 %collective-permute-start.51 = (bf16[64,2048]{1,0:T(8,128)(2,1)}, bf16[64,2048]{1,0:T(8,128)(2,1)S(1)}, u32[]{:S(2)}, u32[]{:S(2)}) collective-permute-start(bf16[64,2048]{1,0:T(8,128)(2,1)} %refs_4_.1), channel_id=1, source_target_pairs={{0,4},{2,6},{4,0},{6,2},{8,12},{10,14},{12,8},{14,10},{16,20},{18,... | collective-permute-start | bytes 786440 | tf_op jit(solution)/shard_map/ppermute | solution.py:26
  3.7 14.1 %collective-permute-start.50 = (bf16[64,2048]{1,0:T(8,128)(2,1)}, bf16[64,2048]{1,0:T(8,128)(2,1)S(1)}, u32[]{:S(2)}, u32[]{:S(2)}) collective-permute-start(bf16[64,2048]{1,0:T(8,128)(2,1)} %refs_4_.1), channel_id=1, source_target_pairs={{0,8},{2,10},{4,12},{6,14},{8,0},{10,2},{12,4},{14,6},{16,24},{18,... | collective-permute-start | bytes 786440 | tf_op jit(solution)/shard_map/ppermute | solution.py:26
  6.3 18.5 %collective-permute-start.53 = (bf16[2,128,1024]{2,1,0:T(8,128)(2,1)S(1)}, bf16[2,128,1024]{2,1,0:T(8,128)(2,1)S(1)}, u32[]{:S(2)}, u32[]{:S(2)}) collective-permute-start(bf16[2,128,1024]{2,1,0:T(8,128)(2,1)S(1)} %pad_maximum_fusion.11), channel_id=1, source_target_pairs={{0,1},{2,3},{4,5},{6,7},{8,9},{10,11},{12,13},{14,15},{16,17},{18,... | collective-permute-start | bytes 1572872 | tf_op jit(solution)/shard_map/ppermute | solution.py:368
  9.8 14.0 %collective-permute-start.48 = (bf16[64,2048]{1,0:T(8,128)(2,1)}, bf16[64,2048]{1,0:T(8,128)(2,1)S(1)}, u32[]{:S(2)}, u32[]{:S(2)}) collective-permute-start(bf16[64,2048]{1,0:T(8,128)(2,1)} %refs_4_.1), channel_id=1, source_target_pairs={{0,16},{2,18},{4,20},{6,22},{8,24},{10,26},{12,28},{14,30},{16,0},... | collective-permute-start | bytes 786440 | tf_op jit(solution)/shard_map/ppermute | solution.py:26
  17.8 10.5 %copy-start.6 = (s32[1,128,6]{2,1,0:T(8,128)S(1)}, s32[1,128,6]{2,1,0:T(8,128)}, u32[]{:S(2)}) copy-start(s32[1,128,6]{2,1,0:T(8,128)} %copy.34) | copy-start | bytes 9220
  17.8 10.5 %copy-start.7 = (f32[1,128,6]{2,1,0:T(8,128)S(1)}, f32[1,128,6]{2,1,0:T(8,128)}, u32[]{:S(2)}) copy-start(f32[1,128,6]{2,1,0:T(8,128)} %copy.35) | copy-start | bytes 9220
  17.8 10.5 %copy-start.11 = (bf16[1,128,1024]{2,1,0:T(8,128)(2,1)S(1)}, bf16[1,128,1024]{2,1,0:T(8,128)(2,1)}, u32[]{:S(2)}) copy-start(bf16[1,128,1024]{2,1,0:T(8,128)(2,1)} %param.20) | copy-start | bytes 786436
  17.8 7.0 %collective-permute-start.52 = (bf16[64,2048]{1,0:T(8,128)(2,1)S(1)}, bf16[64,2048]{1,0:T(8,128)(2,1)S(1)}, u32[]{:S(2)}, u32[]{:S(2)}) collective-permute-start(bf16[64,2048]{1,0:T(8,128)(2,1)S(1)} %collective-permute-done.50.refs_6_), channel_id=1, source_target_pairs={{0,4},{2,6},{4,0},{6,2},{8,12},{10,14},{12,8},{14,10},{16,20},{18,... | collective-permute-start | bytes 786440 | tf_op jit(solution)/shard_map/ppermute | solution.py:26
  23.8 8.4 %collective-permute-start.49 = (bf16[64,2048]{1,0:T(8,128)(2,1)S(1)}, bf16[64,2048]{1,0:T(8,128)(2,1)S(1)}, u32[]{:S(2)}, u32[]{:S(2)}) collective-permute-start(bf16[64,2048]{1,0:T(8,128)(2,1)S(1)} %collective-permute-done.48.refs_8_), channel_id=1, source_target_pairs={{0,8},{2,10},{4,12},{6,14},{8,0},{10,2},{12,4},{14,6},{16,24},{18,... | collective-permute-start | bytes 786440 | tf_op jit(solution)/shard_map/ppermute | solution.py:26
  24.8 0.8 copy-start.9
  25.6 6.6 %collective-permute-start.54 = (bf16[64,2048]{1,0:T(8,128)(2,1)S(1)}, bf16[64,2048]{1,0:T(8,128)(2,1)S(1)}, u32[]{:S(2)}, u32[]{:S(2)}) collective-permute-start(bf16[64,2048]{1,0:T(8,128)(2,1)S(1)} %collective-permute-done.48.refs_8_), channel_id=1, source_target_pairs={{0,4},{2,6},{4,0},{6,2},{8,12},{10,14},{12,8},{14,10},{16,20},{18,... | collective-permute-start | bytes 786440 | tf_op jit(solution)/shard_map/ppermute | solution.py:26
  26.1 2.1 %copy-start.10 = (bf16[2,128,1024]{2,1,0:T(8,128)(2,1)S(1)}, bf16[2,128,1024]{2,1,0:T(8,128)(2,1)}, u32[]{:S(2)}) copy-start(bf16[2,128,1024]{2,1,0:T(8,128)(2,1)} %copy-done.9) | copy-start | bytes 1572868
  28.2 16.6 %collective-permute-start.56 = (bf16[4,64,2048]{2,1,0:T(8,128)(2,1)}, bf16[4,64,2048]{2,1,0:T(8,128)(2,1)S(1)}, u32[]{:S(2)}, u32[]{:S(2)}) collective-permute-start(bf16[4,64,2048]{2,1,0:T(8,128)(2,1)} %pad_maximum_fusion.9), channel_id=1, source_target_pairs={{0,2},{2,0},{4,6},{6,4},{8,10},{10,8},{12,14},{14,12},{16,18},{18,... | collective-permute-start | bytes 3145736 | tf_op jit(solution)/shard_map/ppermute | solution.py:26
  31.5 0.7 copy-start.2
  32.2 9.8 %copy-start.12 = (s32[16]{0:T(128)S(1)}, s32[16]{0:T(128)}, u32[]{:S(2)}) copy-start(s32[16]{0:T(128)} %param.31) | copy-start | bytes 196
  32.2 12.7 %copy-start = (bf16[64,2048]{1,0:T(8,128)(2,1)S(1)}, bf16[64,2048]{1,0:T(8,128)(2,1)}, u32[]{:S(2)}) copy-start(bf16[64,2048]{1,0:T(8,128)(2,1)} %refs_4_.1) | copy-start | bytes 786436
  32.2 12.7 %copy-start.1 = (bf16[1,128,2048]{2,1,0:T(8,128)(2,1)S(1)}, bf16[1,128,2048]{2,1,0:T(8,128)(2,1)}, u32[]{:S(2)}) copy-start(bf16[1,128,2048]{2,1,0:T(8,128)(2,1)} %param.23) | copy-start | bytes 1572868
  32.2 12.7 %copy-start.8 = (f32[2048]{0:T(1024)S(1)}, f32[2048]{0:T(1024)}, u32[]{:S(2)}) copy-start(f32[2048]{0:T(1024)} %param.25) | copy-start | bytes 24580
  33.2 11.6 %collective-permute-start.57 = (bf16[3,64,2048]{2,1,0:T(8,128)(2,1)}, bf16[3,64,2048]{2,1,0:T(8,128)(2,1)}, u32[]{:S(2)}, u32[]{:S(2)}) collective-permute-start(bf16[3,64,2048]{2,1,0:T(8,128)(2,1)} %pad_maximum_fusion.10), channel_id=1, source_target_pairs={{0,2},{2,0},{4,6},{6,4},{8,10},{10,8},{12,14},{14,12},{16,18},{18,... | collective-permute-start | bytes 2359304 | tf_op jit(solution)/shard_map/ppermute | solution.py:26
  33.7 8.3 %collective-permute-start.55 = (bf16[64,2048]{1,0:T(8,128)(2,1)S(1)}, bf16[64,2048]{1,0:T(8,128)(2,1)}, u32[]{:S(2)}, u32[]{:S(2)}) collective-permute-start(bf16[64,2048]{1,0:T(8,128)(2,1)S(1)} %collective-permute-done.49.refs_10_), channel_id=1, source_target_pairs={{0,4},{2,6},{4,0},{6,2},{8,12},{10,14},{12,8},{14,10},{16,20},{18,... | collective-permute-start | bytes 786440 | tf_op jit(solution)/shard_map/ppermute | solution.py:26
  42.0 2.8 %collective-permute-start.58 = (bf16[1,64,2048]{2,1,0:T(8,128)(2,1)}, bf16[1,64,2048]{2,1,0:T(8,128)(2,1)}, u32[]{:S(2)}, u32[]{:S(2)}) collective-permute-start(bf16[1,64,2048]{2,1,0:T(8,128)(2,1)} %bitcast.83), channel_id=1, source_target_pairs={{0,2},{2,0},{4,6},{6,4},{8,10},{10,8},{12,14},{14,12},{16,18},{18,... | collective-permute-start | bytes 786440 | tf_op jit(solution)/shard_map/ppermute | solution.py:26
  44.9 1.0 copy-start.3
  53.3 30.7 %collective-permute-start.7 = (bf16[2,704,2048]{2,1,0:T(8,128)(2,1)}, bf16[2,704,2048]{2,1,0:T(8,128)(2,1)}, u32[]{:S(2)}, u32[]{:S(2)}) collective-permute-start(bf16[2,704,2048]{2,1,0:T(8,128)(2,1)} %get-tuple-element.174), channel_id=1, source_target_pairs={{0,2},{2,0},{4,6},{6,4},{8,10},{10,8},{12,14},{14,12},{16,18},{18,... | collective-permute-start | bytes 17301512 | tf_op jit(solution)/shard_map/while/body/cond/branch_0_fun/ppermute | solution.py:26
  53.9 30.1 %collective-permute-start.8 = (bf16[704,2048]{1,0:T(8,128)(2,1)}, bf16[704,2048]{1,0:T(8,128)(2,1)}, u32[]{:S(2)}, u32[]{:S(2)}) collective-permute-start(bf16[704,2048]{1,0:T(8,128)(2,1)} %bitcast.209), channel_id=1, source_target_pairs={{0,2},{2,0},{4,6},{6,4},{8,10},{10,8},{12,14},{14,12},{16,18},{18,... | collective-permute-start | bytes 8650760 | tf_op jit(solution)/shard_map/while/body/cond/branch_0_fun/ppermute | solution.py:26
  53.9 12.3 %collective-permute-start.2 = (bf16[24,2048]{1,0:T(8,128)(2,1)S(1)}, bf16[24,2048]{1,0:T(8,128)(2,1)S(1)}, u32[]{:S(2)}, u32[]{:S(2)}) collective-permute-start(bf16[24,2048]{1,0:T(8,128)(2,1)S(1)} %get-tuple-element.173), channel_id=1, source_target_pairs={{0,24},{2,26},{4,28},{6,30},{8,16},{10,18},{12,20},{14,22},{16,8},... | collective-permute-start | bytes 294920 | tf_op jit(solution)/shard_map/while/body/cond/branch_0_fun/ppermute | solution.py:26
  56.0 10.2 %collective-permute-start = (bf16[24,2048]{1,0:T(8,128)(2,1)S(1)}, bf16[24,2048]{1,0:T(8,128)(2,1)S(1)}, u32[]{:S(2)}, u32[]{:S(2)}) collective-permute-start(bf16[24,2048]{1,0:T(8,128)(2,1)S(1)} %get-tuple-element.173), channel_id=1, source_target_pairs={{0,16},{2,18},{4,20},{6,22},{8,24},{10,26},{12,28},{14,30},{16,0},... | collective-permute-start | bytes 294920 | tf_op jit(solution)/shard_map/while/body/cond/branch_0_fun/ppermute | solution.py:26
  56.8 9.4 %collective-permute-start.1 = (bf16[24,2048]{1,0:T(8,128)(2,1)S(1)}, bf16[24,2048]{1,0:T(8,128)(2,1)S(1)}, u32[]{:S(2)}, u32[]{:S(2)}) collective-permute-start(bf16[24,2048]{1,0:T(8,128)(2,1)S(1)} %get-tuple-element.172), channel_id=1, source_target_pairs={{0,8},{2,10},{4,12},{6,14},{8,0},{10,2},{12,4},{14,6},{16,24},{18,... | collective-permute-start | bytes 294920 | tf_op jit(solution)/shard_map/while/body/cond/branch_0_fun/ppermute | solution.py:26
  66.4 6.5 %collective-permute-start.5 = (bf16[96,1024]{1,0:T(8,128)(2,1)S(1)}, bf16[96,1024]{1,0:T(8,128)(2,1)S(1)}, u32[]{:S(2)}, u32[]{:S(2)}) collective-permute-start(bf16[96,1024]{1,0:T(8,128)(2,1)S(1)} %get-tuple-element.283), channel_id=1, source_target_pairs={{0,1},{1,0},{2,3},{3,2},{4,5},{5,4},{6,7},{7,6},{8,9},{9,8},{10,11... | collective-permute-start | bytes 589832 | tf_op jit(solution)/shard_map/while/body/cond/branch_0_fun/ppermute | solution.py:26
  66.4 7.7 %collective-permute-start.3 = (bf16[96,1024]{1,0:T(8,128)(2,1)S(1)}, bf16[96,1024]{1,0:T(8,128)(2,1)S(1)}, u32[]{:S(2)}, u32[]{:S(2)}) collective-permute-start(bf16[96,1024]{1,0:T(8,128)(2,1)S(1)} %get-tuple-element.284), channel_id=1, source_target_pairs={{0,4},{2,6},{4,0},{6,2},{8,12},{10,14},{12,8},{14,10},{16,20},{18,... | collective-permute-start | bytes 589832 | tf_op jit(solution)/shard_map/while/body/cond/branch_0_fun/ppermute | solution.py:26
  72.9 9.8 %collective-permute-start.6 = (bf16[2,96,1024]{2,1,0:T(8,128)(2,1)S(1)}, bf16[2,96,1024]{2,1,0:T(8,128)(2,1)S(1)}, u32[]{:S(2)}, u32[]{:S(2)}) collective-permute-start(bf16[2,96,1024]{2,1,0:T(8,128)(2,1)S(1)} %get-tuple-element.286), channel_id=1, source_target_pairs={{0,4},{2,6},{4,0},{6,2},{8,12},{10,14},{12,8},{14,10},{16,20},{18,... | collective-permute-start | bytes 1179656 | tf_op jit(solution)/shard_map/while/body/cond/branch_0_fun/ppermute | solution.py:26
  74.2 9.6 %collective-permute-start.4 = (bf16[2,96,1024]{2,1,0:T(8,128)(2,1)S(1)}, bf16[2,96,1024]{2,1,0:T(8,128)(2,1)S(1)}, u32[]{:S(2)}, u32[]{:S(2)}) collective-permute-start(bf16[2,96,1024]{2,1,0:T(8,128)(2,1)S(1)} %get-tuple-element.280), channel_id=1, source_target_pairs={{0,1},{1,0},{2,3},{3,2},{4,5},{5,4},{6,7},{7,6},{8,9},{9,8},{10,11... | collective-permute-start | bytes 1179656 | tf_op jit(solution)/shard_map/while/body/cond/branch_0_fun/ppermute | solution.py:26
  91.2 8.6 %collective-permute-start.27 = (bf16[2,96,1024]{2,1,0:T(8,128)(2,1)S(1)}, bf16[2,96,1024]{2,1,0:T(8,128)(2,1)S(1)}, u32[]{:S(2)}, u32[]{:S(2)}) collective-permute-start(bf16[2,96,1024]{2,1,0:T(8,128)(2,1)S(1)} %slice_bitcast_fusion.8), channel_id=1, source_target_pairs={{0,1},{1,0},{2,3},{3,2},{4,5},{5,4},{6,7},{7,6},{8,9},{9,8},{10,11... | collective-permute-start | bytes 1179656 | tf_op jit(solution)/shard_map/while/body/cond/branch_0_fun/ppermute | solution.py:26
  91.9 9.5 %collective-permute-start.29 = (bf16[2,96,1024]{2,1,0:T(8,128)(2,1)S(1)}, bf16[2,96,1024]{2,1,0:T(8,128)(2,1)S(1)}, u32[]{:S(2)}, u32[]{:S(2)}) collective-permute-start(bf16[2,96,1024]{2,1,0:T(8,128)(2,1)S(1)} %slice_bitcast_fusion.6), channel_id=1, source_target_pairs={{0,4},{2,6},{4,0},{6,2},{8,12},{10,14},{12,8},{14,10},{16,20},{18,... | collective-permute-start | bytes 1179656 | tf_op jit(solution)/shard_map/while/body/cond/branch_0_fun/ppermute | solution.py:26
  100.0 5.7 %collective-permute-start.28 = (bf16[96,1024]{1,0:T(8,128)(2,1)S(1)}, bf16[96,1024]{1,0:T(8,128)(2,1)S(1)}, u32[]{:S(2)}, u32[]{:S(2)}) collective-permute-start(bf16[96,1024]{1,0:T(8,128)(2,1)S(1)} %slice_bitcast_fusion.12), channel_id=1, source_target_pairs={{0,4},{2,6},{4,0},{6,2},{8,12},{10,14},{12,8},{14,10},{16,20},{18,... | collective-permute-start | bytes 589832 | tf_op jit(solution)/shard_map/while/body/cond/branch_0_fun/ppermute | solution.py:26
  101.5 5.7 %collective-permute-start.30 = (bf16[96,1024]{1,0:T(8,128)(2,1)S(1)}, bf16[96,1024]{1,0:T(8,128)(2,1)S(1)}, u32[]{:S(2)}, u32[]{:S(2)}) collective-permute-start(bf16[96,1024]{1,0:T(8,128)(2,1)S(1)} %slice_bitcast_fusion.10), channel_id=1, source_target_pairs={{0,1},{1,0},{2,3},{3,2},{4,5},{5,4},{6,7},{7,6},{8,9},{9,8},{10,11... | collective-permute-start | bytes 589832 | tf_op jit(solution)/shard_map/while/body/cond/branch_0_fun/ppermute | solution.py:26
  107.3 5.8 %collective-permute-start.31 = (bf16[24,2048]{1,0:T(8,128)(2,1)S(1)}, bf16[24,2048]{1,0:T(8,128)(2,1)S(1)}, u32[]{:S(2)}, u32[]{:S(2)}) collective-permute-start(bf16[24,2048]{1,0:T(8,128)(2,1)S(1)} %fusion.13), channel_id=1, source_target_pairs={{0,8},{2,10},{4,12},{6,14},{8,0},{10,2},{12,4},{14,6},{16,24},{18,... | collective-permute-start | bytes 294920 | tf_op jit(solution)/shard_map/while/body/cond/branch_0_fun/ppermute | solution.py:26
  113.1 6.5 %collective-permute-start.33 = (bf16[24,2048]{1,0:T(8,128)(2,1)S(1)}, bf16[24,2048]{1,0:T(8,128)(2,1)S(1)}, u32[]{:S(2)}, u32[]{:S(2)}) collective-permute-start(bf16[24,2048]{1,0:T(8,128)(2,1)S(1)} %get-tuple-element.303), channel_id=1, source_target_pairs={{0,24},{2,26},{4,28},{6,30},{8,16},{10,18},{12,20},{14,22},{16,8},... | collective-permute-start | bytes 294920 | tf_op jit(solution)/shard_map/while/body/cond/branch_0_fun/ppermute | solution.py:26
  116.2 5.5 %collective-permute-start.32 = (bf16[24,2048]{1,0:T(8,128)(2,1)S(1)}, bf16[24,2048]{1,0:T(8,128)(2,1)S(1)}, u32[]{:S(2)}, u32[]{:S(2)}) collective-permute-start(bf16[24,2048]{1,0:T(8,128)(2,1)S(1)} %get-tuple-element.305), channel_id=1, source_target_pairs={{0,16},{2,18},{4,20},{6,22},{8,24},{10,26},{12,28},{14,30},{16,0},... | collective-permute-start | bytes 294920 | tf_op jit(solution)/shard_map/while/body/cond/branch_0_fun/ppermute | solution.py:26

commit v3 on v2

--- a/solution.py
+++ b/solution.py
@@ -185,33 +185,27 @@
         mixed = jnp.where(jnp.broadcast_to(info[2], mixed.shape) == 0, mixed, swapped)
         attended[head ^ info[1]] = mixed.astype(jnp.bfloat16)
 
-    slots = PASS_SPECIALISTS * CAP
-    lane = lax.broadcasted_iota(jnp.int32, (token_count, slots), 1)
-    routed = jnp.zeros((token_count, slots), jnp.float32)
-    limit = jnp.zeros((token_count, slots), jnp.int32)
-    for expert in range(PASS_SPECIALISTS):
-        matches = ids[...] == expert
+    slot = lax.broadcasted_iota(jnp.int32, (token_count, CAP), 1)
+    earlier = (col < row).astype(jnp.bfloat16)
+    for k in range(PASS_SPECIALISTS):
+        matches = ids[...] == info[3 + 2 * k]
         named = jnp.max(matches.astype(jnp.float32), axis=1, keepdims=True)
-        gate_values[:, expert : expert + 1] = jnp.sum(
+        gate_values[:, k : k + 1] = jnp.sum(
             jnp.where(matches, gates[...], 0.0), axis=1, keepdims=True
         )
-        mine = (lane >= expert * CAP) & (lane < (expert + 1) * CAP)
-        routed = jnp.where(mine, named, routed)
-        limit = jnp.where(mine, info[3 + expert], limit)
-    earlier = (col < row).astype(jnp.bfloat16)
-    rank = jnp.dot(
-        earlier, routed.astype(jnp.bfloat16), preferred_element_type=jnp.float32
-    ).astype(jnp.int32)
-    slot = jnp.where(lane >= CAP, lane - CAP, lane)
-    place[...] = ((routed > 0.0) & (rank == slot) & (rank < limit)).astype(jnp.bfloat16)
-
-
-def project_kernel(far_place, *refs):
-    attended, residual, gain, place = refs[:4]
-    near = refs[4 : 4 + HEADS]
-    groups = refs[4 + HEADS : -3]
+        routed = jnp.broadcast_to(named, (token_count, CAP))
+        rank = jnp.dot(
+            earlier, routed.astype(jnp.bfloat16), preferred_element_type=jnp.float32
+        ).astype(jnp.int32)
+        kept = (routed > 0.0) & (rank == slot) & (rank < info[4 + 2 * k])
+        place[k] = kept.astype(jnp.bfloat16)
+
+
+def project_kernel(far_place, same, attended, residual, gain, place, *refs):
+    near = refs[:HEADS]
+    groups = refs[HEADS:-5]
+    attn_proj, kept, sent, second, combined = refs[-5:]
     far = [groups[group].at[k] for group, k in far_place]
-    attn_proj, chosen, combined = refs[-3:]
     token_count, width = residual.shape
     tile = 512
     squares = jnp.zeros((token_count, 1), jnp.float32)
@@ -232,12 +226,43 @@
         combined[:, span] = added
         squares = squares + jnp.sum(added * added, axis=1, keepdims=True)
     scale = lax.rsqrt(squares / width + EPSILON)
+    contract_first = (((0,), (0,)), ((), ()))
     for start in range(0, width, tile):
         span = slice(start, start + tile)
         normed = (combined[:, span] * scale * gain[:, span]).astype(jnp.bfloat16)
-        chosen[:, span] = lax.dot_general(
-            place[...], normed, (((0,), (0,)), ((), ())), preferred_element_type=jnp.float32
-        ).astype(jnp.bfloat16)
+        rows = [
+            lax.dot_general(place[k], normed, contract_first, preferred_element_type=jnp.float32)
+            for k in range(PASS_SPECIALISTS)
+        ]
+        kept[:, span] = rows[0].astype(jnp.bfloat16)
+        second[:, span] = rows[1].astype(jnp.bfloat16)
+        use_first = jnp.broadcast_to(same[0], rows[0].shape) != 0
+        sent[:, span] = jnp.where(use_first, rows[0], rows[1]).astype(jnp.bfloat16)
+
+
+def combine_kernel(flags, own, other, last_own, last_other, place, gate_values, out):
+    width = own.shape[1]
+    for start in range(0, width, 512):
+        span = slice(start, start + 512)
+        shape = (own.shape[0], 512)
+        same = jnp.broadcast_to(flags[0], shape) != 0
+        first_here = jnp.broadcast_to(flags[1], shape) != 0
+        second_here = jnp.broadcast_to(flags[2], shape) != 0
+        near, far = own[:, span].astype(jnp.float32), other[:, span].astype(jnp.float32)
+        last = jnp.where(
+            first_here,
+            last_own[:, span].astype(jnp.float32),
+            last_other[:, span].astype(jnp.float32),
+        )
+        first = jnp.where(same, last, near)
+        second = jnp.where(same, jnp.where(second_here, near, far), far)
+        total = 0.0
+        for k, rows in enumerate((first, second)):
+            picked = jnp.dot(
+                place[k], rows.astype(jnp.bfloat16), preferred_element_type=jnp.float32
+            )
+            total = total + gate_values[:, k : k + 1] * picked
+        out[:, span] = total.astype(jnp.bfloat16)
 
 
 def expert_kernel(other, rows, gate_up_near, gate_up_far, down_near, down_far, made, gate_up, down, hidden, sems):
@@ -328,7 +353,7 @@
     left = jnp.where(near, left[0], hop(left[1], "dp", dp_size, last))
     right = add(right[0], hop(right[1], "ctx", 2, 1))
     unit = jnp.concatenate([left, right], axis=-1)
-    here, across, beside, beyond = jnp.split(unit, 4, axis=0)
+    here, across, beside, beyond = lax.optimization_barrier(jnp.split(unit, 4, axis=0))
     across = hop(across, "dp", dp_size, first)
     beside = hop(beside, "dp", dp_size, second)
     beyond = hop(beyond, "dp", dp_size, first | second)
@@ -364,28 +389,80 @@
     ctx = lax.axis_index("ctx")
     bits = [1 << k for k in reversed(range(1, dp_size.bit_length() - 1))]
 
-    info = jnp.stack([ctx, me >> 1, core, capacity[0, 0, 0], capacity[0, 0, 1]]).astype(jnp.int32)
+    owners = expert_owner[:PASS_SPECIALISTS]
+    differ = owners[0] ^ owners[1]
+    branch = 0
+    split_bit = 0
+    for k in reversed(range(len(bits))):
+        parted = (differ & bits[k]) != 0
+        branch = jnp.where(parted, k, branch)
+        split_bit = jnp.where(parted, bits[k], split_bit)
+    same = split_bit == 0
+    swapped = ((me ^ owners[0]) & split_bit) != 0
+    offset = me ^ jnp.where(swapped, owners[1], owners[0])
+    second_offset = me ^ jnp.where(swapped, owners[0], owners[1])
+    other_offset = jnp.where(same, offset, second_offset)
+    first_expert = swapped.astype(jnp.int32)
+    caps = capacity[0, 0]
+    info = jnp.stack(
+        [
+            ctx,
+            me >> 1,
+            core,
+            first_expert,
+            jnp.where(swapped, caps[1], caps[0]),
+            1 - first_expert,
+            jnp.where(swapped, caps[0], caps[1]),
+        ]
+    ).astype(jnp.int32)
+    flags = jnp.stack(
+        [same, (offset & bits[0]) == 0, (second_offset & bits[0]) == 0]
+    ).astype(jnp.int32)
+    passes = jnp.where(same, 2, 1)
     before = lax.ppermute(jnp.stack([key_vecs[0], value_vecs[0]]), "ctx", [(0, 1)])
     z_far, z_near, x_bit = bits
     z_both = z_far | z_near
     near = {0: w_out}
     for bit in (z_near, x_bit, z_far):
         near[bit] = hop(w_out, "dp", dp_size, bit)
-    near[z_near], near[x_bit], info, ids, gates = lax.optimization_barrier(
-        (near[z_near], near[x_bit], info, expert_ids[0], route_gates[0])
+    (
+        near[z_near],
+        near[x_bit],
+        near[z_far],
+        info,
+        flags,
+        passes,
+        branch,
+        offset,
+        second_offset,
+        other_offset,
+        ids,
+        gates,
+    ) = lax.optimization_barrier(
+        (
+            near[z_near],
+            near[x_bit],
+            near[z_far],
+            info,
+            flags,
+            passes,
+            branch,
+            offset,
+            second_offset,
+            other_offset,
+            expert_ids[0],
+            route_gates[0],
+        )
     )
     near[z_near | x_bit] = hop(near[z_near], "dp", dp_size, x_bit)
     near[z_both] = hop(near[z_far], "dp", dp_size, z_near)
-    next_sent, near[z_near | x_bit], before = lax.optimization_barrier(
-        (near[z_far], near[z_near | x_bit], before)
-    )
-    near[z_far | x_bit] = hop(next_sent, "dp", dp_size, x_bit)
-    slots = PASS_SPECIALISTS * CAP
+    near[z_far | x_bit] = hop(near[z_far], "dp", dp_size, x_bit)
+    before, near[z_near | x_bit] = lax.optimization_barrier((before, near[z_near | x_bit]))
     attended, place, gate_values = pl.pallas_call(
         attend_kernel,
         out_shape=(
             jax.ShapeDtypeStruct((HEADS, token_count, HD), jnp.bfloat16),
-            jax.ShapeDtypeStruct((token_count, slots), jnp.bfloat16),
+            jax.ShapeDtypeStruct((PASS_SPECIALISTS, token_count, CAP), jnp.bfloat16),
             jax.ShapeDtypeStruct((token_count, PASS_SPECIALISTS), jnp.float32),
         ),
         in_specs=[pl.BlockSpec(memory_space=pltpu.SMEM)] + vmem(6),
@@ -395,7 +472,7 @@
             bytes_accessed=6 * 2 * token_count * HEADS * HD,
             transcendentals=2 * HEADS * token_count * token_count,
         ),
-        compiler_params=pltpu.CompilerParams(vmem_limit_bytes=16 * 2**20),
+        compiler_params=pltpu.CompilerParams(vmem_limit_bytes=8 * 2**20),
     )(
         info,
         query_vecs[0],
@@ -405,16 +482,14 @@
         ids,
         gates,
     )
-    near[z_both], near[z_far | x_bit], attended = lax.optimization_barrier(
-        (near[z_both], near[z_far | x_bit], attended)
-    )
+    near[z_both], attended = lax.optimization_barrier((near[z_both], attended))
     near[z_both | x_bit] = hop(near[z_both], "dp", dp_size, x_bit)
     far = [
         hop(jnp.stack([near[j] for j in group]), "dp", dp_size, 1)
         for group in (
             (0, z_near, x_bit, z_far),
-            (z_near | x_bit, z_far | x_bit, z_both),
-            (z_both | x_bit,),
+            (z_near | x_bit, z_both),
+            (z_far | x_bit, z_both | x_bit),
         )
     ]
     far_place = {
@@ -423,41 +498,34 @@
         x_bit: (0, 2),
         z_far: (0, 3),
         z_near | x_bit: (1, 0),
-        z_far | x_bit: (1, 1),
-        z_both: (1, 2),
-        z_both | x_bit: (2, 0),
+        z_both: (1, 1),
+        z_far | x_bit: (2, 0),
+        z_both | x_bit: (2, 1),
     }
     far_place = [far_place[2 * j] for j in range(HEADS)]
     shares = [near[2 * j] for j in range(HEADS)] + far
     gate_up_near = jnp.swapaxes(w_gate_up[0], 1, 2)
 
-    attn_proj, chosen = pl.pallas_call(
+    some_rows = jax.ShapeDtypeStruct((CAP, width), jnp.bfloat16)
+    attn_proj, kept, sent, second = pl.pallas_call(
         functools.partial(project_kernel, far_place),
         out_shape=(
             jax.ShapeDtypeStruct((token_count, width), jnp.bfloat16),
-            jax.ShapeDtypeStruct((slots, width), jnp.bfloat16),
+            some_rows,
+            some_rows,
+            some_rows,
         ),
-        in_specs=vmem(4 + len(shares)),
-        out_specs=tuple(vmem(2)),
+        in_specs=[pl.BlockSpec(memory_space=pltpu.SMEM)] + vmem(4 + len(shares)),
+        out_specs=tuple(vmem(4)),
         scratch_shapes=[pltpu.VMEM((token_count, width), jnp.float32)],
         cost_estimate=pl.CostEstimate(
             flops=2 * token_count * HEADS * HD * width,
             bytes_accessed=2 * HEADS * HD * width,
             transcendentals=0,
         ),
-        compiler_params=pltpu.CompilerParams(vmem_limit_bytes=24 * 2**20),
-    )(attended, residual[0], norm_gain[None], place, *shares)
-
-    owners = expert_owner[:PASS_SPECIALISTS]
-    differ = owners[0] ^ owners[1]
-    branch = 0
-    split_bit = 0
-    for k in reversed(range(len(bits))):
-        parted = (differ & bits[k]) != 0
-        branch = jnp.where(parted, k, branch)
-        split_bit = jnp.where(parted, bits[k], split_bit)
-    same = split_bit == 0
-    side = jnp.where(((me ^ owners[0]) & split_bit) == 0, 0, 1)
+        compiler_params=pltpu.CompilerParams(vmem_limit_bytes=16 * 2**20),
+    )(flags, attended, residual[0], norm_gain[None], place, *shares)
+
     units = w_down.shape[1]
     row_count = dp_size * CAP
 
@@ -480,14 +548,8 @@
 
         return run
 
-    def one_pass(step, produced):
-        local = jnp.where(same, step, side)
-        sent_expert = jnp.where(same, step, 1 - side)
-        owner = jnp.where(local == 0, owners[0], owners[1])
-        offset = me ^ owner
-        other_offset = me ^ jnp.where(sent_expert == 0, owners[0], owners[1])
-        kept = jnp.where(local == 0, chosen[:CAP], chosen[CAP:])
-        sent = jnp.where(sent_expert == 0, chosen[:CAP], chosen[CAP:])
+    def one_pass(_, carried):
+        kept, sent, offset, other_offset, last_own, last_other, _, _ = carried
         rows, gate_up_far, down_far = lax.switch(
             branch, [dispatch(bit) for bit in bits], kept, sent
         )
@@ -509,28 +571,23 @@
                 bytes_accessed=6 * units * width,
                 transcendentals=row_count * units,
             ),
-            compiler_params=pltpu.CompilerParams(vmem_limit_bytes=30 * 2**20),
+            compiler_params=pltpu.CompilerParams(vmem_limit_bytes=22 * 2**20),
         )((offset & 1)[None], rows, gate_up_near, gate_up_far, w_down[0], down_far)
-        own, other = lax.switch(branch, [give_back(bit) for bit in bits], made, offset, other_offset)
-        served = jnp.where((offset & bits[0]) == 0, own, other)
-        first = jnp.where(same, served, jnp.where(local == 0, own, other))
-        second = jnp.where(same, served, jnp.where(local == 0, other, own))
-        return (
-            jnp.where(same & (step != 0), produced[0], first),
-            jnp.where(same & (step != 1), produced[1], second),
-        )
+        own, other = lax.switch(
+            branch, [give_back(bit) for bit in bits], made, offset, other_offset
+        )
+        return second, second, second_offset, second_offset, own, other, last_own, last_other
 
     nothing = jnp.zeros((CAP, width), jnp.bfloat16)
-    produced = lax.fori_loop(0, jnp.where(same, 2, 1), one_pass, (nothing, nothing))
-    summed = 0.0
-    for expert in range(PASS_SPECIALISTS):
-        picked = jnp.dot(
-            place[:, expert * CAP : (expert + 1) * CAP],
-            produced[expert],
-            preferred_element_type=jnp.float32,
-        )
-        summed = summed + gate_values[:, expert : expert + 1] * picked
-    expert_sum = summed.astype(jnp.bfloat16)
+    carried = (kept, sent, offset, other_offset) + (nothing,) * 4
+    produced = lax.fori_loop(0, passes, one_pass, carried)[4:]
+    expert_sum = pl.pallas_call(
+        combine_kernel,
+        out_shape=jax.ShapeDtypeStruct((token_count, width), jnp.bfloat16),
+        in_specs=[pl.BlockSpec(memory_space=pltpu.SMEM)] + vmem(6),
+        out_specs=vmem(1)[0],
+        compiler_params=pltpu.CompilerParams(vmem_limit_bytes=8 * 2**20),
+    )(flags, *produced, place, gate_values)
     return (attn_proj[None], expert_sum[None])
 
 

time: 124 us -> 125 us (level)
  waiting for transfers between devices: 57.5 us -> 48.9 us
  between operations: 2.85 us -> 7.71 us
  local copies, waits for them, and re-layouts: 9.57 us -> 13.9 us
  Pallas kernels: 13.4 us -> 16.3 us
  loops' own time: 2.96 us -> 0.21 us
  matrix products: 1.42 us -> 0 us
    ppermute x26, waiting for transfers between devices: 57.5 us -> 48.9 us  [hop(): return lax.ppermute(array, axis, [(i, i ^ bit) for i in range(size)])]
    while x0 -> x8, local copies, waits for them, and re-layouts: none -> 4.09 us
    another operation x1, loops' own time: 2.76 us -> 0.04 us  [body_move_rows(): produced = lax.fori_loop(0, passes, one_pass, carried)[4:]]
    pallas_call x0 -> x1, Pallas kernels: none -> 2.23 us  [body_move_rows(): pl.pallas_call(combine_kernel, out_shape=jax.ShapeDtypeStruct((token_coun...]
    broadcast_in_dim x2 -> x4, local copies, waits for them, and re-layouts: 0.02 us -> 1.93 us  [body_move_rows(): nothing = jnp.zeros((CAP, width), jnp.bfloat16)]
    dot_general x2 -> x0, matrix products: 1.42 us -> none  [body_move_rows(): jnp.dot(place[:, expert * CAP:(expert + 1) * CAP], produced[expert], pref...]
    unnamed x28 -> x20, local copies, waits for them, and re-layouts: 5.31 us -> 3.9 us
    another operation x2 -> x3, other arithmetic: 3.06 us -> 3.73 us  [body_move_rows(): jnp.stack([near[j] for j in group])]
  transfers between devices with their start and end apart: 27 -> 27, of which waited for: 14 -> 16; matrix products, arithmetic and copies ran while one was open for 9% -> 10% of each run, Pallas kernels for 3% -> 3%
where the time goes in v3:
time: 125 us; the launch traced here: 124 us
  waiting for transfers between devices  48.9 us (39%)
  starting transfers between devices  30.9 us (25%)
  Pallas kernels  16.3 us (13%)
  local copies, waits for them, and re-layouts  13.9 us (11%)
  between operations  7.71 us (6%)
  other arithmetic  6.21 us (5%)
    ppermute x26, waiting for transfers between devices, hop(): return lax.ppermute(array, axis, [(i, i ^ bit) for i in range(size)])  48.9 us
    ppermute x26, starting transfers between devices, hop(): return lax.ppermute(array, axis, [(i, i ^ bit) for i in range(size)])  26.7 us
    pallas_call x1, Pallas kernels, one_pass(): pl.pallas_call(expert_kernel, out_shape=jax.ShapeDtypeStruct((row_count,...  7.18 us
    ppermute x1, starting transfers between devices, body_move_rows(): lax.ppermute(jnp.stack([key_vecs[0], value_vecs[0]]), 'ctx', [(0, 1)])  4.21 us
    while x8, local copies, waits for them, and re-layouts  4.09 us
    unnamed x20, local copies, waits for them, and re-layouts  3.9 us
    pallas_call x1, Pallas kernels, body_move_rows(): pl.pallas_call(attend_kernel, out_shape=(jax.ShapeDtypeStruct((HEADS, tok...  3.74 us
    another operation x3, other arithmetic, body_move_rows(): jnp.stack([near[j] for j in group])  3.73 us
  transfers between devices with their start and end apart: 27, of which 16 were waited for; matrix products, arithmetic and copies ran while one was open for 10% of the time, Pallas kernels for 3%

profile of v3, /device:TPU:0, one launch (start us, length us, event | category | flops | bytes accessed | tf_op | source)
XLA Modules:
  0.0 124.1 jit_solution(380407899919580279)
XLA Ops:
  0.6 3.1 %collective-permute-start.48 = (bf16[64,2048]{1,0:T(8,128)(2,1)}, bf16[64,2048]{1,0:T(8,128)(2,1)S(1)}, u32[]{:S(2)}, u32[]{:S(2)}) collective-permute-start(bf16[64,2048]{1,0:T(8,128)(2,1)} %refs_0_.1), channel_id=1, source_target_pairs={{0,8},{2,10},{4,12},{6,14},{8,0},{10,2},{12,4},{14,6},{16,24},{18,... | collective-permute-start | bytes 786440 | tf_op jit(solution)/shard_map/ppermute | solution.py:26
  3.7 1.5 %collective-permute-start.49 = (bf16[64,2048]{1,0:T(8,128)(2,1)}, bf16[64,2048]{1,0:T(8,128)(2,1)S(1)}, u32[]{:S(2)}, u32[]{:S(2)}) collective-permute-start(bf16[64,2048]{1,0:T(8,128)(2,1)} %refs_0_.1), channel_id=1, source_target_pairs={{0,4},{2,6},{4,0},{6,2},{8,12},{10,14},{12,8},{14,10},{16,20},{18,... | collective-permute-start | bytes 786440 | tf_op jit(solution)/shard_map/ppermute | solution.py:26
  5.2 2.6 %collective-permute-start.50 = (bf16[64,2048]{1,0:T(8,128)(2,1)}, bf16[64,2048]{1,0:T(8,128)(2,1)S(1)}, u32[]{:S(2)}, u32[]{:S(2)}) collective-permute-start(bf16[64,2048]{1,0:T(8,128)(2,1)} %refs_0_.1), channel_id=1, source_target_pairs={{0,16},{2,18},{4,20},{6,22},{8,24},{10,26},{12,28},{14,30},{16,0},... | collective-permute-start | bytes 786440 | tf_op jit(solution)/shard_map/ppermute | solution.py:26
  7.8 1.9 %pad_maximum_fusion.10 = bf16[2,128,1024]{2,1,0:T(8,128)(2,1)} fusion(bf16[1,128,1024]{2,1,0:T(8,128)(2,1)} %param.22, bf16[1,128,1024]{2,1,0:T(8,128)(2,1)} %param.21), kind=kLoop, calls=%fused_computation.112 | loop fusion | flops 262144 | bytes 1048576 | tf_op jit(solution)/shard_map/stack | solution.py:422
  9.7 4.2 %collective-permute-start.52 = (bf16[2,128,1024]{2,1,0:T(8,128)(2,1)}, bf16[2,128,1024]{2,1,0:T(8,128)(2,1)}, u32[]{:S(2)}, u32[]{:S(2)}) collective-permute-start(bf16[2,128,1024]{2,1,0:T(8,128)(2,1)} %pad_maximum_fusion.10), channel_id=1, source_target_pairs={{0,1},{2,3},{4,5},{6,7},{8,9},{10,11},{12,13},{14,15},{16,17},{18,... | collective-permute-start | bytes 1572872 | tf_op jit(solution)/shard_map/ppermute | solution.py:422
  13.9 1.3 %fusion.28 = (s32[1]{0:T(128)}, s32[1]{0:T(128)}) fusion(s32[16]{0:T(128)} %param.31), kind=kLoop, calls=%fused_computation.117 | loop fusion | bytes 16 | tf_op jit(solution)/shard_map/slice | solution.py:393
  17.1 1.3 %fusion.27 = (s32[1,1,1]{2,1,0:T(1,128)}, s32[1,1,1]{2,1,0:T(1,128)}) fusion(s32[1,1,2]{2,1,0:T(1,128)} %param.30), kind=kLoop, calls=%fused_computation.116 | loop fusion | bytes 16 | tf_op jit(solution)/shard_map/slice | solution.py:413
  23.6 0.8 copy.34
  24.4 1.4 %copy.35 = f32[1,128,6]{2,1,0:T(8,128)} copy(f32[1,128,6]{1,0,2:T(1,128)} %param.29) | data formatting | bytes 6144 | tf_op args[9]
  26.0 0.6 collective-permute-start.53
  26.6 0.4 collective-permute-start.51
  27.0 1.5 %collective-permute-start.54 = (bf16[64,2048]{1,0:T(8,128)(2,1)S(1)}, bf16[64,2048]{1,0:T(8,128)(2,1)S(1)}, u32[]{:S(2)}, u32[]{:S(2)}) collective-permute-start(bf16[64,2048]{1,0:T(8,128)(2,1)S(1)} %collective-permute-done.50.refs_4_), channel_id=1, source_target_pairs={{0,4},{2,6},{4,0},{6,2},{8,12},{10,14},{12,8},{14,10},{16,20},{18,... | collective-permute-start | bytes 786440 | tf_op jit(solution)/shard_map/ppermute | solution.py:26
  28.5 2.0 %pad_maximum_fusion.9 = bf16[4,64,2048]{2,1,0:T(8,128)(2,1)} fusion(bf16[1,64,2048]{2,1,0:T(8,128)(2,1)S(1)} %bitcast.182, bf16[1,64,2048]{2,1,0:T(8,128)(2,1)S(1)} %bitcast.181, bf16[1,64,2048]{2,1,0:T(8,128)(2,1)S(1)} %bitcast.180, bf16[1,64,2048]{2,1,0:T(8,128)(2,1)} %bitcast.179), kind=kLoop, calls=%fused_computation.111 | loop fusion | flops 1572864 | bytes 2097152 | tf_op jit(solution)/shard_map/stack | solution.py:488
  30.5 4.7 %collective-permute-done.53.refs_3_ = bf16[64,2048]{1,0:T(8,128)(2,1)S(1)} collective-permute-done((bf16[64,2048]{1,0:T(8,128)(2,1)S(1)}, bf16[64,2048]{1,0:T(8,128)(2,1)S(1)}, u32[]{:S(2)}, u32[]{:S(2)}) %collective-permute-start.53) | collective-permute-done | bytes 262176 | tf_op jit(solution)/shard_map/ppermute | solution.py:26
  35.3 3.7 %shard_map.131 = (bf16[8,128,128]{2,1,0:T(8,128)(2,1)S(1)}, bf16[2,128,24]{2,1,0:T(8,128)(2,1)S(1)}, f32[128,2]{1,0:T(8,128)S(1)}) custom-call(s32[7]{0:T(128)S(1)} %stack.187.info, bf16[128,1024]{1,0:T(8,128)(2,1)S(1)} %bitcast.189, bf16[128,1024]{1,0:T(8,128)(2,1)S(1)} %bitcast.184, bf16[128,1024]{1,0:T(8,128)(2,1)S(1)} %bitcast.185, ...), custom_call_target="tpu_custom_call" | custom-call | flops 2147483648 | bytes 1572864 | tf_op jit(solution)/shard_map/pallas_call | solution.py:461
  39.0 0.6 copy-done.5
  39.7 0.5 collective-permute-start.55
  40.2 0.8 pad_maximum_fusion.11
  41.1 5.0 %collective-permute-done.55.refs_7_ = bf16[64,2048]{1,0:T(8,128)(2,1)S(1)} collective-permute-done((bf16[64,2048]{1,0:T(8,128)(2,1)S(1)}, bf16[64,2048]{1,0:T(8,128)(2,1)S(1)}, u32[]{:S(2)}, u32[]{:S(2)}) %collective-permute-start.55) | collective-permute-done | bytes 262176 | tf_op jit(solution)/shard_map/ppermute | solution.py:26
  46.0 0.8 pad_maximum_fusion.12
  46.9 2.2 %collective-permute-done.58.refs_10_ = bf16[2,64,2048]{2,1,0:T(8,128)(2,1)} collective-permute-done((bf16[2,64,2048]{2,1,0:T(8,128)(2,1)}, bf16[2,64,2048]{2,1,0:T(8,128)(2,1)}, u32[]{:S(2)}, u32[]{:S(2)}) %collective-permute-start.58) | collective-permute-done | bytes 524320 | tf_op jit(solution)/shard_map/ppermute | solution.py:26
  49.2 1.0 copy-done.1
  50.2 3.1 %shard_map.132 = (bf16[128,2048]{1,0:T(8,128)(2,1)}, bf16[24,2048]{1,0:T(8,128)(2,1)}, bf16[24,2048]{1,0:T(8,128)(2,1)}, bf16[24,2048]{1,0:T(8,128)(2,1)}) custom-call(s32[3]{0:T(128)S(1)} %add_convert_fusion.same.flags, bf16[8,128,128]{2,1,0:T(8,128)(2,1)S(1)} %get-tuple-element.285.attended, bf16[128,2048]{1,0:T(8,128)(2,1)S(1)} %bitcast.183, ...), custom_call_target="tpu_custom_call" | custom-call | flops 536870912 | bytes 4194304 | tf_op jit(solution)/shard_map/pallas_call | solution.py:510
  53.3 0.6 broadcast_in_dim.17.clone
  54.0 0.6 broadcast_in_dim.17.clone.1
  54.6 0.6 broadcast_in_dim.17.clone.2
  55.3 66.6 %while.26 = (s32[]{:T(128)}, bf16[24,2048]{1,0:T(8,128)(2,1)}, bf16[24,2048]{1,0:T(8,128)(2,1)}, s32[]{:T(128)}, s32[]{:T(128)}, /*index=5*/bf16[24,2048]{1,0:T(...) while((s32[]{:T(128)}, bf16[24,2048]{1,0:T(8,128)(2,1)}, ...), condition=%wide.region_7.8_spmd, body=%wide.region_0.7_spmd.sunk | while | flops 3330932736 | bytes 74515440 | solution.py:583
  55.3 28.2 %conditional.4 = (bf16[384,2048]{1,0:T(8,128)(2,1)S(1)}, bf16[2,704,2048]{2,1,0:T(8,128)(2,1)}, bf16[704,2048]{1,0:T(8,128)(2,1)}) conditional(s32[]{:T(128)} %get-tuple-element.531, (bf16[24,2048]{1,0:T(8,128)(2,1)}, bf16[24,2048]{1,0:T(8,128)(2,1)}, bf16[2,704,2048]{2,1,0:T(8,128)(2,1)}, ...), branch_computations={%region_1.1_spmd, %region_2.2_spmd, %region_3.3_spmd} | conditional | flops 6684672 | bytes 51118464 | solution.py:553
  55.3 0.1 collective-permute-start.7
  55.4 0.4 collective-permute-start.8
  55.8 0.3 collective-permute-start
  56.1 2.5 %collective-permute-start.2 = (bf16[24,2048]{1,0:T(8,128)(2,1)}, bf16[24,2048]{1,0:T(8,128)(2,1)S(1)}, u32[]{:S(2)}, u32[]{:S(2)}) collective-permute-start(bf16[24,2048]{1,0:T(8,128)(2,1)} %get-tuple-element.196), channel_id=1, source_target_pairs={{0,24},{2,26},{4,28},{6,30},{8,16},{10,18},{12,20},{14,22},{16,8},... | collective-permute-start | bytes 294920 | tf_op jit(solution)/shard_map/while/body/cond/branch_0_fun/ppermute | solution.py:26
  58.6 0.7 collective-permute-start.1
  59.3 0.9 constant_dynamic-update-slice_fusion.3
  60.2 5.7 %collective-permute-done = bf16[24,2048]{1,0:T(8,128)(2,1)S(1)} collective-permute-done((bf16[24,2048]{1,0:T(8,128)(2,1)}, bf16[24,2048]{1,0:T(8,128)(2,1)S(1)}, u32[]{:S(2)}, u32[]{:S(2)}) %collective-permute-start) | collective-permute-done | bytes 98336 | tf_op jit(solution)/shard_map/while/body/cond/branch_0_fun/ppermute | solution.py:26
  65.9 1.2 collective-permute-done.1
  67.3 0.6 collective-permute-start.3
  67.9 5.6 %collective-permute-done.3 = bf16[96,1024]{1,0:T(8,128)(2,1)S(1)} collective-permute-done((bf16[96,1024]{1,0:T(8,128)(2,1)S(1)}, bf16[96,1024]{1,0:T(8,128)(2,1)S(1)}, u32[]{:S(2)}, u32[]{:S(2)}) %collective-permute-start.3) | collective-permute-done | bytes 196640 | tf_op jit(solution)/shard_map/while/body/cond/branch_0_fun/ppermute | solution.py:26
  73.8 1.6 %collective-permute-start.6 = (bf16[2,96,1024]{2,1,0:T(8,128)(2,1)S(1)}, bf16[2,96,1024]{2,1,0:T(8,128)(2,1)S(1)}, u32[]{:S(2)}, u32[]{:S(2)}) collective-permute-start(bf16[2,96,1024]{2,1,0:T(8,128)(2,1)S(1)} %get-tuple-element.341), channel_id=1, source_target_pairs={{0,4},{2,6},{4,0},{6,2},{8,12},{10,14},{12,8},{14,10},{16,20},{18,... | collective-permute-start | bytes 1179656 | tf_op jit(solution)/shard_map/while/body/cond/branch_0_fun/ppermute | solution.py:26
  75.4 7.7 %collective-permute-done.4 = bf16[2,96,1024]{2,1,0:T(8,128)(2,1)S(1)} collective-permute-done((bf16[2,96,1024]{2,1,0:T(8,128)(2,1)S(1)}, bf16[2,96,1024]{2,1,0:T(8,128)(2,1)S(1)}, u32[]{:S(2)}, u32[]{:S(2)}) %collective-permute-start.4) | collective-permute-done | bytes 393248 | tf_op jit(solution)/shard_map/while/body/cond/branch_0_fun/ppermute | solution.py:26
  83.1 0.2 collective-permute-done.6
  83.2 0.1 maximum_maximum_fusion
  83.5 7.2 %body.3 = bf16[384,2048]{1,0:T(8,128)(2,1)S(1)} custom-call(s32[1]{0:T(128)} %bitcast.173.other, bf16[384,2048]{1,0:T(8,128)(2,1)S(1)} %get-tuple-element.467.rows, bf16[2,704,2048]{2,1,0:T(8,128)(2,1)} %get-tuple-element.529.gate_up_near, bf16[2,704,2048]{2,1,0:T(8,128)(2,1)} %get-tuple-element.468.gate_up_far, bf16[704,2048]{1,0:T(8,128)(2,1)} %bitcast.206, ...), custom_call_target="tpu_custom_call" | custom-call | flops 3321888768 | bytes 8650752 | tf_op jit(solution)/shard_map/while/body/pallas_call | solution.py:556
  90.7 27.0 %conditional.5 = (bf16[24,2048]{1,0:T(8,128)(2,1)S(1)}, bf16[24,2048]{1,0:T(8,128)(2,1)S(1)}) conditional(s32[]{:T(128)} %get-tuple-element.531, (s32[]{:T(128)}, bf16[384,2048]{1,0:T(8,128)(2,1)S(1)}, s32[]{:T(128)}) %tuple.91, (s32[]{:T(128)}, bf16[384,2048]{1,0:T(8,128)(2,1)S(1)}, s32[]{:T(128)}) %tuple.91, (s32[]{:T(128)}, ...), branch_computations={%region_4.4_spmd, %region_5.5_spmd, %region_6.6_spmd} | conditional | flops 2359302 | bytes 13173099 | solution.py:576
  90.8 1.4 %collective-permute-start.29 = (bf16[2,96,1024]{2,1,0:T(8,128)(2,1)S(1)}, bf16[2,96,1024]{2,1,0:T(8,128)(2,1)S(1)}, u32[]{:S(2)}, u32[]{:S(2)}) collective-permute-start(bf16[2,96,1024]{2,1,0:T(8,128)(2,1)S(1)} %slice_bitcast_fusion.6), channel_id=1, source_target_pairs={{0,4},{2,6},{4,0},{6,2},{8,12},{10,14},{12,8},{14,10},{16,20},{18,... | collective-permute-start | bytes 1179656 | tf_op jit(solution)/shard_map/while/body/cond/branch_0_fun/ppermute | solution.py:26
  92.2 1.0 collective-permute-start.27
  93.2 6.1 %collective-permute-done.29 = bf16[2,96,1024]{2,1,0:T(8,128)(2,1)S(1)} collective-permute-done((bf16[2,96,1024]{2,1,0:T(8,128)(2,1)S(1)}, bf16[2,96,1024]{2,1,0:T(8,128)(2,1)S(1)}, u32[]{:S(2)}, u32[]{:S(2)}) %collective-permute-start.29) | collective-permute-done | bytes 393248 | tf_op jit(solution)/shard_map/while/body/cond/branch_0_fun/ppermute | solution.py:26
  99.3 1.9 %collective-permute-start.30 = (bf16[96,1024]{1,0:T(8,128)(2,1)S(1)}, bf16[96,1024]{1,0:T(8,128)(2,1)S(1)}, u32[]{:S(2)}, u32[]{:S(2)}) collective-permute-start(bf16[96,1024]{1,0:T(8,128)(2,1)S(1)} %slice_bitcast_fusion.10), channel_id=1, source_target_pairs={{0,1},{1,0},{2,3},{3,2},{4,5},{5,4},{6,7},{7,6},{8,9},{9,8},{10,11... | collective-permute-start | bytes 589832 | tf_op jit(solution)/shard_map/while/body/cond/branch_0_fun/ppermute | solution.py:26
  101.2 0.7 collective-permute-done.27
  101.9 0.1 fusion.6
  102.1 0.9 collective-permute-start.28
  102.9 2.1 %collective-permute-done.30 = bf16[96,1024]{1,0:T(8,128)(2,1)S(1)} collective-permute-done((bf16[96,1024]{1,0:T(8,128)(2,1)S(1)}, bf16[96,1024]{1,0:T(8,128)(2,1)S(1)}, u32[]{:S(2)}, u32[]{:S(2)}) %collective-permute-start.30) | collective-permute-done | bytes 196640 | tf_op jit(solution)/shard_map/while/body/cond/branch_0_fun/ppermute | solution.py:26
  105.1 2.7 %collective-permute-done.28 = bf16[96,1024]{1,0:T(8,128)(2,1)S(1)} collective-permute-done((bf16[96,1024]{1,0:T(8,128)(2,1)S(1)}, bf16[96,1024]{1,0:T(8,128)(2,1)S(1)}, u32[]{:S(2)}, u32[]{:S(2)}) %collective-permute-start.28) | collective-permute-done | bytes 196640 | tf_op jit(solution)/shard_map/while/body/cond/branch_0_fun/ppermute | solution.py:26
  107.9 1.8 %collective-permute-start.32 = (bf16[24,2048]{1,0:T(8,128)(2,1)S(1)}, bf16[24,2048]{1,0:T(8,128)(2,1)S(1)}, u32[]{:S(2)}, u32[]{:S(2)}) collective-permute-start(bf16[24,2048]{1,0:T(8,128)(2,1)S(1)} %get-tuple-element.212), channel_id=1, source_target_pairs={{0,16},{2,18},{4,20},{6,22},{8,24},{10,26},{12,28},{14,30},{16,0},... | collective-permute-start | bytes 294920 | tf_op jit(solution)/shard_map/while/body/cond/branch_0_fun/ppermute | solution.py:26
  109.6 3.3 %collective-permute-start.33 = (bf16[24,2048]{1,0:T(8,128)(2,1)S(1)}, bf16[24,2048]{1,0:T(8,128)(2,1)S(1)}, u32[]{:S(2)}, u32[]{:S(2)}) collective-permute-start(bf16[24,2048]{1,0:T(8,128)(2,1)S(1)} %get-tuple-element.213), channel_id=1, source_target_pairs={{0,24},{2,26},{4,28},{6,30},{8,16},{10,18},{12,20},{14,22},{16,8},... | collective-permute-start | bytes 294920 | tf_op jit(solution)/shard_map/while/body/cond/branch_0_fun/ppermute | solution.py:26
  112.9 0.5 collective-permute-done.32
  113.4 3.2 %collective-permute-done.33 = bf16[24,2048]{1,0:T(8,128)(2,1)S(1)} collective-permute-done((bf16[24,2048]{1,0:T(8,128)(2,1)S(1)}, bf16[24,2048]{1,0:T(8,128)(2,1)S(1)}, u32[]{:S(2)}, u32[]{:S(2)}) %collective-permute-start.33) | collective-permute-done | bytes 98336 | tf_op jit(solution)/shard_map/while/body/cond/branch_0_fun/ppermute | solution.py:26
  116.7 1.0 collective-permute-done.31
  117.7 0.6 copy.88
  118.4 1.5 %copy.89 = bf16[24,2048]{1,0:T(8,128)(2,1)} copy(bf16[24,2048]{1,0:T(8,128)(2,1)} %get-tuple-element.509) | data formatting | bytes 196608 | tf_op jit(solution)/shard_map/while
  119.9 0.6 copy.87
  120.5 0.6 copy.82
  121.2 0.6 copy.83
  121.8 2.2 %shard_map.133 = bf16[128,2048]{1,0:T(8,128)(2,1)} custom-call(s32[3]{0:T(128)S(1)} %add_convert_fusion.same.flags, bf16[24,2048]{1,0:T(8,128)(2,1)S(1)} %get-tuple-element.299.own, bf16[24,2048]{1,0:T(8,128)(2,1)} %get-tuple-element.300.other, bf16[24,2048]{1,0:T(8,128)(2,1)} %get-tuple-element.301.last_own, ...), custom_call_target="tpu_custom_call" | custom-call | tf_op jit(solution)/shard_map/pallas_call | solution.py:584
  (57 shorter events, 1.0 us)
Async XLA Ops:
  0.6 34.6 %copy-start.2 = (bf16[1,128,1024]{2,1,0:T(8,128)(2,1)S(1)}, bf16[1,128,1024]{2,1,0:T(8,128)(2,1)}, u32[]{:S(2)}) copy-start(bf16[1,128,1024]{2,1,0:T(8,128)(2,1)} %param.21) | copy-start | bytes 786436
  0.6 34.6 %copy-start.3 = (bf16[1,128,1024]{2,1,0:T(8,128)(2,1)S(1)}, bf16[1,128,1024]{2,1,0:T(8,128)(2,1)}, u32[]{:S(2)}) copy-start(bf16[1,128,1024]{2,1,0:T(8,128)(2,1)} %param.22) | copy-start | bytes 786436
  0.6 25.3 %collective-permute-start.48 = (bf16[64,2048]{1,0:T(8,128)(2,1)}, bf16[64,2048]{1,0:T(8,128)(2,1)S(1)}, u32[]{:S(2)}, u32[]{:S(2)}) collective-permute-start(bf16[64,2048]{1,0:T(8,128)(2,1)} %refs_0_.1), channel_id=1, source_target_pairs={{0,8},{2,10},{4,12},{6,14},{8,0},{10,2},{12,4},{14,6},{16,24},{18,... | collective-permute-start | bytes 786440 | tf_op jit(solution)/shard_map/ppermute | solution.py:26
  3.7 22.2 %collective-permute-start.49 = (bf16[64,2048]{1,0:T(8,128)(2,1)}, bf16[64,2048]{1,0:T(8,128)(2,1)S(1)}, u32[]{:S(2)}, u32[]{:S(2)}) collective-permute-start(bf16[64,2048]{1,0:T(8,128)(2,1)} %refs_0_.1), channel_id=1, source_target_pairs={{0,4},{2,6},{4,0},{6,2},{8,12},{10,14},{12,8},{14,10},{16,20},{18,... | collective-permute-start | bytes 786440 | tf_op jit(solution)/shard_map/ppermute | solution.py:26
  5.2 20.7 %collective-permute-start.50 = (bf16[64,2048]{1,0:T(8,128)(2,1)}, bf16[64,2048]{1,0:T(8,128)(2,1)S(1)}, u32[]{:S(2)}, u32[]{:S(2)}) collective-permute-start(bf16[64,2048]{1,0:T(8,128)(2,1)} %refs_0_.1), channel_id=1, source_target_pairs={{0,16},{2,18},{4,20},{6,22},{8,24},{10,26},{12,28},{14,30},{16,0},... | collective-permute-start | bytes 786440 | tf_op jit(solution)/shard_map/ppermute | solution.py:26
  9.7 25.6 %collective-permute-start.52 = (bf16[2,128,1024]{2,1,0:T(8,128)(2,1)}, bf16[2,128,1024]{2,1,0:T(8,128)(2,1)}, u32[]{:S(2)}, u32[]{:S(2)}) collective-permute-start(bf16[2,128,1024]{2,1,0:T(8,128)(2,1)} %pad_maximum_fusion.10), channel_id=1, source_target_pairs={{0,1},{2,3},{4,5},{6,7},{8,9},{10,11},{12,13},{14,15},{16,17},{18,... | collective-permute-start | bytes 1572872 | tf_op jit(solution)/shard_map/ppermute | solution.py:422
  25.9 9.4 %copy-start.4 = (f32[1,128,6]{2,1,0:T(8,128)S(1)}, f32[1,128,6]{2,1,0:T(8,128)}, u32[]{:S(2)}) copy-start(f32[1,128,6]{2,1,0:T(8,128)} %copy.35) | copy-start | bytes 9220
  25.9 9.4 %copy-start.8 = (bf16[1,128,1024]{2,1,0:T(8,128)(2,1)S(1)}, bf16[1,128,1024]{2,1,0:T(8,128)(2,1)}, u32[]{:S(2)}) copy-start(bf16[1,128,1024]{2,1,0:T(8,128)(2,1)} %param.20) | copy-start | bytes 786436
  26.0 9.3 %collective-permute-start.53 = (bf16[64,2048]{1,0:T(8,128)(2,1)S(1)}, bf16[64,2048]{1,0:T(8,128)(2,1)S(1)}, u32[]{:S(2)}, u32[]{:S(2)}) collective-permute-start(bf16[64,2048]{1,0:T(8,128)(2,1)S(1)} %collective-permute-done.48.refs_2_), channel_id=1, source_target_pairs={{0,4},{2,6},{4,0},{6,2},{8,12},{10,14},{12,8},{14,10},{16,20},{18,... | collective-permute-start | bytes 786440 | tf_op jit(solution)/shard_map/ppermute | solution.py:26
  26.6 13.1 %collective-permute-start.51 = (bf16[64,2048]{1,0:T(8,128)(2,1)S(1)}, bf16[64,2048]{1,0:T(8,128)(2,1)S(1)}, u32[]{:S(2)}, u32[]{:S(2)}) collective-permute-start(bf16[64,2048]{1,0:T(8,128)(2,1)S(1)} %collective-permute-done.50.refs_4_), channel_id=1, source_target_pairs={{0,8},{2,10},{4,12},{6,14},{8,0},{10,2},{12,4},{14,6},{16,24},{18,... | collective-permute-start | bytes 786440 | tf_op jit(solution)/shard_map/ppermute | solution.py:26
  27.0 14.1 %collective-permute-start.54 = (bf16[64,2048]{1,0:T(8,128)(2,1)S(1)}, bf16[64,2048]{1,0:T(8,128)(2,1)S(1)}, u32[]{:S(2)}, u32[]{:S(2)}) collective-permute-start(bf16[64,2048]{1,0:T(8,128)(2,1)S(1)} %collective-permute-done.50.refs_4_), channel_id=1, source_target_pairs={{0,4},{2,6},{4,0},{6,2},{8,12},{10,14},{12,8},{14,10},{16,20},{18,... | collective-permute-start | bytes 786440 | tf_op jit(solution)/shard_map/ppermute | solution.py:26
  30.5 18.6 %collective-permute-start.56 = (bf16[4,64,2048]{2,1,0:T(8,128)(2,1)}, bf16[4,64,2048]{2,1,0:T(8,128)(2,1)S(1)}, u32[]{:S(2)}, u32[]{:S(2)}) collective-permute-start(bf16[4,64,2048]{2,1,0:T(8,128)(2,1)} %pad_maximum_fusion.9), channel_id=1, source_target_pairs={{0,2},{2,0},{4,6},{6,4},{8,10},{10,8},{12,14},{14,12},{16,18},{18,... | collective-permute-start | bytes 3145736 | tf_op jit(solution)/shard_map/ppermute | solution.py:26
  39.0 0.6 copy-start.5
  39.7 9.5 %copy-start = (bf16[64,2048]{1,0:T(8,128)(2,1)S(1)}, bf16[64,2048]{1,0:T(8,128)(2,1)}, u32[]{:S(2)}) copy-start(bf16[64,2048]{1,0:T(8,128)(2,1)} %refs_0_.1) | copy-start | bytes 786436
  39.7 9.5 %copy-start.7 = (f32[2048]{0:T(1024)S(1)}, f32[2048]{0:T(1024)}, u32[]{:S(2)}) copy-start(f32[2048]{0:T(1024)} %param.25) | copy-start | bytes 24580
  39.7 6.4 %collective-permute-start.55 = (bf16[64,2048]{1,0:T(8,128)(2,1)S(1)}, bf16[64,2048]{1,0:T(8,128)(2,1)S(1)}, u32[]{:S(2)}, u32[]{:S(2)}) collective-permute-start(bf16[64,2048]{1,0:T(8,128)(2,1)S(1)} %collective-permute-done.51.refs_6_), channel_id=1, source_target_pairs={{0,4},{2,6},{4,0},{6,2},{8,12},{10,14},{12,8},{14,10},{16,20},{18,... | collective-permute-start | bytes 786440 | tf_op jit(solution)/shard_map/ppermute | solution.py:26
  41.1 5.8 %collective-permute-start.57 = (bf16[2,64,2048]{2,1,0:T(8,128)(2,1)}, bf16[2,64,2048]{2,1,0:T(8,128)(2,1)}, u32[]{:S(2)}, u32[]{:S(2)}) collective-permute-start(bf16[2,64,2048]{2,1,0:T(8,128)(2,1)} %pad_maximum_fusion.11), channel_id=1, source_target_pairs={{0,2},{2,0},{4,6},{6,4},{8,10},{10,8},{12,14},{14,12},{16,18},{18,... | collective-permute-start | bytes 1572872 | tf_op jit(solution)/shard_map/ppermute | solution.py:26
  46.9 2.3 %collective-permute-start.58 = (bf16[2,64,2048]{2,1,0:T(8,128)(2,1)}, bf16[2,64,2048]{2,1,0:T(8,128)(2,1)}, u32[]{:S(2)}, u32[]{:S(2)}) collective-permute-start(bf16[2,64,2048]{2,1,0:T(8,128)(2,1)} %pad_maximum_fusion.12), channel_id=1, source_target_pairs={{0,2},{2,0},{4,6},{6,4},{8,10},{10,8},{12,14},{14,12},{16,18},{18,... | collective-permute-start | bytes 1572872 | tf_op jit(solution)/shard_map/ppermute | solution.py:26
  49.2 1.0 copy-start.1
  55.3 66.6 %copy-start.6 = (f32[128,2]{1,0:T(8,128)S(1)}, f32[128,2]{1,0:T(8,128)}, u32[]{:S(2)}) copy-start(f32[128,2]{1,0:T(8,128)} %copy-done.5) | copy-start | bytes 3076
  55.3 28.2 %collective-permute-start.7 = (bf16[2,704,2048]{2,1,0:T(8,128)(2,1)}, bf16[2,704,2048]{2,1,0:T(8,128)(2,1)}, u32[]{:S(2)}, u32[]{:S(2)}) collective-permute-start(bf16[2,704,2048]{2,1,0:T(8,128)(2,1)} %get-tuple-element.197), channel_id=1, source_target_pairs={{0,2},{2,0},{4,6},{6,4},{8,10},{10,8},{12,14},{14,12},{16,18},{18,... | collective-permute-start | bytes 17301512 | tf_op jit(solution)/shard_map/while/body/cond/branch_0_fun/ppermute | solution.py:26
  55.4 28.1 %collective-permute-start.8 = (bf16[704,2048]{1,0:T(8,128)(2,1)}, bf16[704,2048]{1,0:T(8,128)(2,1)}, u32[]{:S(2)}, u32[]{:S(2)}) collective-permute-start(bf16[704,2048]{1,0:T(8,128)(2,1)} %bitcast.207), channel_id=1, source_target_pairs={{0,2},{2,0},{4,6},{6,4},{8,10},{10,8},{12,14},{14,12},{16,18},{18,... | collective-permute-start | bytes 8650760 | tf_op jit(solution)/shard_map/while/body/cond/branch_0_fun/ppermute | solution.py:26
  55.8 10.2 %collective-permute-start = (bf16[24,2048]{1,0:T(8,128)(2,1)}, bf16[24,2048]{1,0:T(8,128)(2,1)S(1)}, u32[]{:S(2)}, u32[]{:S(2)}) collective-permute-start(bf16[24,2048]{1,0:T(8,128)(2,1)} %get-tuple-element.196), channel_id=1, source_target_pairs={{0,16},{2,18},{4,20},{6,22},{8,24},{10,26},{12,28},{14,30},{16,0},... | collective-permute-start | bytes 294920 | tf_op jit(solution)/shard_map/while/body/cond/branch_0_fun/ppermute | solution.py:26
  56.1 11.1 %collective-permute-start.2 = (bf16[24,2048]{1,0:T(8,128)(2,1)}, bf16[24,2048]{1,0:T(8,128)(2,1)S(1)}, u32[]{:S(2)}, u32[]{:S(2)}) collective-permute-start(bf16[24,2048]{1,0:T(8,128)(2,1)} %get-tuple-element.196), channel_id=1, source_target_pairs={{0,24},{2,26},{4,28},{6,30},{8,16},{10,18},{12,20},{14,22},{16,8},... | collective-permute-start | bytes 294920 | tf_op jit(solution)/shard_map/while/body/cond/branch_0_fun/ppermute | solution.py:26
  58.6 8.6 %collective-permute-start.1 = (bf16[24,2048]{1,0:T(8,128)(2,1)}, bf16[24,2048]{1,0:T(8,128)(2,1)S(1)}, u32[]{:S(2)}, u32[]{:S(2)}) collective-permute-start(bf16[24,2048]{1,0:T(8,128)(2,1)} %get-tuple-element.195), channel_id=1, source_target_pairs={{0,8},{2,10},{4,12},{6,14},{8,0},{10,2},{12,4},{14,6},{16,24},{18,... | collective-permute-start | bytes 294920 | tf_op jit(solution)/shard_map/while/body/cond/branch_0_fun/ppermute | solution.py:26
  67.3 6.2 %collective-permute-start.3 = (bf16[96,1024]{1,0:T(8,128)(2,1)S(1)}, bf16[96,1024]{1,0:T(8,128)(2,1)S(1)}, u32[]{:S(2)}, u32[]{:S(2)}) collective-permute-start(bf16[96,1024]{1,0:T(8,128)(2,1)S(1)} %get-tuple-element.339), channel_id=1, source_target_pairs={{0,4},{2,6},{4,0},{6,2},{8,12},{10,14},{12,8},{14,10},{16,20},{18,... | collective-permute-start | bytes 589832 | tf_op jit(solution)/shard_map/while/body/cond/branch_0_fun/ppermute | solution.py:26
  67.9 5.9 %collective-permute-start.5 = (bf16[96,1024]{1,0:T(8,128)(2,1)S(1)}, bf16[96,1024]{1,0:T(8,128)(2,1)S(1)}, u32[]{:S(2)}, u32[]{:S(2)}) collective-permute-start(bf16[96,1024]{1,0:T(8,128)(2,1)S(1)} %get-tuple-element.338), channel_id=1, source_target_pairs={{0,1},{1,0},{2,3},{3,2},{4,5},{5,4},{6,7},{7,6},{8,9},{9,8},{10,11... | collective-permute-start | bytes 589832 | tf_op jit(solution)/shard_map/while/body/cond/branch_0_fun/ppermute | solution.py:26
  73.6 9.5 %collective-permute-start.4 = (bf16[2,96,1024]{2,1,0:T(8,128)(2,1)S(1)}, bf16[2,96,1024]{2,1,0:T(8,128)(2,1)S(1)}, u32[]{:S(2)}, u32[]{:S(2)}) collective-permute-start(bf16[2,96,1024]{2,1,0:T(8,128)(2,1)S(1)} %get-tuple-element.335), channel_id=1, source_target_pairs={{0,1},{1,0},{2,3},{3,2},{4,5},{5,4},{6,7},{7,6},{8,9},{9,8},{10,11... | collective-permute-start | bytes 1179656 | tf_op jit(solution)/shard_map/while/body/cond/branch_0_fun/ppermute | solution.py:26
  73.8 9.4 %collective-permute-start.6 = (bf16[2,96,1024]{2,1,0:T(8,128)(2,1)S(1)}, bf16[2,96,1024]{2,1,0:T(8,128)(2,1)S(1)}, u32[]{:S(2)}, u32[]{:S(2)}) collective-permute-start(bf16[2,96,1024]{2,1,0:T(8,128)(2,1)S(1)} %get-tuple-element.341), channel_id=1, source_target_pairs={{0,4},{2,6},{4,0},{6,2},{8,12},{10,14},{12,8},{14,10},{16,20},{18,... | collective-permute-start | bytes 1179656 | tf_op jit(solution)/shard_map/while/body/cond/branch_0_fun/ppermute | solution.py:26
  90.7 29.8 %copy-start.9 = (bf16[24,2048]{1,0:T(8,128)(2,1)S(1)}, bf16[24,2048]{1,0:T(8,128)(2,1)}, u32[]{:S(2)}) copy-start(bf16[24,2048]{1,0:T(8,128)(2,1)} %get-tuple-element.532) | copy-start | bytes 294916 | tf_op jit(solution)/shard_map/while
  90.8 8.5 %collective-permute-start.29 = (bf16[2,96,1024]{2,1,0:T(8,128)(2,1)S(1)}, bf16[2,96,1024]{2,1,0:T(8,128)(2,1)S(1)}, u32[]{:S(2)}, u32[]{:S(2)}) collective-permute-start(bf16[2,96,1024]{2,1,0:T(8,128)(2,1)S(1)} %slice_bitcast_fusion.6), channel_id=1, source_target_pairs={{0,4},{2,6},{4,0},{6,2},{8,12},{10,14},{12,8},{14,10},{16,20},{18,... | collective-permute-start | bytes 1179656 | tf_op jit(solution)/shard_map/while/body/cond/branch_0_fun/ppermute | solution.py:26
  92.2 9.7 %collective-permute-start.27 = (bf16[2,96,1024]{2,1,0:T(8,128)(2,1)S(1)}, bf16[2,96,1024]{2,1,0:T(8,128)(2,1)S(1)}, u32[]{:S(2)}, u32[]{:S(2)}) collective-permute-start(bf16[2,96,1024]{2,1,0:T(8,128)(2,1)S(1)} %slice_bitcast_fusion.8), channel_id=1, source_target_pairs={{0,1},{1,0},{2,3},{3,2},{4,5},{5,4},{6,7},{7,6},{8,9},{9,8},{10,11... | collective-permute-start | bytes 1179656 | tf_op jit(solution)/shard_map/while/body/cond/branch_0_fun/ppermute | solution.py:26
  99.3 5.7 %collective-permute-start.30 = (bf16[96,1024]{1,0:T(8,128)(2,1)S(1)}, bf16[96,1024]{1,0:T(8,128)(2,1)S(1)}, u32[]{:S(2)}, u32[]{:S(2)}) collective-permute-start(bf16[96,1024]{1,0:T(8,128)(2,1)S(1)} %slice_bitcast_fusion.10), channel_id=1, source_target_pairs={{0,1},{1,0},{2,3},{3,2},{4,5},{5,4},{6,7},{7,6},{8,9},{9,8},{10,11... | collective-permute-start | bytes 589832 | tf_op jit(solution)/shard_map/while/body/cond/branch_0_fun/ppermute | solution.py:26
  102.1 5.7 %collective-permute-start.28 = (bf16[96,1024]{1,0:T(8,128)(2,1)S(1)}, bf16[96,1024]{1,0:T(8,128)(2,1)S(1)}, u32[]{:S(2)}, u32[]{:S(2)}) collective-permute-start(bf16[96,1024]{1,0:T(8,128)(2,1)S(1)} %slice_bitcast_fusion.12), channel_id=1, source_target_pairs={{0,4},{2,6},{4,0},{6,2},{8,12},{10,14},{12,8},{14,10},{16,20},{18,... | collective-permute-start | bytes 589832 | tf_op jit(solution)/shard_map/while/body/cond/branch_0_fun/ppermute | solution.py:26
  107.9 5.6 %collective-permute-start.32 = (bf16[24,2048]{1,0:T(8,128)(2,1)S(1)}, bf16[24,2048]{1,0:T(8,128)(2,1)S(1)}, u32[]{:S(2)}, u32[]{:S(2)}) collective-permute-start(bf16[24,2048]{1,0:T(8,128)(2,1)S(1)} %get-tuple-element.212), channel_id=1, source_target_pairs={{0,16},{2,18},{4,20},{6,22},{8,24},{10,26},{12,28},{14,30},{16,0},... | collective-permute-start | bytes 294920 | tf_op jit(solution)/shard_map/while/body/cond/branch_0_fun/ppermute | solution.py:26
  109.6 7.0 %collective-permute-start.33 = (bf16[24,2048]{1,0:T(8,128)(2,1)S(1)}, bf16[24,2048]{1,0:T(8,128)(2,1)S(1)}, u32[]{:S(2)}, u32[]{:S(2)}) collective-permute-start(bf16[24,2048]{1,0:T(8,128)(2,1)S(1)} %get-tuple-element.213), channel_id=1, source_target_pairs={{0,24},{2,26},{4,28},{6,30},{8,16},{10,18},{12,20},{14,22},{16,8},... | collective-permute-start | bytes 294920 | tf_op jit(solution)/shard_map/while/body/cond/branch_0_fun/ppermute | solution.py:26
  112.9 4.8 %collective-permute-start.31 = (bf16[24,2048]{1,0:T(8,128)(2,1)S(1)}, bf16[24,2048]{1,0:T(8,128)(2,1)S(1)}, u32[]{:S(2)}, u32[]{:S(2)}) collective-permute-start(bf16[24,2048]{1,0:T(8,128)(2,1)S(1)} %get-tuple-element.210), channel_id=1, source_target_pairs={{0,8},{2,10},{4,12},{6,14},{8,0},{10,2},{12,4},{14,6},{16,24},{18,... | collective-permute-start | bytes 294920 | tf_op jit(solution)/shard_map/while/body/cond/branch_0_fun/ppermute | solution.py:26

commit v4 on v2

--- a/solution.py
+++ b/solution.py
@@ -151,12 +151,63 @@
     return (attn_proj[None], expert_sum[None])
 
 
-def attend_kernel(info, query, key, value, before_both, ids, gates, attended, place, gate_values):
+CTX, CHIP, CORE, FIRST, FIRST_CAP, SECOND, SECOND_CAP, SAME = range(8)
+FIRST_HERE, SECOND_HERE, PASSES, BRANCH, PASS_INFO = range(8, 13)
+USE_FAR, NEAR_LAST, NEAR_SECOND, OTHER_NEAR, PASS_COUNT = range(5)
+
+
+def work_out_places(bits, owners, caps, info):
+    me = lax.axis_index("dp")
+    differ = owners[0] ^ owners[1]
+    branch = 0
+    split_bit = 0
+    rest = [bits[1], bits[2]]
+    for k in reversed(range(len(bits))):
+        parted = (differ & bits[k]) != 0
+        branch = jnp.where(parted, k, branch)
+        split_bit = jnp.where(parted, bits[k], split_bit)
+        others = [bit for bit in bits if bit != bits[k]]
+        rest = [jnp.where(parted, others[i], rest[i]) for i in range(2)]
+    same = split_bit == 0
+    swapped = ((me ^ owners[0]) & split_bit) != 0
+    first_offset = me ^ jnp.where(swapped, owners[1], owners[0])
+    second_offset = me ^ jnp.where(swapped, owners[0], owners[1])
+
+    def put(place, value):
+        info[place] = value.astype(jnp.int32)
+
+    put(CTX, lax.axis_index("ctx"))
+    put(CHIP, me >> 1)
+    put(CORE, me & 1)
+    put(FIRST, jnp.where(swapped, 1, 0))
+    put(FIRST_CAP, jnp.where(swapped, caps[0, 0, 1], caps[0, 0, 0]))
+    put(SECOND, jnp.where(swapped, 0, 1))
+    put(SECOND_CAP, jnp.where(swapped, caps[0, 0, 0], caps[0, 0, 1]))
+    put(SAME, jnp.where(same, 1, 0))
+    put(FIRST_HERE, jnp.where((first_offset & bits[0]) == 0, 1, 0))
+    put(SECOND_HERE, jnp.where((second_offset & bits[0]) == 0, 1, 0))
+    put(PASSES, jnp.where(same, 2, 1))
+    put(BRANCH, branch)
+    pairs = (
+        (first_offset, jnp.where(same, first_offset, second_offset)),
+        (second_offset, second_offset),
+    )
+    for k, (offset, other_offset) in enumerate(pairs):
+        base = PASS_INFO + k * PASS_COUNT
+        put(base + USE_FAR, offset & 1)
+        put(base + NEAR_LAST, jnp.where((offset & rest[1]) == 0, 1, 0))
+        put(base + NEAR_SECOND, jnp.where((offset & rest[0]) == 0, 1, 0))
+        put(base + OTHER_NEAR, jnp.where((other_offset & rest[0]) == 0, 1, 0))
+
+
+def attend_kernel(bits, owners, caps, query, key, value, before_both, ids, gates, *outs):
+    attended, select, gate_values, info = outs
+    work_out_places(bits, owners, caps, info)
     token_count = query.shape[0]
     row = lax.broadcasted_iota(jnp.int32, (token_count, token_count), 0)
     col = lax.broadcasted_iota(jnp.int32, (token_count, token_count), 1)
     own_visible = col <= row
-    before_visible = jnp.broadcast_to(info[0], (token_count, token_count)) == 1
+    before_visible = jnp.broadcast_to(info[CTX], (token_count, token_count)) == 1
     contract_last = (((1,), (1,)), ((), ()))
     for head in range(HEADS):
         span = slice(head * HD, (head + 1) * HD)
@@ -182,36 +233,32 @@
         )
         mixed = mixed / total
         swapped = pltpu.roll(mixed, HD // 2, 1)
-        mixed = jnp.where(jnp.broadcast_to(info[2], mixed.shape) == 0, mixed, swapped)
-        attended[head ^ info[1]] = mixed.astype(jnp.bfloat16)
-
-    slots = PASS_SPECIALISTS * CAP
-    lane = lax.broadcasted_iota(jnp.int32, (token_count, slots), 1)
-    routed = jnp.zeros((token_count, slots), jnp.float32)
-    limit = jnp.zeros((token_count, slots), jnp.int32)
-    for expert in range(PASS_SPECIALISTS):
-        matches = ids[...] == expert
-        named = jnp.max(matches.astype(jnp.float32), axis=1, keepdims=True)
-        gate_values[:, expert : expert + 1] = jnp.sum(
-            jnp.where(matches, gates[...], 0.0), axis=1, keepdims=True
-        )
-        mine = (lane >= expert * CAP) & (lane < (expert + 1) * CAP)
-        routed = jnp.where(mine, named, routed)
-        limit = jnp.where(mine, info[3 + expert], limit)
-    earlier = (col < row).astype(jnp.bfloat16)
-    rank = jnp.dot(
-        earlier, routed.astype(jnp.bfloat16), preferred_element_type=jnp.float32
-    ).astype(jnp.int32)
-    slot = jnp.where(lane >= CAP, lane - CAP, lane)
-    place[...] = ((routed > 0.0) & (rank == slot) & (rank < limit)).astype(jnp.bfloat16)
-
-
-def project_kernel(far_place, *refs):
-    attended, residual, gain, place = refs[:4]
-    near = refs[4 : 4 + HEADS]
-    groups = refs[4 + HEADS : -3]
-    far = [groups[group].at[k] for group, k in far_place]
-    attn_proj, chosen, combined = refs[-3:]
+        mixed = jnp.where(jnp.broadcast_to(info[CORE], mixed.shape) == 0, mixed, swapped)
+        attended[head ^ info[CHIP]] = mixed.astype(jnp.bfloat16)
+
+    slot = lax.broadcasted_iota(jnp.int32, (CAP, token_count), 0)
+    earlier = (row < col).astype(jnp.bfloat16)
+    for k in range(PASS_SPECIALISTS):
+        matches = ids[...] == info[FIRST + 2 * k]
+        named = jnp.max(matches.astype(jnp.float32), axis=0, keepdims=True)
+        gate_row = jnp.sum(jnp.where(matches, gates[...], 0.0), axis=0, keepdims=True)
+        gate_values[:, k : k + 1] = jnp.sum(
+            jnp.where(row == col, jnp.broadcast_to(gate_row, row.shape), 0.0),
+            axis=1,
+            keepdims=True,
+        )
+        routed = jnp.broadcast_to(named, (CAP, token_count))
+        rank = jnp.dot(
+            routed.astype(jnp.bfloat16), earlier, preferred_element_type=jnp.float32
+        ).astype(jnp.int32)
+        kept = (routed > 0.0) & (rank == slot) & (rank < info[FIRST_CAP + 2 * k])
+        select[k] = kept.astype(jnp.bfloat16)
+
+
+def project_kernel(info, attended, residual, gain, select, *refs):
+    near = refs[:HEADS]
+    far = refs[HEADS : 2 * HEADS]
+    attn_proj, kept, sent, second, _, _, combined = refs[-7:]
     token_count, width = residual.shape
     tile = 512
     squares = jnp.zeros((token_count, 1), jnp.float32)
@@ -235,12 +282,52 @@
     for start in range(0, width, tile):
         span = slice(start, start + tile)
         normed = (combined[:, span] * scale * gain[:, span]).astype(jnp.bfloat16)
-        chosen[:, span] = lax.dot_general(
-            place[...], normed, (((0,), (0,)), ((), ())), preferred_element_type=jnp.float32
-        ).astype(jnp.bfloat16)
-
-
-def expert_kernel(other, rows, gate_up_near, gate_up_far, down_near, down_far, made, gate_up, down, hidden, sems):
+        rows = [
+            jnp.dot(select[k], normed, preferred_element_type=jnp.float32)
+            for k in range(PASS_SPECIALISTS)
+        ]
+        kept[:, span] = rows[0].astype(jnp.bfloat16)
+        second[:, span] = rows[1].astype(jnp.bfloat16)
+        use_first = jnp.broadcast_to(info[SAME], rows[0].shape) != 0
+        sent[:, span] = jnp.where(use_first, rows[0], rows[1]).astype(jnp.bfloat16)
+
+
+def combine_kernel(info, step, own, other, last, second, select, gate_values, *outs):
+    out, next_last, next_kept, next_sent = outs
+    same = info[SAME] != 0
+    contract_first = (((0,), (0,)), ((), ()))
+
+    def add_up(first_rows, second_rows):
+        total = 0.0
+        for k, rows in enumerate((first_rows, second_rows)):
+            picked = lax.dot_general(
+                select[k], rows, contract_first, preferred_element_type=jnp.float32
+            )
+            total = total + gate_values[:, k : k + 1] * picked
+        return total.astype(jnp.bfloat16)
+
+    @pl.when(jnp.logical_not(same))
+    def _():
+        for start in range(0, own.shape[1], 512):
+            span = slice(start, start + 512)
+            out[:, span] = add_up(own[:, span], other[:, span])
+
+    @pl.when(same)
+    def _():
+        here = jnp.where(step[0] == 0, info[FIRST_HERE], info[SECOND_HERE])
+        for start in range(0, own.shape[1], 512):
+            span = slice(start, start + 512)
+            use_own = jnp.broadcast_to(here, (own.shape[0], 512)) != 0
+            served = jnp.where(
+                use_own, own[:, span].astype(jnp.float32), other[:, span].astype(jnp.float32)
+            ).astype(jnp.bfloat16)
+            out[:, span] = add_up(last[:, span], served)
+            next_last[:, span] = served
+            next_kept[:, span] = second[:, span]
+            next_sent[:, span] = second[:, span]
+
+
+def expert_kernel(info, step, rows, gate_up_near, gate_up_far, down_near, down_far, made, gate_up, down, hidden, sems):
     units = down.shape[0]
     starts = list(range(0, units, 256))
 
@@ -258,12 +345,14 @@
         out.append(pltpu.make_async_copy(down_from, down, sems.at[2 * len(starts)]))
         return out
 
-    @pl.when(other[0] == 0)
+    use_far = info[PASS_INFO + USE_FAR + PASS_COUNT * step[0]]
+
+    @pl.when(use_far == 0)
     def _():
         for copy in copies(gate_up_near, down_near):
             copy.start()
 
-    @pl.when(other[0] != 0)
+    @pl.when(use_far != 0)
     def _():
         for copy in copies(gate_up_far, down_far):
             copy.start()
@@ -313,7 +402,7 @@
     return rows.reshape(-1, rows.shape[-1])
 
 
-def scatter_rows(rows, first, bits, dp_size, offset, other_offset):
+def scatter_rows(rows, first, bits, dp_size, near_last, near_second, other_near):
     second, last = bits
     half = rows.shape[1] // 2
     rows = rows.reshape(2, 2, -1, rows.shape[1])
@@ -322,20 +411,23 @@
     def add(kept, came):
         return (kept.astype(jnp.float32) + came.astype(jnp.float32)).astype(jnp.bfloat16)
 
-    near = (offset & last) == 0
     left = add(left[0], hop(left[1], "ctx", 2, 1))
-    right = jnp.where(near, right[:, 0], hop(right[:, 1], "dp", dp_size, last))
-    left = jnp.where(near, left[0], hop(left[1], "dp", dp_size, last))
+    right = jnp.where(near_last, right[:, 0], hop(right[:, 1], "dp", dp_size, last))
+    left = jnp.where(near_last, left[0], hop(left[1], "dp", dp_size, last))
     right = add(right[0], hop(right[1], "ctx", 2, 1))
     unit = jnp.concatenate([left, right], axis=-1)
-    here, across, beside, beyond = jnp.split(unit, 4, axis=0)
+    here, across, beside, beyond = lax.optimization_barrier(jnp.split(unit, 4, axis=0))
     across = hop(across, "dp", dp_size, first)
     beside = hop(beside, "dp", dp_size, second)
     beyond = hop(beyond, "dp", dp_size, first | second)
     return (
-        jnp.where((offset & second) == 0, here, beside),
-        jnp.where((other_offset & second) == 0, across, beyond),
-    )
+        jnp.where(near_second, here, beside),
+        jnp.where(other_near, across, beyond),
+    )
+
+
+def smem(count):
+    return [pl.BlockSpec(memory_space=pltpu.SMEM)] * count
 
 
 def vmem(count):
@@ -359,105 +451,69 @@
     token_count = query_vecs.shape[1]
     width = residual.shape[2]
     dp_size = lax.axis_size("dp")
-    me = lax.axis_index("dp")
-    core = me & 1
-    ctx = lax.axis_index("ctx")
     bits = [1 << k for k in reversed(range(1, dp_size.bit_length() - 1))]
 
-    info = jnp.stack([ctx, me >> 1, core, capacity[0, 0, 0], capacity[0, 0, 1]]).astype(jnp.int32)
     before = lax.ppermute(jnp.stack([key_vecs[0], value_vecs[0]]), "ctx", [(0, 1)])
     z_far, z_near, x_bit = bits
     z_both = z_far | z_near
     near = {0: w_out}
     for bit in (z_near, x_bit, z_far):
         near[bit] = hop(w_out, "dp", dp_size, bit)
-    near[z_near], near[x_bit], info, ids, gates = lax.optimization_barrier(
-        (near[z_near], near[x_bit], info, expert_ids[0], route_gates[0])
+    near[z_near], near[x_bit], near[z_far] = lax.optimization_barrier(
+        (near[z_near], near[x_bit], near[z_far])
     )
     near[z_near | x_bit] = hop(near[z_near], "dp", dp_size, x_bit)
     near[z_both] = hop(near[z_far], "dp", dp_size, z_near)
-    next_sent, near[z_near | x_bit], before = lax.optimization_barrier(
-        (near[z_far], near[z_near | x_bit], before)
-    )
-    near[z_far | x_bit] = hop(next_sent, "dp", dp_size, x_bit)
-    slots = PASS_SPECIALISTS * CAP
-    attended, place, gate_values = pl.pallas_call(
-        attend_kernel,
+    near[z_far | x_bit] = hop(near[z_far], "dp", dp_size, x_bit)
+    before, near[z_near | x_bit] = lax.optimization_barrier((before, near[z_near | x_bit]))
+    attended, select, gate_values, info = pl.pallas_call(
+        functools.partial(attend_kernel, bits),
         out_shape=(
             jax.ShapeDtypeStruct((HEADS, token_count, HD), jnp.bfloat16),
-            jax.ShapeDtypeStruct((token_count, slots), jnp.bfloat16),
+            jax.ShapeDtypeStruct((PASS_SPECIALISTS, CAP, token_count), jnp.bfloat16),
             jax.ShapeDtypeStruct((token_count, PASS_SPECIALISTS), jnp.float32),
+            jax.ShapeDtypeStruct((PASS_INFO + 2 * PASS_COUNT,), jnp.int32),
         ),
-        in_specs=[pl.BlockSpec(memory_space=pltpu.SMEM)] + vmem(6),
-        out_specs=tuple(vmem(3)),
+        in_specs=smem(2) + vmem(6),
+        out_specs=tuple(vmem(3) + smem(1)),
         cost_estimate=pl.CostEstimate(
             flops=64 * HEADS * HD * 2 * token_count * token_count,
             bytes_accessed=6 * 2 * token_count * HEADS * HD,
             transcendentals=2 * HEADS * token_count * token_count,
         ),
-        compiler_params=pltpu.CompilerParams(vmem_limit_bytes=16 * 2**20),
+        compiler_params=pltpu.CompilerParams(vmem_limit_bytes=8 * 2**20),
     )(
-        info,
+        expert_owner,
+        capacity,
         query_vecs[0],
         key_vecs[0],
         value_vecs[0],
         before,
-        ids,
-        gates,
-    )
-    near[z_both], near[z_far | x_bit], attended = lax.optimization_barrier(
-        (near[z_both], near[z_far | x_bit], attended)
-    )
+        jnp.transpose(expert_ids[0]),
+        jnp.transpose(route_gates[0]),
+    )
+    near[z_both], attended = lax.optimization_barrier((near[z_both], attended))
     near[z_both | x_bit] = hop(near[z_both], "dp", dp_size, x_bit)
-    far = [
-        hop(jnp.stack([near[j] for j in group]), "dp", dp_size, 1)
-        for group in (
-            (0, z_near, x_bit, z_far),
-            (z_near | x_bit, z_far | x_bit, z_both),
-            (z_both | x_bit,),
-        )
-    ]
-    far_place = {
-        0: (0, 0),
-        z_near: (0, 1),
-        x_bit: (0, 2),
-        z_far: (0, 3),
-        z_near | x_bit: (1, 0),
-        z_far | x_bit: (1, 1),
-        z_both: (1, 2),
-        z_both | x_bit: (2, 0),
-    }
-    far_place = [far_place[2 * j] for j in range(HEADS)]
+    far = [hop(near[2 * j], "dp", dp_size, 1) for j in range(HEADS)]
     shares = [near[2 * j] for j in range(HEADS)] + far
     gate_up_near = jnp.swapaxes(w_gate_up[0], 1, 2)
 
-    attn_proj, chosen = pl.pallas_call(
-        functools.partial(project_kernel, far_place),
-        out_shape=(
-            jax.ShapeDtypeStruct((token_count, width), jnp.bfloat16),
-            jax.ShapeDtypeStruct((slots, width), jnp.bfloat16),
-        ),
-        in_specs=vmem(4 + len(shares)),
-        out_specs=tuple(vmem(2)),
+    some_rows = jax.ShapeDtypeStruct((CAP, width), jnp.bfloat16)
+    all_rows = jax.ShapeDtypeStruct((token_count, width), jnp.bfloat16)
+    attn_proj, kept, sent, second, last, expert_sum = pl.pallas_call(
+        project_kernel,
+        out_shape=(all_rows, some_rows, some_rows, some_rows, some_rows, all_rows),
+        in_specs=smem(1) + vmem(4 + len(shares)),
+        out_specs=tuple(vmem(4) + [pl.BlockSpec(memory_space=pl.ANY)] * 2),
         scratch_shapes=[pltpu.VMEM((token_count, width), jnp.float32)],
         cost_estimate=pl.CostEstimate(
             flops=2 * token_count * HEADS * HD * width,
             bytes_accessed=2 * HEADS * HD * width,
             transcendentals=0,
         ),
-        compiler_params=pltpu.CompilerParams(vmem_limit_bytes=24 * 2**20),
-    )(attended, residual[0], norm_gain[None], place, *shares)
-
-    owners = expert_owner[:PASS_SPECIALISTS]
-    differ = owners[0] ^ owners[1]
-    branch = 0
-    split_bit = 0
-    for k in reversed(range(len(bits))):
-        parted = (differ & bits[k]) != 0
-        branch = jnp.where(parted, k, branch)
-        split_bit = jnp.where(parted, bits[k], split_bit)
-    same = split_bit == 0
-    side = jnp.where(((me ^ owners[0]) & split_bit) == 0, 0, 1)
+        compiler_params=pltpu.CompilerParams(vmem_limit_bytes=16 * 2**20),
+    )(info, attended, residual[0], norm_gain[None], select, *shares)
+
     units = w_down.shape[1]
     row_count = dp_size * CAP
 
@@ -475,28 +531,26 @@
     def give_back(bit):
         rest = [b for b in bits if b != bit]
 
-        def run(made, offset, other_offset):
-            return scatter_rows(made, bit, rest, dp_size, offset, other_offset)
+        def run(made, info, step):
+            places = [
+                jnp.where(step == 0, info[PASS_INFO + k], info[PASS_INFO + PASS_COUNT + k]) != 0
+                for k in (NEAR_LAST, NEAR_SECOND, OTHER_NEAR)
+            ]
+            return scatter_rows(made, bit, rest, dp_size, *places)
 
         return run
 
-    def one_pass(step, produced):
-        local = jnp.where(same, step, side)
-        sent_expert = jnp.where(same, step, 1 - side)
-        owner = jnp.where(local == 0, owners[0], owners[1])
-        offset = me ^ owner
-        other_offset = me ^ jnp.where(sent_expert == 0, owners[0], owners[1])
-        kept = jnp.where(local == 0, chosen[:CAP], chosen[CAP:])
-        sent = jnp.where(sent_expert == 0, chosen[:CAP], chosen[CAP:])
+    branch = info[BRANCH]
+
+    def one_pass(step, carried):
+        kept, sent, last, _ = carried
         rows, gate_up_far, down_far = lax.switch(
             branch, [dispatch(bit) for bit in bits], kept, sent
         )
         made = pl.pallas_call(
             expert_kernel,
             out_shape=jax.ShapeDtypeStruct((row_count, width), jnp.bfloat16),
-            in_specs=[pl.BlockSpec(memory_space=pltpu.SMEM)]
-            + vmem(1)
-            + [pl.BlockSpec(memory_space=pl.ANY)] * 4,
+            in_specs=smem(2) + vmem(1) + [pl.BlockSpec(memory_space=pltpu.HBM)] * 4,
             out_specs=vmem(1)[0],
             scratch_shapes=[
                 pltpu.VMEM((2, units, width), jnp.bfloat16),
@@ -509,28 +563,20 @@
                 bytes_accessed=6 * units * width,
                 transcendentals=row_count * units,
             ),
-            compiler_params=pltpu.CompilerParams(vmem_limit_bytes=30 * 2**20),
-        )((offset & 1)[None], rows, gate_up_near, gate_up_far, w_down[0], down_far)
-        own, other = lax.switch(branch, [give_back(bit) for bit in bits], made, offset, other_offset)
-        served = jnp.where((offset & bits[0]) == 0, own, other)
-        first = jnp.where(same, served, jnp.where(local == 0, own, other))
-        second = jnp.where(same, served, jnp.where(local == 0, other, own))
-        return (
-            jnp.where(same & (step != 0), produced[0], first),
-            jnp.where(same & (step != 1), produced[1], second),
-        )
-
-    nothing = jnp.zeros((CAP, width), jnp.bfloat16)
-    produced = lax.fori_loop(0, jnp.where(same, 2, 1), one_pass, (nothing, nothing))
-    summed = 0.0
-    for expert in range(PASS_SPECIALISTS):
-        picked = jnp.dot(
-            place[:, expert * CAP : (expert + 1) * CAP],
-            produced[expert],
-            preferred_element_type=jnp.float32,
-        )
-        summed = summed + gate_values[:, expert : expert + 1] * picked
-    expert_sum = summed.astype(jnp.bfloat16)
+            compiler_params=pltpu.CompilerParams(vmem_limit_bytes=22 * 2**20),
+        )(info, step[None], rows, gate_up_near, gate_up_far, w_down[0], down_far)
+        own, other = lax.switch(branch, [give_back(bit) for bit in bits], made, info, step)
+        expert_sum, last, kept, sent = pl.pallas_call(
+            combine_kernel,
+            out_shape=(all_rows, some_rows, some_rows, some_rows),
+            in_specs=smem(2) + vmem(6),
+            out_specs=tuple(vmem(4)),
+            compiler_params=pltpu.CompilerParams(vmem_limit_bytes=8 * 2**20),
+        )(info, step[None], own, other, last, second, select, gate_values)
+        return kept, sent, last, expert_sum
+
+    carried = (kept, sent, last, expert_sum)
+    expert_sum = lax.fori_loop(0, info[PASSES], one_pass, carried)[3]
     return (attn_proj[None], expert_sum[None])
 
 

time: 124 us -> 120 us (0.968)
  other arithmetic: 5.69 us -> 1.61 us
  Pallas kernels: 13.4 us -> 16.7 us
  local copies, waits for them, and re-layouts: 9.57 us -> 7.08 us
  loops' own time: 2.96 us -> 5.34 us
  matrix products: 1.42 us -> 0 us
  starting transfers between devices: 29.8 us -> 31.2 us
  waiting for transfers between devices: 57.5 us -> 56.2 us
  between operations: 2.85 us -> 1.56 us
    another operation x2 -> x0, other arithmetic: 3.06 us -> none  [body_move_rows(): jnp.stack([near[j] for j in group])]
    pallas_call x2 -> x3, Pallas kernels: 6.29 us -> 8.96 us  [the longest x1 3.81 us: body_move_rows(): pl.pallas_call(functools.partial(attend_kernel, bits), out_shape=(jax.Sha...]
    another operation x2, loops' own time: 2.85 us -> 5.23 us  [the longest x1 3.72 us: one_pass(): lax.switch(branch, [give_back(bit) for bit in bits], made, info, step)]
    slice x4 -> x2, local copies, waits for them, and re-layouts: 2.73 us -> 1.21 us  [the longest x1 0.62 us: run(): info[PASS_INFO + PASS_COUNT + k]]
    dot_general x2 -> x0, matrix products: 1.42 us -> none  [body_move_rows(): jnp.dot(place[:, expert * CAP:(expert + 1) * CAP], produced[expert], pref...]
    ppermute x26 -> x31, starting transfers between devices: 26.4 us -> 27.8 us  [hop(): return lax.ppermute(array, axis, [(i, i ^ bit) for i in range(size)])]
    ppermute x26 -> x31, waiting for transfers between devices: 57.5 us -> 56.2 us  [hop(): return lax.ppermute(array, axis, [(i, i ^ bit) for i in range(size)])]
    unnamed x28 -> x18, local copies, waits for them, and re-layouts: 5.31 us -> 5.54 us
  transfers between devices with their start and end apart: 27 -> 32, of which waited for: 14 -> 16; matrix products, arithmetic and copies ran while one was open for 9% -> 4% of each run, Pallas kernels for 3% -> 3%
where the time goes in v4:
time: 120 us
  waiting for transfers between devices  56.2 us (47%)
  starting transfers between devices  31.2 us (26%)
  Pallas kernels  16.7 us (14%)
  local copies, waits for them, and re-layouts  7.08 us (6%)
  loops' own time  5.34 us (4%)
  other arithmetic  1.61 us (1%)
  between operations  1.56 us (1%)
    ppermute x31, waiting for transfers between devices, hop(): return lax.ppermute(array, axis, [(i, i ^ bit) for i in range(size)])  56.2 us
    ppermute x31, starting transfers between devices, hop(): return lax.ppermute(array, axis, [(i, i ^ bit) for i in range(size)])  27.8 us
    pallas_call x1, Pallas kernels, one_pass(): pl.pallas_call(expert_kernel, out_shape=jax.ShapeDtypeStruct((row_count,...  7.72 us
    unnamed x18, local copies, waits for them, and re-layouts  5.54 us
    pallas_call x1, Pallas kernels, body_move_rows(): pl.pallas_call(functools.partial(attend_kernel, bits), out_shape=(jax.Sha...  3.81 us
    another operation x1, loops' own time, one_pass(): lax.switch(branch, [give_back(bit) for bit in bits], made, info, step)  3.72 us
    ppermute x1, starting transfers between devices, body_move_rows(): lax.ppermute(jnp.stack([key_vecs[0], value_vecs[0]]), 'ctx', [(0, 1)])  3.46 us
    pallas_call x1, Pallas kernels, body_move_rows(): pl.pallas_call(project_kernel, out_shape=(all_rows, some_rows, some_rows,...  3.24 us
  transfers between devices with their start and end apart: 32, of which 16 were waited for; matrix products, arithmetic and copies ran while one was open for 4% of the time, Pallas kernels for 3%

profile of v4, /device:TPU:0, one launch (start us, length us, event | category | flops | bytes accessed | tf_op | source)
XLA Modules:
  0.0 119.7 jit_solution(17111310807909678569)
XLA Ops:
  0.6 3.1 %collective-permute-start.49 = (bf16[64,2048]{1,0:T(8,128)(2,1)}, bf16[64,2048]{1,0:T(8,128)(2,1)S(1)}, u32[]{:S(2)}, u32[]{:S(2)}) collective-permute-start(bf16[64,2048]{1,0:T(8,128)(2,1)} %refs_0_.1), channel_id=1, source_target_pairs={{0,8},{2,10},{4,12},{6,14},{8,0},{10,2},{12,4},{14,6},{16,24},{18,... | collective-permute-start | bytes 786440 | tf_op jit(solution)/shard_map/ppermute | solution.py:26
  3.7 1.5 %collective-permute-start.50 = (bf16[64,2048]{1,0:T(8,128)(2,1)}, bf16[64,2048]{1,0:T(8,128)(2,1)S(1)}, u32[]{:S(2)}, u32[]{:S(2)}) collective-permute-start(bf16[64,2048]{1,0:T(8,128)(2,1)} %refs_0_.1), channel_id=1, source_target_pairs={{0,4},{2,6},{4,0},{6,2},{8,12},{10,14},{12,8},{14,10},{16,20},{18,... | collective-permute-start | bytes 786440 | tf_op jit(solution)/shard_map/ppermute | solution.py:26
  5.2 2.6 %collective-permute-start.51 = (bf16[64,2048]{1,0:T(8,128)(2,1)}, bf16[64,2048]{1,0:T(8,128)(2,1)S(1)}, u32[]{:S(2)}, u32[]{:S(2)}) collective-permute-start(bf16[64,2048]{1,0:T(8,128)(2,1)} %refs_0_.1), channel_id=1, source_target_pairs={{0,16},{2,18},{4,20},{6,22},{8,24},{10,26},{12,28},{14,30},{16,0},... | collective-permute-start | bytes 786440 | tf_op jit(solution)/shard_map/ppermute | solution.py:26
  7.8 1.1 pad_maximum_fusion.9
  8.9 3.5 %collective-permute-start.48 = (bf16[2,128,1024]{2,1,0:T(8,128)(2,1)S(1)}, bf16[2,128,1024]{2,1,0:T(8,128)(2,1)S(1)}, u32[]{:S(2)}, u32[]{:S(2)}) collective-permute-start(bf16[2,128,1024]{2,1,0:T(8,128)(2,1)S(1)} %pad_maximum_fusion.9), channel_id=1, source_target_pairs={{0,1},{2,3},{4,5},{6,7},{8,9},{10,11},{12,13},{14,15},{16,17},{18,... | collective-permute-start | bytes 1572872 | tf_op jit(solution)/shard_map/ppermute | solution.py:456
  12.3 2.2 %collective-permute-done.49.refs_2_ = bf16[64,2048]{1,0:T(8,128)(2,1)S(1)} collective-permute-done((bf16[64,2048]{1,0:T(8,128)(2,1)}, bf16[64,2048]{1,0:T(8,128)(2,1)S(1)}, u32[]{:S(2)}, u32[]{:S(2)}) %collective-permute-start.49) | collective-permute-done | bytes 262176 | tf_op jit(solution)/shard_map/ppermute | solution.py:26
  14.5 5.0 %collective-permute-done.51.refs_4_ = bf16[64,2048]{1,0:T(8,128)(2,1)S(1)} collective-permute-done((bf16[64,2048]{1,0:T(8,128)(2,1)}, bf16[64,2048]{1,0:T(8,128)(2,1)S(1)}, u32[]{:S(2)}, u32[]{:S(2)}) %collective-permute-start.51) | collective-permute-done | bytes 262176 | tf_op jit(solution)/shard_map/ppermute | solution.py:26
  19.5 0.5 collective-permute-start.52
  20.0 0.2 collective-permute-start.53
  20.2 0.7 copy.39
  20.9 0.7 copy.40
  21.6 1.3 %collective-permute-start.54 = (bf16[64,2048]{1,0:T(8,128)(2,1)S(1)}, bf16[64,2048]{1,0:T(8,128)(2,1)S(1)}, u32[]{:S(2)}, u32[]{:S(2)}) collective-permute-start(bf16[64,2048]{1,0:T(8,128)(2,1)S(1)} %collective-permute-done.51.refs_4_), channel_id=1, source_target_pairs={{0,4},{2,6},{4,0},{6,2},{8,12},{10,14},{12,8},{14,10},{16,20},{18,... | collective-permute-start | bytes 786440 | tf_op jit(solution)/shard_map/ppermute | solution.py:26
  22.9 4.1 %collective-permute-done.52.refs_3_ = bf16[64,2048]{1,0:T(8,128)(2,1)S(1)} collective-permute-done((bf16[64,2048]{1,0:T(8,128)(2,1)S(1)}, bf16[64,2048]{1,0:T(8,128)(2,1)S(1)}, u32[]{:S(2)}, u32[]{:S(2)}) %collective-permute-start.52) | collective-permute-done | bytes 262176 | tf_op jit(solution)/shard_map/ppermute | solution.py:26
  27.0 0.5 collective-permute-start.58
  27.5 0.9 copy-done.2
  28.4 0.9 copy-done.3
  29.4 0.9 copy-done.5
  30.3 0.7 copy-done.6
  31.0 0.7 copy-done.7
  31.7 3.8 %shard_map.131 = (bf16[8,128,128]{2,1,0:T(8,128)(2,1)S(1)}, bf16[2,24,128]{2,1,0:T(8,128)(2,1)S(1)}, f32[128,2]{1,0:T(8,128)}, s32[20]{0:T(128)S(1)}) custom-call(s32[16]{0:T(128)S(1)} %copy-done.6, s32[1,1,2]{2,1,0:T(1,128)S(1)} %copy-done.7, bf16[128,1024]{1,0:T(8,128)(2,1)S(1)} %bitcast.187, bf16[128,1024]{1,0:T(8,128)(2,1)S(1)} %bitcast.182, ...), custom_call_target="tpu_custom_call" | custom-call | flops 2147483648 | bytes 1572864 | tf_op jit(solution)/shard_map/pallas_call | solution.py:469
  35.5 0.1 collective-permute-start.55
  35.6 0.1 collective-permute-start.57
  35.7 0.5 collective-permute-start.62
  36.2 0.1 collective-permute-start.59
  36.3 0.4 collective-permute-start.61
  36.7 7.2 %collective-permute-done.55.refs_7_ = bf16[64,2048]{1,0:T(8,128)(2,1)} collective-permute-done((bf16[64,2048]{1,0:T(8,128)(2,1)S(1)}, bf16[64,2048]{1,0:T(8,128)(2,1)}, u32[]{:S(2)}, u32[]{:S(2)}) %collective-permute-start.55) | collective-permute-done | bytes 262176 | tf_op jit(solution)/shard_map/ppermute | solution.py:26
  43.9 0.6 fusion.30
  45.2 0.6 collective-permute-done.63.refs_15_
  45.8 3.2 %shard_map.132 = (bf16[128,2048]{1,0:T(8,128)(2,1)}, bf16[24,2048]{1,0:T(8,128)(2,1)S(1)}, bf16[24,2048]{1,0:T(8,128)(2,1)}, bf16[24,2048]{1,0:T(8,128)(2,1)}, b...) custom-call(s32[20]{0:T(128)S(1)} %get-tuple-element.470.info, bf16[8,128,128]{2,1,0:T(8,128)(2,1)S(1)} %get-tuple-element.255.attended, ...), custom_call_target="tpu_custom_call" | custom-call | flops 536870912 | bytes 4194304 | tf_op jit(solution)/shard_map/pallas_call | solution.py:503
  49.0 70.5 %while.18 = (s32[]{:T(128)}, bf16[24,2048]{1,0:T(8,128)(2,1)S(1)}, bf16[24,2048]{1,0:T(8,128)(2,1)}, bf16[24,2048]{1,0:T(8,128)(2,1)}, bf16[128,2048]{1,0:T(8,12...) while((s32[]{:T(128)}, bf16[24,2048]{1,0:T(8,128)(2,1)S(1)}, ...), condition=%wide.region_7.8_spmd, body=%wide.region_0.7_spmd.sunk | while | flops 3330932736 | bytes 73929792 | solution.py:579
  49.8 31.7 %conditional.4 = (bf16[384,2048]{1,0:T(8,128)(2,1)S(1)}, bf16[2,704,2048]{2,1,0:T(8,128)(2,1)}, bf16[704,2048]{1,0:T(8,128)(2,1)}) conditional(s32[]{:T(128)} %get-tuple-element.497, (bf16[24,2048]{1,0:T(8,128)(2,1)}, bf16[24,2048]{1,0:T(8,128)(2,1)S(1)}, bf16[2,704,2048]{2,1,0:T(8,128)(2,1)}, ...), branch_computations={%region_1.0_spmd, %region_2.0_spmd, %region_3.0_spmd} | conditional | flops 6684672 | bytes 51118464 | solution.py:547
  49.8 0.2 collective-permute-start.16
  50.0 0.4 collective-permute-start.17
  50.4 3.1 %collective-permute-start.11 = (bf16[24,2048]{1,0:T(8,128)(2,1)}, bf16[24,2048]{1,0:T(8,128)(2,1)S(1)}, u32[]{:S(2)}, u32[]{:S(2)}) collective-permute-start(bf16[24,2048]{1,0:T(8,128)(2,1)} %get-tuple-element.179), channel_id=1, source_target_pairs={{0,24},{2,26},{4,28},{6,30},{8,16},{10,18},{12,20},{14,22},{16,8},... | collective-permute-start | bytes 294920 | tf_op jit(solution)/shard_map/while/body/cond/branch_1_fun/ppermute | solution.py:26
  53.5 0.6 collective-permute-start.10
  54.1 1.3 %collective-permute-done.9 = bf16[24,2048]{1,0:T(8,128)(2,1)S(1)} collective-permute-done((bf16[24,2048]{1,0:T(8,128)(2,1)}, bf16[24,2048]{1,0:T(8,128)(2,1)S(1)}, u32[]{:S(2)}, u32[]{:S(2)}) %collective-permute-start.9) | collective-permute-done | bytes 98336 | tf_op jit(solution)/shard_map/while/body/cond/branch_1_fun/ppermute | solution.py:26
  55.5 8.0 %collective-permute-done.10 = bf16[24,2048]{1,0:T(8,128)(2,1)S(1)} collective-permute-done((bf16[24,2048]{1,0:T(8,128)(2,1)S(1)}, bf16[24,2048]{1,0:T(8,128)(2,1)S(1)}, u32[]{:S(2)}, u32[]{:S(2)}) %collective-permute-start.10) | collective-permute-done | bytes 98336 | tf_op jit(solution)/shard_map/while/body/cond/branch_1_fun/ppermute | solution.py:26
  63.5 0.1 slice_bitcast_fusion.3
  63.6 0.3 collective-permute-start.12
  63.9 1.5 %collective-permute-start.14 = (bf16[96,1024]{1,0:T(8,128)(2,1)S(1)}, bf16[96,1024]{1,0:T(8,128)(2,1)S(1)}, u32[]{:S(2)}, u32[]{:S(2)}) collective-permute-start(bf16[96,1024]{1,0:T(8,128)(2,1)S(1)} %get-tuple-element.306), channel_id=1, source_target_pairs={{0,1},{1,0},{2,3},{3,2},{4,5},{5,4},{6,7},{7,6},{8,9},{9,8},{10,11... | collective-permute-start | bytes 589832 | tf_op jit(solution)/shard_map/while/body/cond/branch_1_fun/ppermute | solution.py:26
  65.5 4.6 %collective-permute-done.12 = bf16[96,1024]{1,0:T(8,128)(2,1)S(1)} collective-permute-done((bf16[96,1024]{1,0:T(8,128)(2,1)S(1)}, bf16[96,1024]{1,0:T(8,128)(2,1)S(1)}, u32[]{:S(2)}, u32[]{:S(2)}) %collective-permute-start.12) | collective-permute-done | bytes 196640 | tf_op jit(solution)/shard_map/while/body/cond/branch_1_fun/ppermute | solution.py:26
  70.1 1.6 %collective-permute-start.13 = (bf16[2,96,1024]{2,1,0:T(8,128)(2,1)S(1)}, bf16[2,96,1024]{2,1,0:T(8,128)(2,1)S(1)}, u32[]{:S(2)}, u32[]{:S(2)}) collective-permute-start(bf16[2,96,1024]{2,1,0:T(8,128)(2,1)S(1)} %get-tuple-element.303), channel_id=1, source_target_pairs={{0,1},{1,0},{2,3},{3,2},{4,5},{5,4},{6,7},{7,6},{8,9},{9,8},{10,11... | collective-permute-start | bytes 1179656 | tf_op jit(solution)/shard_map/while/body/cond/branch_1_fun/ppermute | solution.py:26
  71.7 0.4 collective-permute-start.15
  72.1 7.8 %collective-permute-done.13 = bf16[2,96,1024]{2,1,0:T(8,128)(2,1)S(1)} collective-permute-done((bf16[2,96,1024]{2,1,0:T(8,128)(2,1)S(1)}, bf16[2,96,1024]{2,1,0:T(8,128)(2,1)S(1)}, u32[]{:S(2)}, u32[]{:S(2)}) %collective-permute-start.13) | collective-permute-done | bytes 393248 | tf_op jit(solution)/shard_map/while/body/cond/branch_1_fun/ppermute | solution.py:26
  79.8 1.4 %collective-permute-done.15 = bf16[2,96,1024]{2,1,0:T(8,128)(2,1)S(1)} collective-permute-done((bf16[2,96,1024]{2,1,0:T(8,128)(2,1)S(1)}, bf16[2,96,1024]{2,1,0:T(8,128)(2,1)S(1)}, u32[]{:S(2)}, u32[]{:S(2)}) %collective-permute-start.15) | collective-permute-done | bytes 393248 | tf_op jit(solution)/shard_map/while/body/cond/branch_1_fun/ppermute | solution.py:26
  81.2 0.1 maximum_maximum_fusion.1
  81.3 0.1 copy.26
  81.5 7.7 %body.6 = bf16[384,2048]{1,0:T(8,128)(2,1)S(1)} custom-call(s32[20]{0:T(128)S(1)} %get-tuple-element.498.info, s32[1]{0:T(128)} %bitcast.179.step, bf16[384,2048]{1,0:T(8,128)(2,1)S(1)} %get-tuple-element.437.rows, bf16[2,704,2048]{2,1,0:T(8,128)(2,1)} %get-tuple-element.495.gate_up_near, bf16[2,704,2048]{2,1,0:T(8,128)(2,1)} %get-tuple-element.438.gate_up_far, ...), custom_call_target="tpu_custom_call" | custom-call | flops 3321888768 | bytes 8650752 | tf_op jit(solution)/shard_map/while/body/pallas_call | solution.py:550
  89.2 27.7 %conditional.5 = (bf16[24,2048]{1,0:T(8,128)(2,1)S(1)}, bf16[24,2048]{1,0:T(8,128)(2,1)S(1)}) conditional(s32[]{:T(128)} %get-tuple-element.497, (s32[]{:T(128)}, s32[20]{0:T(128)S(1)}, bf16[384,2048]{1,0:T(8,128)(2,1)S(1)}) %tuple.105, (s32[]{:T(128)}, s32[20]{0:T(128)S(1)}, bf16[384,2048]{1,0:T(8,128)(2,1)S(1)}) %tuple.105, ...), branch_computations={%region_4.4_spmd, %region_5.5_spmd, %region_6.6_spmd} | conditional | flops 2359303 | bytes 13173159 | solution.py:568
  89.3 0.3 collective-permute-start.36
  89.7 1.4 %collective-permute-start.34 = (bf16[2,96,1024]{2,1,0:T(8,128)(2,1)S(1)}, bf16[2,96,1024]{2,1,0:T(8,128)(2,1)S(1)}, u32[]{:S(2)}, u32[]{:S(2)}) collective-permute-start(bf16[2,96,1024]{2,1,0:T(8,128)(2,1)S(1)} %slice_bitcast_fusion.16), channel_id=1, source_target_pairs={{0,1},{1,0},{2,3},{3,2},{4,5},{5,4},{6,7},{7,6},{8,9},{9,8},{10,11... | collective-permute-start | bytes 1179656 | tf_op jit(solution)/shard_map/while/body/cond/branch_1_fun/ppermute | solution.py:26
  91.1 0.6 fusion.28
  92.9 5.1 %collective-permute-done.36 = bf16[2,96,1024]{2,1,0:T(8,128)(2,1)S(1)} collective-permute-done((bf16[2,96,1024]{2,1,0:T(8,128)(2,1)S(1)}, bf16[2,96,1024]{2,1,0:T(8,128)(2,1)S(1)}, u32[]{:S(2)}, u32[]{:S(2)}) %collective-permute-start.36) | collective-permute-done | bytes 393248 | tf_op jit(solution)/shard_map/while/body/cond/branch_1_fun/ppermute | solution.py:26
  98.1 0.4 collective-permute-start.37
  98.5 0.2 collective-permute-done.34
  98.7 0.1 fusion.13
  98.9 3.1 %collective-permute-start.35 = (bf16[96,1024]{1,0:T(8,128)(2,1)S(1)}, bf16[96,1024]{1,0:T(8,128)(2,1)S(1)}, u32[]{:S(2)}, u32[]{:S(2)}) collective-permute-start(bf16[96,1024]{1,0:T(8,128)(2,1)S(1)} %slice_bitcast_fusion.20), channel_id=1, source_target_pairs={{0,4},{2,6},{4,0},{6,2},{8,12},{10,14},{12,8},{14,10},{16,20},{18,... | collective-permute-start | bytes 589832 | tf_op jit(solution)/shard_map/while/body/cond/branch_1_fun/ppermute | solution.py:26
  102.0 1.8 %collective-permute-done.37 = bf16[96,1024]{1,0:T(8,128)(2,1)S(1)} collective-permute-done((bf16[96,1024]{1,0:T(8,128)(2,1)S(1)}, bf16[96,1024]{1,0:T(8,128)(2,1)S(1)}, u32[]{:S(2)}, u32[]{:S(2)}) %collective-permute-start.37) | collective-permute-done | bytes 196640 | tf_op jit(solution)/shard_map/while/body/cond/branch_1_fun/ppermute | solution.py:26
  103.9 1.8 %collective-permute-done.35 = bf16[96,1024]{1,0:T(8,128)(2,1)S(1)} collective-permute-done((bf16[96,1024]{1,0:T(8,128)(2,1)S(1)}, bf16[96,1024]{1,0:T(8,128)(2,1)S(1)}, u32[]{:S(2)}, u32[]{:S(2)}) %collective-permute-start.35) | collective-permute-done | bytes 196640 | tf_op jit(solution)/shard_map/while/body/cond/branch_1_fun/ppermute | solution.py:26
  105.8 2.1 %collective-permute-start.40 = (bf16[24,2048]{1,0:T(8,128)(2,1)S(1)}, bf16[24,2048]{1,0:T(8,128)(2,1)S(1)}, u32[]{:S(2)}, u32[]{:S(2)}) collective-permute-start(bf16[24,2048]{1,0:T(8,128)(2,1)S(1)} %get-tuple-element.199), channel_id=1, source_target_pairs={{0,24},{2,26},{4,28},{6,30},{8,16},{10,18},{12,20},{14,22},{16,8},... | collective-permute-start | bytes 294920 | tf_op jit(solution)/shard_map/while/body/cond/branch_1_fun/ppermute | solution.py:26
  110.3 1.5 %collective-permute-start.38 = (bf16[24,2048]{1,0:T(8,128)(2,1)S(1)}, bf16[24,2048]{1,0:T(8,128)(2,1)S(1)}, u32[]{:S(2)}, u32[]{:S(2)}) collective-permute-start(bf16[24,2048]{1,0:T(8,128)(2,1)S(1)} %get-tuple-element.197), channel_id=1, source_target_pairs={{0,16},{2,18},{4,20},{6,22},{8,24},{10,26},{12,28},{14,30},{16,0},... | collective-permute-start | bytes 294920 | tf_op jit(solution)/shard_map/while/body/cond/branch_1_fun/ppermute | solution.py:26
  111.8 0.6 collective-permute-done.40
  112.4 4.5 %collective-permute-done.38 = bf16[24,2048]{1,0:T(8,128)(2,1)S(1)} collective-permute-done((bf16[24,2048]{1,0:T(8,128)(2,1)S(1)}, bf16[24,2048]{1,0:T(8,128)(2,1)S(1)}, u32[]{:S(2)}, u32[]{:S(2)}) %collective-permute-start.38) | collective-permute-done | bytes 98336 | tf_op jit(solution)/shard_map/while/body/cond/branch_1_fun/ppermute | solution.py:26
  117.0 1.9 %body.7 = (bf16[128,2048]{1,0:T(8,128)(2,1)}, bf16[24,2048]{1,0:T(8,128)(2,1)}, bf16[24,2048]{1,0:T(8,128)(2,1)S(1)}, bf16[24,2048]{1,0:T(8,128)(2,1)}) custom-call(s32[20]{0:T(128)S(1)} %get-tuple-element.498.info, s32[1]{0:T(128)} %bitcast.179.step, bf16[24,2048]{1,0:T(8,128)(2,1)S(1)} %get-tuple-element.440.own, ...), custom_call_target="tpu_custom_call" | custom-call | tf_op jit(solution)/shard_map/while/body/pallas_call | solution.py:569
  (55 shorter events, 0.6 us)
Async XLA Ops:
  0.6 13.9 %collective-permute-start.49 = (bf16[64,2048]{1,0:T(8,128)(2,1)}, bf16[64,2048]{1,0:T(8,128)(2,1)S(1)}, u32[]{:S(2)}, u32[]{:S(2)}) collective-permute-start(bf16[64,2048]{1,0:T(8,128)(2,1)} %refs_0_.1), channel_id=1, source_target_pairs={{0,8},{2,10},{4,12},{6,14},{8,0},{10,2},{12,4},{14,6},{16,24},{18,... | collective-permute-start | bytes 786440 | tf_op jit(solution)/shard_map/ppermute | solution.py:26
  3.7 10.8 %collective-permute-start.50 = (bf16[64,2048]{1,0:T(8,128)(2,1)}, bf16[64,2048]{1,0:T(8,128)(2,1)S(1)}, u32[]{:S(2)}, u32[]{:S(2)}) collective-permute-start(bf16[64,2048]{1,0:T(8,128)(2,1)} %refs_0_.1), channel_id=1, source_target_pairs={{0,4},{2,6},{4,0},{6,2},{8,12},{10,14},{12,8},{14,10},{16,20},{18,... | collective-permute-start | bytes 786440 | tf_op jit(solution)/shard_map/ppermute | solution.py:26
  5.2 14.3 %collective-permute-start.51 = (bf16[64,2048]{1,0:T(8,128)(2,1)}, bf16[64,2048]{1,0:T(8,128)(2,1)S(1)}, u32[]{:S(2)}, u32[]{:S(2)}) collective-permute-start(bf16[64,2048]{1,0:T(8,128)(2,1)} %refs_0_.1), channel_id=1, source_target_pairs={{0,16},{2,18},{4,20},{6,22},{8,24},{10,26},{12,28},{14,30},{16,0},... | collective-permute-start | bytes 786440 | tf_op jit(solution)/shard_map/ppermute | solution.py:26
  8.9 18.1 %collective-permute-start.48 = (bf16[2,128,1024]{2,1,0:T(8,128)(2,1)S(1)}, bf16[2,128,1024]{2,1,0:T(8,128)(2,1)S(1)}, u32[]{:S(2)}, u32[]{:S(2)}) collective-permute-start(bf16[2,128,1024]{2,1,0:T(8,128)(2,1)S(1)} %pad_maximum_fusion.9), channel_id=1, source_target_pairs={{0,1},{2,3},{4,5},{6,7},{8,9},{10,11},{12,13},{14,15},{16,17},{18,... | collective-permute-start | bytes 1572872 | tf_op jit(solution)/shard_map/ppermute | solution.py:456
  19.5 7.5 %collective-permute-start.52 = (bf16[64,2048]{1,0:T(8,128)(2,1)S(1)}, bf16[64,2048]{1,0:T(8,128)(2,1)S(1)}, u32[]{:S(2)}, u32[]{:S(2)}) collective-permute-start(bf16[64,2048]{1,0:T(8,128)(2,1)S(1)} %collective-permute-done.49.refs_2_), channel_id=1, source_target_pairs={{0,4},{2,6},{4,0},{6,2},{8,12},{10,14},{12,8},{14,10},{16,20},{18,... | collective-permute-start | bytes 786440 | tf_op jit(solution)/shard_map/ppermute | solution.py:26
  20.0 15.5 %collective-permute-start.53 = (bf16[64,2048]{1,0:T(8,128)(2,1)S(1)}, bf16[64,2048]{1,0:T(8,128)(2,1)S(1)}, u32[]{:S(2)}, u32[]{:S(2)}) collective-permute-start(bf16[64,2048]{1,0:T(8,128)(2,1)S(1)} %collective-permute-done.51.refs_4_), channel_id=1, source_target_pairs={{0,8},{2,10},{4,12},{6,14},{8,0},{10,2},{12,4},{14,6},{16,24},{18,... | collective-permute-start | bytes 786440 | tf_op jit(solution)/shard_map/ppermute | solution.py:26
  20.2 15.4 %collective-permute-start.56 = (bf16[64,2048]{1,0:T(8,128)(2,1)}, bf16[64,2048]{1,0:T(8,128)(2,1)S(1)}, u32[]{:S(2)}, u32[]{:S(2)}) collective-permute-start(bf16[64,2048]{1,0:T(8,128)(2,1)} %refs_0_.1), channel_id=1, source_target_pairs={{0,2},{2,0},{4,6},{6,4},{8,10},{10,8},{12,14},{14,12},{16,18},{18,... | collective-permute-start | bytes 786440 | tf_op jit(solution)/shard_map/ppermute | solution.py:26
  21.6 14.1 %collective-permute-start.54 = (bf16[64,2048]{1,0:T(8,128)(2,1)S(1)}, bf16[64,2048]{1,0:T(8,128)(2,1)S(1)}, u32[]{:S(2)}, u32[]{:S(2)}) collective-permute-start(bf16[64,2048]{1,0:T(8,128)(2,1)S(1)} %collective-permute-done.51.refs_4_), channel_id=1, source_target_pairs={{0,4},{2,6},{4,0},{6,2},{8,12},{10,14},{12,8},{14,10},{16,20},{18,... | collective-permute-start | bytes 786440 | tf_op jit(solution)/shard_map/ppermute | solution.py:26
  27.0 9.2 %collective-permute-start.60 = (bf16[64,2048]{1,0:T(8,128)(2,1)S(1)}, bf16[64,2048]{1,0:T(8,128)(2,1)S(1)}, u32[]{:S(2)}, u32[]{:S(2)}) collective-permute-start(bf16[64,2048]{1,0:T(8,128)(2,1)S(1)} %collective-permute-done.51.refs_4_), channel_id=1, source_target_pairs={{0,2},{2,0},{4,6},{6,4},{8,10},{10,8},{12,14},{14,12},{16,18},{18,... | collective-permute-start | bytes 786440 | tf_op jit(solution)/shard_map/ppermute | solution.py:26
  27.0 9.3 %collective-permute-start.58 = (bf16[64,2048]{1,0:T(8,128)(2,1)S(1)}, bf16[64,2048]{1,0:T(8,128)(2,1)S(1)}, u32[]{:S(2)}, u32[]{:S(2)}) collective-permute-start(bf16[64,2048]{1,0:T(8,128)(2,1)S(1)} %collective-permute-done.49.refs_2_), channel_id=1, source_target_pairs={{0,2},{2,0},{4,6},{6,4},{8,10},{10,8},{12,14},{14,12},{16,18},{18,... | collective-permute-start | bytes 786440 | tf_op jit(solution)/shard_map/ppermute | solution.py:26
  27.5 0.9 copy-start.2
  28.4 0.9 copy-start.3
  29.4 0.9 copy-start.5
  30.3 0.7 copy-start.6
  31.0 0.7 copy-start.7
  31.6 14.1 %copy-start = (bf16[1,128,2048]{2,1,0:T(8,128)(2,1)S(1)}, bf16[1,128,2048]{2,1,0:T(8,128)(2,1)}, u32[]{:S(2)}) copy-start(bf16[1,128,2048]{2,1,0:T(8,128)(2,1)} %param.23) | copy-start | bytes 1572868
  31.7 14.1 %copy-start.1 = (bf16[64,2048]{1,0:T(8,128)(2,1)S(1)}, bf16[64,2048]{1,0:T(8,128)(2,1)}, u32[]{:S(2)}) copy-start(bf16[64,2048]{1,0:T(8,128)(2,1)} %refs_0_.1) | copy-start | bytes 786436
  31.7 14.1 %copy-start.4 = (f32[2048]{0:T(1024)S(1)}, f32[2048]{0:T(1024)}, u32[]{:S(2)}) copy-start(f32[2048]{0:T(1024)} %param.25) | copy-start | bytes 24580
  35.5 8.4 %collective-permute-start.55 = (bf16[64,2048]{1,0:T(8,128)(2,1)S(1)}, bf16[64,2048]{1,0:T(8,128)(2,1)}, u32[]{:S(2)}, u32[]{:S(2)}) collective-permute-start(bf16[64,2048]{1,0:T(8,128)(2,1)S(1)} %collective-permute-done.53.refs_6_), channel_id=1, source_target_pairs={{0,4},{2,6},{4,0},{6,2},{8,12},{10,14},{12,8},{14,10},{16,20},{18,... | collective-permute-start | bytes 786440 | tf_op jit(solution)/shard_map/ppermute | solution.py:26
  35.6 9.5 %collective-permute-start.57 = (bf16[64,2048]{1,0:T(8,128)(2,1)S(1)}, bf16[64,2048]{1,0:T(8,128)(2,1)}, u32[]{:S(2)}, u32[]{:S(2)}) collective-permute-start(bf16[64,2048]{1,0:T(8,128)(2,1)S(1)} %collective-permute-done.50.refs_1_), channel_id=1, source_target_pairs={{0,2},{2,0},{4,6},{6,4},{8,10},{10,8},{12,14},{14,12},{16,18},{18,... | collective-permute-start | bytes 786440 | tf_op jit(solution)/shard_map/ppermute | solution.py:26
  35.7 9.5 %collective-permute-start.62 = (bf16[64,2048]{1,0:T(8,128)(2,1)S(1)}, bf16[64,2048]{1,0:T(8,128)(2,1)}, u32[]{:S(2)}, u32[]{:S(2)}) collective-permute-start(bf16[64,2048]{1,0:T(8,128)(2,1)S(1)} %collective-permute-done.53.refs_6_), channel_id=1, source_target_pairs={{0,2},{2,0},{4,6},{6,4},{8,10},{10,8},{12,14},{14,12},{16,18},{18,... | collective-permute-start | bytes 786440 | tf_op jit(solution)/shard_map/ppermute | solution.py:26
  36.2 9.0 %collective-permute-start.59 = (bf16[64,2048]{1,0:T(8,128)(2,1)S(1)}, bf16[64,2048]{1,0:T(8,128)(2,1)}, u32[]{:S(2)}, u32[]{:S(2)}) collective-permute-start(bf16[64,2048]{1,0:T(8,128)(2,1)S(1)} %collective-permute-done.52.refs_3_), channel_id=1, source_target_pairs={{0,2},{2,0},{4,6},{6,4},{8,10},{10,8},{12,14},{14,12},{16,18},{18,... | collective-permute-start | bytes 786440 | tf_op jit(solution)/shard_map/ppermute | solution.py:26
  36.3 8.9 %collective-permute-start.61 = (bf16[64,2048]{1,0:T(8,128)(2,1)S(1)}, bf16[64,2048]{1,0:T(8,128)(2,1)}, u32[]{:S(2)}, u32[]{:S(2)}) collective-permute-start(bf16[64,2048]{1,0:T(8,128)(2,1)S(1)} %collective-permute-done.54.refs_5_), channel_id=1, source_target_pairs={{0,2},{2,0},{4,6},{6,4},{8,10},{10,8},{12,14},{14,12},{16,18},{18,... | collective-permute-start | bytes 786440 | tf_op jit(solution)/shard_map/ppermute | solution.py:26
  43.9 1.9 %collective-permute-start.63 = (bf16[64,2048]{1,0:T(8,128)(2,1)}, bf16[64,2048]{1,0:T(8,128)(2,1)}, u32[]{:S(2)}, u32[]{:S(2)}) collective-permute-start(bf16[64,2048]{1,0:T(8,128)(2,1)} %collective-permute-done.55.refs_7_), channel_id=1, source_target_pairs={{0,2},{2,0},{4,6},{6,4},{8,10},{10,8},{12,14},{14,12},{16,18},{18,... | collective-permute-start | bytes 786440 | tf_op jit(solution)/shard_map/ppermute | solution.py:26
  49.8 31.6 %collective-permute-start.16 = (bf16[2,704,2048]{2,1,0:T(8,128)(2,1)}, bf16[2,704,2048]{2,1,0:T(8,128)(2,1)}, u32[]{:S(2)}, u32[]{:S(2)}) collective-permute-start(bf16[2,704,2048]{2,1,0:T(8,128)(2,1)} %get-tuple-element.180), channel_id=1, source_target_pairs={{0,2},{2,0},{4,6},{6,4},{8,10},{10,8},{12,14},{14,12},{16,18},{18,... | collective-permute-start | bytes 17301512 | tf_op jit(solution)/shard_map/while/body/cond/branch_1_fun/ppermute | solution.py:26
  50.0 31.4 %collective-permute-start.17 = (bf16[704,2048]{1,0:T(8,128)(2,1)}, bf16[704,2048]{1,0:T(8,128)(2,1)}, u32[]{:S(2)}, u32[]{:S(2)}) collective-permute-start(bf16[704,2048]{1,0:T(8,128)(2,1)} %bitcast.206), channel_id=1, source_target_pairs={{0,2},{2,0},{4,6},{6,4},{8,10},{10,8},{12,14},{14,12},{16,18},{18,... | collective-permute-start | bytes 8650760 | tf_op jit(solution)/shard_map/while/body/cond/branch_1_fun/ppermute | solution.py:26
  50.4 5.0 %collective-permute-start.9 = (bf16[24,2048]{1,0:T(8,128)(2,1)}, bf16[24,2048]{1,0:T(8,128)(2,1)S(1)}, u32[]{:S(2)}, u32[]{:S(2)}) collective-permute-start(bf16[24,2048]{1,0:T(8,128)(2,1)} %get-tuple-element.179), channel_id=1, source_target_pairs={{0,8},{2,10},{4,12},{6,14},{8,0},{10,2},{12,4},{14,6},{16,24},{18,... | collective-permute-start | bytes 294920 | tf_op jit(solution)/shard_map/while/body/cond/branch_1_fun/ppermute | solution.py:26
  50.4 13.1 %collective-permute-start.11 = (bf16[24,2048]{1,0:T(8,128)(2,1)}, bf16[24,2048]{1,0:T(8,128)(2,1)S(1)}, u32[]{:S(2)}, u32[]{:S(2)}) collective-permute-start(bf16[24,2048]{1,0:T(8,128)(2,1)} %get-tuple-element.179), channel_id=1, source_target_pairs={{0,24},{2,26},{4,28},{6,30},{8,16},{10,18},{12,20},{14,22},{16,8},... | collective-permute-start | bytes 294920 | tf_op jit(solution)/shard_map/while/body/cond/branch_1_fun/ppermute | solution.py:26
  53.5 9.9 %collective-permute-start.10 = (bf16[24,2048]{1,0:T(8,128)(2,1)S(1)}, bf16[24,2048]{1,0:T(8,128)(2,1)S(1)}, u32[]{:S(2)}, u32[]{:S(2)}) collective-permute-start(bf16[24,2048]{1,0:T(8,128)(2,1)S(1)} %get-tuple-element.178), channel_id=1, source_target_pairs={{0,16},{2,18},{4,20},{6,22},{8,24},{10,26},{12,28},{14,30},{16,0},... | collective-permute-start | bytes 294920 | tf_op jit(solution)/shard_map/while/body/cond/branch_1_fun/ppermute | solution.py:26
  63.6 6.4 %collective-permute-start.12 = (bf16[96,1024]{1,0:T(8,128)(2,1)S(1)}, bf16[96,1024]{1,0:T(8,128)(2,1)S(1)}, u32[]{:S(2)}, u32[]{:S(2)}) collective-permute-start(bf16[96,1024]{1,0:T(8,128)(2,1)S(1)} %get-tuple-element.307), channel_id=1, source_target_pairs={{0,4},{2,6},{4,0},{6,2},{8,12},{10,14},{12,8},{14,10},{16,20},{18,... | collective-permute-start | bytes 589832 | tf_op jit(solution)/shard_map/while/body/cond/branch_1_fun/ppermute | solution.py:26
  63.9 7.7 %collective-permute-start.14 = (bf16[96,1024]{1,0:T(8,128)(2,1)S(1)}, bf16[96,1024]{1,0:T(8,128)(2,1)S(1)}, u32[]{:S(2)}, u32[]{:S(2)}) collective-permute-start(bf16[96,1024]{1,0:T(8,128)(2,1)S(1)} %get-tuple-element.306), channel_id=1, source_target_pairs={{0,1},{1,0},{2,3},{3,2},{4,5},{5,4},{6,7},{7,6},{8,9},{9,8},{10,11... | collective-permute-start | bytes 589832 | tf_op jit(solution)/shard_map/while/body/cond/branch_1_fun/ppermute | solution.py:26
  70.1 9.7 %collective-permute-start.13 = (bf16[2,96,1024]{2,1,0:T(8,128)(2,1)S(1)}, bf16[2,96,1024]{2,1,0:T(8,128)(2,1)S(1)}, u32[]{:S(2)}, u32[]{:S(2)}) collective-permute-start(bf16[2,96,1024]{2,1,0:T(8,128)(2,1)S(1)} %get-tuple-element.303), channel_id=1, source_target_pairs={{0,1},{1,0},{2,3},{3,2},{4,5},{5,4},{6,7},{7,6},{8,9},{9,8},{10,11... | collective-permute-start | bytes 1179656 | tf_op jit(solution)/shard_map/while/body/cond/branch_1_fun/ppermute | solution.py:26
  71.7 9.5 %collective-permute-start.15 = (bf16[2,96,1024]{2,1,0:T(8,128)(2,1)S(1)}, bf16[2,96,1024]{2,1,0:T(8,128)(2,1)S(1)}, u32[]{:S(2)}, u32[]{:S(2)}) collective-permute-start(bf16[2,96,1024]{2,1,0:T(8,128)(2,1)S(1)} %get-tuple-element.309), channel_id=1, source_target_pairs={{0,4},{2,6},{4,0},{6,2},{8,12},{10,14},{12,8},{14,10},{16,20},{18,... | collective-permute-start | bytes 1179656 | tf_op jit(solution)/shard_map/while/body/cond/branch_1_fun/ppermute | solution.py:26
  89.2 27.7 %copy-start.9 = (bf16[24,2048]{1,0:T(8,128)(2,1)S(1)}, bf16[24,2048]{1,0:T(8,128)(2,1)}, u32[]{:S(2)}) copy-start(bf16[24,2048]{1,0:T(8,128)(2,1)} %get-tuple-element.478) | copy-start | bytes 294916 | tf_op jit(solution)/shard_map/while
  89.2 27.8 %copy-start.8 = (bf16[24,2048]{1,0:T(8,128)(2,1)S(1)}, bf16[24,2048]{1,0:T(8,128)(2,1)}, u32[]{:S(2)}) copy-start(bf16[24,2048]{1,0:T(8,128)(2,1)} %get-tuple-element.499.second) | copy-start | bytes 294916 | tf_op jit(solution)/shard_map/while
  89.2 27.8 %copy-start.10 = (f32[128,2]{1,0:T(8,128)S(1)}, f32[128,2]{1,0:T(8,128)}, u32[]{:S(2)}) copy-start(f32[128,2]{1,0:T(8,128)} %get-tuple-element.501.gate_values) | copy-start | bytes 3076 | tf_op jit(solution)/shard_map/while
  89.3 8.7 %collective-permute-start.36 = (bf16[2,96,1024]{2,1,0:T(8,128)(2,1)S(1)}, bf16[2,96,1024]{2,1,0:T(8,128)(2,1)S(1)}, u32[]{:S(2)}, u32[]{:S(2)}) collective-permute-start(bf16[2,96,1024]{2,1,0:T(8,128)(2,1)S(1)} %slice_bitcast_fusion.14), channel_id=1, source_target_pairs={{0,4},{2,6},{4,0},{6,2},{8,12},{10,14},{12,8},{14,10},{16,20},{18,... | collective-permute-start | bytes 1179656 | tf_op jit(solution)/shard_map/while/body/cond/branch_1_fun/ppermute | solution.py:26
  89.7 9.1 %collective-permute-start.34 = (bf16[2,96,1024]{2,1,0:T(8,128)(2,1)S(1)}, bf16[2,96,1024]{2,1,0:T(8,128)(2,1)S(1)}, u32[]{:S(2)}, u32[]{:S(2)}) collective-permute-start(bf16[2,96,1024]{2,1,0:T(8,128)(2,1)S(1)} %slice_bitcast_fusion.16), channel_id=1, source_target_pairs={{0,1},{1,0},{2,3},{3,2},{4,5},{5,4},{6,7},{7,6},{8,9},{9,8},{10,11... | collective-permute-start | bytes 1179656 | tf_op jit(solution)/shard_map/while/body/cond/branch_1_fun/ppermute | solution.py:26
  98.1 5.7 %collective-permute-start.37 = (bf16[96,1024]{1,0:T(8,128)(2,1)S(1)}, bf16[96,1024]{1,0:T(8,128)(2,1)S(1)}, u32[]{:S(2)}, u32[]{:S(2)}) collective-permute-start(bf16[96,1024]{1,0:T(8,128)(2,1)S(1)} %slice_bitcast_fusion.18), channel_id=1, source_target_pairs={{0,1},{1,0},{2,3},{3,2},{4,5},{5,4},{6,7},{7,6},{8,9},{9,8},{10,11... | collective-permute-start | bytes 589832 | tf_op jit(solution)/shard_map/while/body/cond/branch_1_fun/ppermute | solution.py:26
  98.9 6.8 %collective-permute-start.35 = (bf16[96,1024]{1,0:T(8,128)(2,1)S(1)}, bf16[96,1024]{1,0:T(8,128)(2,1)S(1)}, u32[]{:S(2)}, u32[]{:S(2)}) collective-permute-start(bf16[96,1024]{1,0:T(8,128)(2,1)S(1)} %slice_bitcast_fusion.20), channel_id=1, source_target_pairs={{0,4},{2,6},{4,0},{6,2},{8,12},{10,14},{12,8},{14,10},{16,20},{18,... | collective-permute-start | bytes 589832 | tf_op jit(solution)/shard_map/while/body/cond/branch_1_fun/ppermute | solution.py:26
  105.7 6.0 %collective-permute-start.39 = (bf16[24,2048]{1,0:T(8,128)(2,1)S(1)}, bf16[24,2048]{1,0:T(8,128)(2,1)S(1)}, u32[]{:S(2)}, u32[]{:S(2)}) collective-permute-start(bf16[24,2048]{1,0:T(8,128)(2,1)S(1)} %get-tuple-element.198), channel_id=1, source_target_pairs={{0,8},{2,10},{4,12},{6,14},{8,0},{10,2},{12,4},{14,6},{16,24},{18,... | collective-permute-start | bytes 294920 | tf_op jit(solution)/shard_map/while/body/cond/branch_1_fun/ppermute | solution.py:26
  105.8 6.6 %collective-permute-start.40 = (bf16[24,2048]{1,0:T(8,128)(2,1)S(1)}, bf16[24,2048]{1,0:T(8,128)(2,1)S(1)}, u32[]{:S(2)}, u32[]{:S(2)}) collective-permute-start(bf16[24,2048]{1,0:T(8,128)(2,1)S(1)} %get-tuple-element.199), channel_id=1, source_target_pairs={{0,24},{2,26},{4,28},{6,30},{8,16},{10,18},{12,20},{14,22},{16,8},... | collective-permute-start | bytes 294920 | tf_op jit(solution)/shard_map/while/body/cond/branch_1_fun/ppermute | solution.py:26
  110.3 6.6 %collective-permute-start.38 = (bf16[24,2048]{1,0:T(8,128)(2,1)S(1)}, bf16[24,2048]{1,0:T(8,128)(2,1)S(1)}, u32[]{:S(2)}, u32[]{:S(2)}) collective-permute-start(bf16[24,2048]{1,0:T(8,128)(2,1)S(1)} %get-tuple-element.197), channel_id=1, source_target_pairs={{0,16},{2,18},{4,20},{6,22},{8,24},{10,26},{12,28},{14,30},{16,0},... | collective-permute-start | bytes 294920 | tf_op jit(solution)/shard_map/while/body/cond/branch_1_fun/ppermute | solution.py:26
